TPU v7x, 256 devices: a whole 4x4x8 slice. The times are simulated.
256 devices in a mesh: mp: 4 (over z_lo), seq: 32 (over x, z_hi, y), tp: 2 (over core).
Axes of the slice: x: 4, y: 4, z: 8 (z_hi: 2, z_lo: 4; z = z_hi * 4 + z_lo), core: 2. Of those that a mesh axis runs over, the one named last changes fastest.
Arguments:
- latent_noise: bfloat16 [2048, 64], P(('mp', 'tp')), may hold values from -6 to 6
- score_noise: bfloat16 [2048, 64], P(('mp', 'tp')), may hold values from -6 to 6
- gen_step: int32 [1], replicated, may hold values from 600 to 999
- score_step: int32 [1], replicated, may hold values from 100 to 949
- embed_weight: bfloat16 [4, 64, 5120], P('mp'), may hold values from -0.75 to 0.75
- qkv_weight: bfloat16 [4, 32, 384, 5120], P('mp', 'seq'), may hold values from -0.078125 to 0.078125
- mod_weight: bfloat16 [4, 256, 10240], P('mp'), may hold values from -0.375 to 0.375
- head_out: bfloat16 [4, 32, 128, 64], P('mp', 'seq'), may hold values from -0.09375 to 0.09375
Outputs:
- generated: bfloat16 [2048, 64], P(('mp', 'tp'))
- dmd_grad: float32 [2048, 64], P(('mp', 'tp'))
All inputs are finite; a program needn't handle non-finite values.
Results may differ from a plain program's by a relative error of at most 0.014.
Values may be sent and summed in bfloat16 or wider, within the bound.
No kernel may reach another device: no remote copies, remote signals or barrier semaphores. Data moves between devices by JAX's collectives and lax.ppermute only.
A program may use at most 128 MiB of HBM per device.

v0:
```python
import math

import jax
import jax.numpy as jnp
from jax import lax
from jax.sharding import PartitionSpec as P

norm_eps = 1e-06
guide_weight = 2.0
step_scale = 1000.0


def sinusoid(step_index, freq_count):
    half_freq = freq_count // 2
    frequency = jnp.exp(
        -math.log(10000.0) * jnp.arange(half_freq, dtype=jnp.float32) * 2.0 / freq_count
    )
    angles = step_index.astype(jnp.float32)[0] * frequency
    return jnp.concatenate([jnp.cos(angles), jnp.sin(angles)])


def attend_rows(queries, key_value, head_size):
    rows = queries.shape[0]
    heads = queries.shape[1]
    blocks = queries.reshape(rows // rows, rows, heads, head_size)

    def one_block(block_queries):
        logits = jnp.einsum(
            "qhc,khc->hqk",
            block_queries,
            key_value[:, :, :head_size],
            preferred_element_type=jnp.float32,
        ) * head_size ** (-0.5)
        logits = logits - jnp.max(logits, -1, keepdims=True)
        expo = jnp.exp(logits)
        attn_probs = (expo / jnp.sum(expo, -1, keepdims=True)).astype(jnp.bfloat16)
        return jnp.einsum(
            "hqk,khc->qhc",
            attn_probs,
            key_value[:, :, head_size:],
            preferred_element_type=jnp.float32,
        ).astype(jnp.bfloat16)

    return lax.map(one_block, blocks).reshape(rows, heads, head_size)


def norm_rows(embedded, mod_shift, mod_scale, row_mean, row_var):
    return (
        (embedded - row_mean) * lax.rsqrt(row_var + norm_eps) * (1.0 + mod_scale) + mod_shift
    ).astype(jnp.bfloat16)


def shards(
    latent_noise, score_noise, gen_step, score_step, embed_weight, qkv_weight, mod_weight, head_out
):
    width = embed_weight.shape[2]
    triple = qkv_weight.shape[2]
    head_size = triple // 3
    own_model = lax.axis_index("mp")
    own_step = jnp.where(own_model == 0, gen_step, score_step)
    own_mod = jnp.dot(
        sinusoid(own_step, mod_weight.shape[1])[None, :],
        mod_weight[0].astype(jnp.float32),
        precision=lax.Precision.HIGHEST,
    )
    gen_sigma = gen_step[0].astype(jnp.float32) / step_scale
    score_sigma = score_step[0].astype(jnp.float32) / step_scale
    local_maps = lax.all_gather(head_out, "mp", axis=0, tiled=True)
    all_maps = lax.all_gather(local_maps, "seq", axis=1, tiled=True)

    def velocity(model_index, attended):
        received = lax.all_to_all(attended, "seq", split_axis=0, concat_axis=1, tiled=True)
        partial_value = jnp.einsum(
            "qhc,hce->qe", received, all_maps[model_index], preferred_element_type=jnp.float32
        )
        return lax.all_gather(partial_value, "seq", axis=0, tiled=True)

    modulations = lax.all_gather(own_mod, "mp", axis=0, tiled=True)
    embeds, weights = (
        lax.all_gather(embed_weight, "mp", axis=0, tiled=True),
        lax.all_gather(qkv_weight, "mp", axis=0, tiled=True),
    )

    def project(model_index, latent):
        embedded = jnp.dot(latent, embeds[model_index], preferred_element_type=jnp.float32)
        row_mean = jnp.mean(embedded, -1, keepdims=True)
        row_var = jnp.mean(embedded * embedded, -1, keepdims=True) - row_mean * row_mean
        mod_vec = modulations[model_index]
        normed = norm_rows(embedded, mod_vec[:width], mod_vec[width:], row_mean, row_var)
        return jnp.einsum(
            "nd,hcd->nhc", normed, weights[model_index], preferred_element_type=jnp.float32
        ).astype(jnp.bfloat16)

    def run_model(model_index, prepared):
        projected = project(model_index, prepared)
        key_value = lax.all_gather(projected[:, :, head_size:], ("mp", "tp"), axis=0, tiled=True)
        return velocity(model_index, attend_rows(projected[:, :, :head_size], key_value, head_size))

    clean = latent_noise.astype(jnp.float32) - gen_sigma * run_model(0, latent_noise)
    noisy_latent = (
        (1.0 - score_sigma) * clean + score_sigma * score_noise.astype(jnp.float32)
    ).astype(jnp.bfloat16)
    prepared = noisy_latent
    predicted = []
    for model_index in range(1, 4):
        predicted.append(
            noisy_latent.astype(jnp.float32) - score_sigma * run_model(model_index, prepared)
        )
    real_guided = predicted[2] + guide_weight * (predicted[1] - predicted[2])
    dmd_grad = predicted[0] - real_guided
    return (clean.astype(jnp.bfloat16), dmd_grad)


def solution(mesh):
    placed = (
        P(("mp", "tp"), None),
        P(("mp", "tp"), None),
        P(),
        P(),
        P("mp", None, None),
        P("mp", "seq", None, None),
        P("mp", None, None),
        P("mp", "seq", None, None),
    )
    return jax.shard_map(
        shards,
        mesh=mesh,
        in_specs=placed,
        out_specs=(P(("mp", "tp"), None), P(("mp", "tp"), None)),
        check_vma=False,
    )
```

profile of v0, /device:TPU:8, one launch (start us, length us, event | category | flops | bytes accessed | tf_op | source)
XLA Modules:
  0.0 1078.5 jit_solution(2285592311784132916)
XLA Ops:
  10.1 4.6 fusion
  14.7 14.7 %all-gather = f32[40960]{0:T(1024)S(1)} all-gather(f32[10240]{0:T(1024)S(1)} %bitcast.194), channel_id=2, replica_groups=mesh['mp'=4,'seq'=32,'tp'=2] {'mp'}, dimensions={0}, use_global_device_ids=true | all-gather | bytes 204800 | tf_op jit(solution)/shard_map/all_gather | solution.py:78
  29.6 41.7 %all-gather.9.cloned.1.call-done = bf16[4,64,5120]{2,1,0:T(8,128)(2,1)} async-done(((bf16[1,64,5120]{2,1,0:T(8,128)(2,1)}), bf16[4,64,5120]{2,1,0:T(8,128)(2,1)}) %all-gather.9.cloned.1.call-update) | async-done | bytes 2621456 | tf_op jit(solution)/shard_map/all_gather | solution.py:80
  71.3 4.2 fusion.60
  75.6 271.7 %all-gather.11.cloned.1.call-done = bf16[4,1,384,5120]{3,2,1,0:T(8,128)(2,1)} async-done(((bf16[1,1,384,5120]{3,2,1,0:T(8,128)(2,1)}), bf16[4,1,384,5120]{3,2,1,0:T(8,128)(2,1)}) %all-gather.11.cloned.1.call-update) | async-done | bytes 15728656 | tf_op jit(solution)/shard_map/all_gather | solution.py:81
  347.2 5.3 fusion.33
  353.2 13.9 %all_gather.43 = bf16[4,1,128,64]{2,3,1,0:T(8,128)(2,1)} all-gather(bf16[1,1,128,64]{2,3,1,0:T(8,128)(2,1)S(1)} %copy-done.8), channel_id=1, replica_groups=mesh['mp'=4,'seq'=32,'tp'=2] {'mp'}, dimensions={0}, use_global_device_ids=true | all-gather | bytes 81920 | tf_op jit(solution)/shard_map/all_gather | solution.py:68
  367.2 22.2 %all-gather.13.cloned.1.call-done = bf16[2048,1,256]{2,0,1:T(8,128)(2,1)} async-done(((bf16[256,1,256]{2,0,1:T(8,128)(2,1)}), bf16[2048,1,256]{2,0,1:T(8,128)(2,1)}) %all-gather.13.cloned.1.call-update) | async-done | bytes 1048592 | tf_op jit(solution)/shard_map/all_gather | solution.py:96
  394.0 10.2 all-to-all-start
  404.5 10.9 %all-to-all-done = bf16[32,2,512]{2,1,0:T(2,128)(2,1)S(1)} async-done(((bf16[32,2,512]{2,1,0:T(2,128)(2,1)}), bf16[32,2,512]{2,1,0:T(2,128)(2,1)S(1)}, u32[]{:S(2)}, u32[]{:S(2)}) %all-to-all-start) | async-done | bytes 65568 | tf_op jit(solution)/shard_map/all_to_all | solution.py:72
  415.5 67.9 %all-gather.15.cloned.1.call-done = bf16[4,32,128,64]{2,3,1,0:T(8,128)(2,1)} async-done(((bf16[4,1,128,64]{2,3,1,0:T(8,128)(2,1)}), bf16[4,32,128,64]{2,3,1,0:T(8,128)(2,1)}) %all-gather.15.cloned.1.call-update) | async-done | bytes 2097168 | tf_op jit(solution)/shard_map/all_gather | solution.py:69
  484.7 109.0 %all_gather.45 = f32[256,64]{1,0:T(8,128)S(1)} all-gather(f32[8,64]{1,0:T(8,128)S(1)} %convolution_bitcast_fusion.3), channel_id=1, replica_groups=mesh['mp'=4,'seq'=32,'tp'=2] {'seq'}, dimensions={0}, use_global_device_ids=true | all-gather | bytes 67584 | tf_op jit(solution)/shard_map/all_gather | solution.py:76
  594.7 3.8 fusion.30
  600.4 3.8 fusion.31
  605.9 3.8 fusion.32
  611.2 20.9 %all-gather.21.cloned.1.call-done = bf16[2048,1,256]{2,0,1:T(8,128)(2,1)} async-done(((bf16[256,1,256]{2,0,1:T(8,128)(2,1)}), bf16[2048,1,256]{2,0,1:T(8,128)(2,1)}) %all-gather.21.cloned.1.call-update) | async-done | bytes 1048592 | tf_op jit(solution)/shard_map/all_gather | solution.py:96
  636.1 9.9 all-to-all-start.3
  646.1 23.8 %all-gather.19.cloned.1.call-done = bf16[2048,1,256]{2,0,1:T(8,128)(2,1)} async-done(((bf16[256,1,256]{2,0,1:T(8,128)(2,1)}), bf16[2048,1,256]{2,0,1:T(8,128)(2,1)}) %all-gather.19.cloned.1.call-update) | async-done | bytes 1048592 | tf_op jit(solution)/shard_map/all_gather | solution.py:96
  671.9 35.9 %all-gather.17.cloned.1.call-done = bf16[2048,1,256]{2,0,1:T(8,128)(2,1)} async-done(((bf16[256,1,256]{2,0,1:T(8,128)(2,1)}), bf16[2048,1,256]{2,0,1:T(8,128)(2,1)}) %all-gather.17.cloned.1.call-update) | async-done | bytes 1048592 | tf_op jit(solution)/shard_map/all_gather | solution.py:96
  714.4 10.0 all-to-all-start.2
  724.7 108.1 %all_gather.51 = f32[256,64]{1,0:T(8,128)S(1)} all-gather(f32[8,64]{1,0:T(8,128)S(1)} %convolution_bitcast_fusion), channel_id=1, replica_groups=mesh['mp'=4,'seq'=32,'tp'=2] {'seq'}, dimensions={0}, use_global_device_ids=true | all-gather | bytes 67584 | tf_op jit(solution)/shard_map/all_gather | solution.py:76
  832.8 12.8 %all-to-all-start.1 = ((bf16[32,2,512]{2,1,0:T(2,128)(2,1)}), bf16[32,2,512]{2,1,0:T(2,128)(2,1)S(1)}, u32[]{:S(2)}, u32[]{:S(2)}) async-start(bf16[32,2,512]{2,1,0:T(2,128)(2,1)} %reshape.287), calls=%async_computation.1 | async-start | bytes 131072 | tf_op jit(solution)/shard_map/all_to_all | solution.py:72
  845.9 108.2 %all_gather.49 = f32[256,64]{1,0:T(8,128)S(1)} all-gather(f32[8,64]{1,0:T(8,128)S(1)} %convolution_bitcast_fusion.1), channel_id=1, replica_groups=mesh['mp'=4,'seq'=32,'tp'=2] {'seq'}, dimensions={0}, use_global_device_ids=true | all-gather | bytes 67584 | tf_op jit(solution)/shard_map/all_gather | solution.py:76
  954.4 116.5 %all_gather.47 = f32[256,64]{1,0:T(8,128)S(1)} all-gather(f32[8,64]{1,0:T(8,128)S(1)} %convolution_bitcast_fusion.2), channel_id=1, replica_groups=mesh['mp'=4,'seq'=32,'tp'=2] {'seq'}, dimensions={0}, use_global_device_ids=true | all-gather | bytes 67584 | tf_op jit(solution)/shard_map/all_gather | solution.py:76
  (89 shorter events, 28.9 us)
Async XLA Ops:
  7.2 64.2 %all-gather.9.cloned.1.call-start = ((), (), s32[]{:S(2)}) async-start(), calls=%async_computation.4 | async-start | bytes 3276800 | tf_op jit(solution)/shard_map/all_gather | solution.py:80
  7.9 339.3 %all-gather.11.cloned.1.call-start = ((), (), s32[]{:S(2)}) async-start(), calls=%async_computation.5 | async-start | bytes 19660800 | tf_op jit(solution)/shard_map/all_gather | solution.py:81
  8.6 380.8 %all-gather.13.cloned.1.call-start = ((), (), s32[]{:S(2)}) async-start(), calls=%async_computation.6 | async-start | bytes 1179648 | tf_op jit(solution)/shard_map/all_gather | solution.py:96
  10.1 61.3 %copy-start.6 = (bf16[256,64]{0,1:T(8,128)(2,1)S(1)}, bf16[256,64]{0,1:T(8,128)(2,1)}, u32[]{:S(2)}) copy-start(bf16[256,64]{0,1:T(8,128)(2,1)} %param.8) | copy-start | bytes 98308
  347.2 6.0 copy-start.8
  353.2 130.2 %all-gather.15.cloned.1.call-start = ((), (), s32[]{:S(2)}) async-start(), calls=%async_computation.7 | async-start | bytes 2162688 | tf_op jit(solution)/shard_map/all_gather | solution.py:69
  389.4 2.1 copy-start.5
  391.5 12.9 %copy-start.7 = (bf16[256,64]{0,1:T(8,128)(2,1)S(1)}, bf16[256,64]{0,1:T(8,128)(2,1)}, u32[]{:S(2)}) copy-start(bf16[256,64]{0,1:T(8,128)(2,1)} %param.9) | copy-start | bytes 98308
  391.5 202.2 %copy-start = (bf16[4,64,5120]{2,1,0:T(8,128)(2,1)S(1)}, bf16[4,64,5120]{2,1,0:T(8,128)(2,1)}, u32[]{:S(2)}) copy-start(bf16[4,64,5120]{2,1,0:T(8,128)(2,1)} %all-gather.9.cloned.1.call-done) | copy-start | bytes 7864324
  394.0 21.4 %all-to-all-start = ((bf16[32,2,512]{2,1,0:T(2,128)(2,1)}), bf16[32,2,512]{2,1,0:T(2,128)(2,1)S(1)}, u32[]{:S(2)}, u32[]{:S(2)}) async-start(bf16[32,2,512]{2,1,0:T(2,128)(2,1)} %reshape.281), calls=%async_computation | async-start | bytes 131072 | tf_op jit(solution)/shard_map/all_to_all | solution.py:72
  404.2 227.9 %all-gather.21.cloned.1.call-start = ((), (), s32[]{:S(2)}) async-start(), calls=%async_computation.10 | async-start | bytes 1179648 | tf_op jit(solution)/shard_map/all_gather | solution.py:96
  599.2 70.7 %all-gather.19.cloned.1.call-start = ((), (), s32[]{:S(2)}) async-start(), calls=%async_computation.9 | async-start | bytes 1179648 | tf_op jit(solution)/shard_map/all_gather | solution.py:96
  604.9 102.8 %all-gather.17.cloned.1.call-start = ((), (), s32[]{:S(2)}) async-start(), calls=%async_computation.8 | async-start | bytes 1179648 | tf_op jit(solution)/shard_map/all_gather | solution.py:96
  632.1 2.1 copy-start.3
  636.1 78.3 %all-to-all-start.3 = ((bf16[32,2,512]{2,1,0:T(2,128)(2,1)}), bf16[32,2,512]{2,1,0:T(2,128)(2,1)S(1)}, u32[]{:S(2)}, u32[]{:S(2)}) async-start(bf16[32,2,512]{2,1,0:T(2,128)(2,1)} %reshape.283), calls=%async_computation.3 | async-start | bytes 131072 | tf_op jit(solution)/shard_map/all_to_all | solution.py:72
  707.7 2.1 copy-start.2
  709.8 1.2 copy-start.4
  711.1 13.4 %copy-start.1 = (bf16[4,32,128,64]{2,3,1,0:T(8,128)(2,1)S(1)}, bf16[4,32,128,64]{2,3,1,0:T(8,128)(2,1)}, u32[]{:S(2)}) copy-start(bf16[4,32,128,64]{2,3,1,0:T(8,128)(2,1)} %all-gather.15.cloned.1.call-done) | copy-start | bytes 6291460
  714.4 118.4 %all-to-all-start.2 = ((bf16[32,2,512]{2,1,0:T(2,128)(2,1)}), bf16[32,2,512]{2,1,0:T(2,128)(2,1)S(1)}, u32[]{:S(2)}, u32[]{:S(2)}) async-start(bf16[32,2,512]{2,1,0:T(2,128)(2,1)} %reshape.285), calls=%async_computation.2 | async-start | bytes 131072 | tf_op jit(solution)/shard_map/all_to_all | solution.py:72
  832.8 121.3 %all-to-all-start.1 = ((bf16[32,2,512]{2,1,0:T(2,128)(2,1)}), bf16[32,2,512]{2,1,0:T(2,128)(2,1)S(1)}, u32[]{:S(2)}, u32[]{:S(2)}) async-start(bf16[32,2,512]{2,1,0:T(2,128)(2,1)} %reshape.287), calls=%async_computation.1 | async-start | bytes 131072 | tf_op jit(solution)/shard_map/all_to_all | solution.py:72
Sparse Core Ops, SparseCore 0:
  9.8 61.4 all-gather.8
  73.1 274.0 all-gather.10
  353.3 36.0 all-gather.12
  392.8 90.5 all-gather.14
  599.3 32.6 all-gather.20
  633.7 36.1 all-gather.18
  671.7 36.0 all-gather.16
where the time goes:
time: 1080 us
  waiting for transfers between devices  496 us (46%)
  blocking collectives  470 us (44%)
  starting transfers between devices  43.3 us (4%)
  matrix products  39.4 us (4%)
  between operations  15.8 us (1%)
    all_gather x4, blocking collectives, velocity(): return lax.all_gather(partial_value, 'seq', axis=0, tiled=True)  442 us
    all_gather x1, waiting for transfers between devices, shards(): lax.all_gather(qkv_weight, 'mp', axis=0, tiled=True)  272 us
    all_gather x4, waiting for transfers between devices, run_model(): lax.all_gather(projected[:, :, head_size:], ('mp', 'tp'), axis=0, tiled=T...  103 us
    all_gather x1, waiting for transfers between devices, shards(): all_maps = lax.all_gather(local_maps, 'seq', axis=1, tiled=True)  67.9 us
    all_to_all x4, starting transfers between devices, velocity(): lax.all_to_all(attended, 'seq', split_axis=0, concat_axis=1, tiled=True)  42.8 us
    all_gather x1, waiting for transfers between devices, shards(): lax.all_gather(embed_weight, 'mp', axis=0, tiled=True)  41.7 us
  transfers between devices with their start and end apart: 11, of which 8 were waited for; matrix products, arithmetic and copies ran while one was open for 4% of the time, Pallas kernels for 0%

commit v1 on v0

v1 whole, which is shorter than its diff:
```python
import functools
import math

import jax
import jax.numpy as jnp
from jax import lax
from jax.experimental import pallas as pl
from jax.experimental.pallas import tpu as pltpu
from jax.sharding import Mesh
from jax.sharding import PartitionSpec as P

norm_eps = 1e-06
step_scale = 1000.0
f32 = jnp.float32
bf16 = jnp.bfloat16
chunk = 1024
lanes = 128
part = 80


def frequencies(freq_count):
    half_freq = freq_count // 2
    index = lax.broadcasted_iota(jnp.int32, (1, half_freq), 1)
    total = jnp.ones((1, half_freq), f32)
    for bit in range(half_freq.bit_length() - 1):
        factor = 10000.0 ** (-2.0 * (1 << bit) / freq_count)
        total = total * jnp.where((index >> bit) & 1 == 1, factor, 1.0)
    return total


def cos_sin(angle):
    turn = jnp.floor(angle * (2.0 / math.pi) + 0.5)
    left = angle - turn * 1.5703125
    left = left - turn * 4.837512969970703125e-4
    left = left - turn * 7.54978995489188216e-8
    square = left * left
    sine = left + left * square * (
        -1.6666654611e-1 + square * (8.3321608736e-3 - square * 1.9515295891e-4)
    )
    cosine = (
        1.0
        - 0.5 * square
        + square
        * square
        * (4.166664568298827e-2 + square * (-1.388731625493765e-3 + square * 2.443315711809948e-5))
    )
    quarter = turn.astype(jnp.int32) & 3
    odd = (quarter & 1) == 1
    cos_out = jnp.where(odd, sine, cosine)
    sin_out = jnp.where(odd, cosine, sine)
    cos_out = jnp.where((quarter == 1) | (quarter == 2), -cos_out, cos_out)
    sin_out = jnp.where(quarter >= 2, -sin_out, sin_out)
    return cos_out, sin_out


def dot(a, b, dims=(1, 0), precision=None):
    return lax.dot_general(
        a, b, (((dims[0],), (dims[1],)), ((), ())), precision=precision, preferred_element_type=f32
    )


def halves(value):
    high = value.astype(bf16)
    return high, (value - high.astype(f32)).astype(bf16)


def dot_halves(a, b):
    a_high, a_low = halves(a)
    b_high, b_low = halves(b)
    return dot(
        jnp.concatenate([a_high, a_high, a_low], 0),
        jnp.concatenate([b_high, b_low, b_high], 0),
        (0, 0),
    )


def maps_kernel(
    gen_ref, score_ref, embed_hbm, head_hbm, mod_hbm, weight_hbm, out_ref,
    embed_ref, head_ref, mod_ref, weight_ref, sems,
):
    chans, head_size = head_ref.shape
    width = embed_ref.shape[1]
    steps = width // chunk
    small = [
        pltpu.make_async_copy(source, target, sems.at[at])
        for at, (source, target) in enumerate(
            ((embed_hbm, embed_ref), (head_hbm, head_ref))
        )
    ]
    for copy in small:
        copy.start()
    copies = []
    for step in range(steps):
        mine = []
        for kind, (source, target, offset) in enumerate(
            ((mod_hbm, mod_ref, 0), (mod_hbm, mod_ref, width), (weight_hbm, weight_ref, 0))
        ):
            at = pl.ds(offset + step * chunk, chunk)
            copy = pltpu.make_async_copy(
                source.at[:, at], target.at[:, at], sems.at[2 + 3 * step + kind]
            )
            copy.start()
            mine.append(copy)
        copies.append(mine)

    small[0].wait()
    mean = jnp.sum(embed_ref[...].astype(f32), 1, keepdims=True) * (1.0 / width)
    ones = jnp.ones((part - chans, chunk), bf16)
    row_at = lax.broadcasted_iota(jnp.int32, (lanes - chans, chunk), 0)
    own_step = jnp.where(lax.axis_index("mp") == 0, gen_ref[0], score_ref[0]).astype(f32)
    waves = cos_sin(frequencies(2 * lanes) * own_step)
    freq = jnp.concatenate([jnp.broadcast_to(wave, (lanes, lanes)).T for wave in waves], 0)
    maps = gram = None
    for step in range(steps):
        own = embed_ref[:, pl.ds(step * chunk, chunk)]
        gram_term = dot(jnp.concatenate([own, ones], 0), own, (1, 1))
        rows = []
        copies[step][0].wait()
        copies[step][1].wait()
        for kind in range(2):
            total = None
            for at in range(0, freq.shape[0], 16):
                here = mod_ref[at : at + 16, pl.ds(kind * width + step * chunk, chunk)]
                scale = jnp.concatenate([freq[at : at + 16]] * (chunk // lanes), 1)
                term = here.astype(f32) * scale
                total = term if total is None else total + term
            rows.append(jnp.sum(total, 0, keepdims=True))
        centred = (own.astype(f32) - mean) * (1.0 + rows[1])
        tail = jnp.where(row_at == 0, jnp.broadcast_to(rows[0], row_at.shape), 0.0)
        lifted = jnp.concatenate([centred.astype(bf16), tail.astype(bf16)], 0)
        copies[step][2].wait()
        maps_term = dot(weight_ref[:, pl.ds(step * chunk, chunk)], lifted, (1, 1))
        maps = maps_term if maps is None else maps + maps_term
        gram = gram_term if gram is None else gram + gram_term

    map_q = maps[:head_size] * (head_size ** (-0.5) * math.log2(math.e))
    map_k = maps[head_size : 2 * head_size]
    map_v = maps[2 * head_size :]
    lane = lax.broadcasted_iota(jnp.int32, (head_size, lanes), 1)
    small[1].wait()
    wide_head = jnp.concatenate([jnp.zeros_like(head_ref), head_ref[...]], 0)
    main = dot_halves(map_q, jnp.where(lane < chans, map_k, 0.0))
    high, low = halves(map_v)
    main += dot(high, wide_head, (0, 1)) + dot(low, wide_head, (0, 1))
    last = dot_halves(map_k, map_q)[chans : chans + 1]
    main = main[:part]
    row = lax.broadcasted_iota(jnp.int32, main.shape, 0)
    main = jnp.where(row == chans + 1, jnp.broadcast_to(last, main.shape), main)
    out_ref[:part] = main.astype(bf16)
    gram = gram * (1.0 / width)
    high, low = halves(gram[:chans] - mean * gram[chans : chans + 1])
    out_ref[part:] = jnp.concatenate([high.astype(f32), low.astype(f32)], 1).astype(bf16)


def fold_maps(gen_step, score_step, head, embed, mod_weight, weight):
    chans, width = embed.shape
    return pl.pallas_call(
        maps_kernel,
        in_specs=[pl.BlockSpec(memory_space=pltpu.SMEM)] * 2
        + [pl.BlockSpec(memory_space=pl.ANY)] * 4,
        out_specs=pl.BlockSpec(memory_space=pltpu.VMEM),
        out_shape=jax.ShapeDtypeStruct((part + chans, lanes), bf16),
        scratch_shapes=[
            pltpu.VMEM(embed.shape, bf16),
            pltpu.VMEM(head.shape, bf16),
            pltpu.VMEM(mod_weight.shape, bf16),
            pltpu.VMEM(weight.shape, bf16),
            pltpu.SemaphoreType.DMA((2 + 3 * (width // chunk),)),
        ],
        compiler_params=pltpu.CompilerParams(vmem_limit_bytes=56_000_000),
        cost_estimate=pl.CostEstimate(
            flops=6_000_000_000, bytes_accessed=10_000_000, transcendentals=0
        ),
        name="fold_maps",
    )(gen_step, score_step, embed, head, mod_weight, weight)


def attend_kernel(terms, count, before, last, *refs):
    refs = list(refs)
    pack_refs, own_ref, token_refs = refs[:4], refs[4], refs[5 : 5 + count]
    keys_ref = refs[-1]
    chans, rows = own_ref.shape
    size = count * rows
    here, upper = lax.axis_index("mp"), lax.axis_index("zh") == 1

    mains, spreads = [], []
    for model, _ in terms:
        at = here ^ model
        pack = pack_refs[0][...]
        for other in range(1, 4):
            pack = jnp.where(at == other, pack_refs[other][...], pack)
        one, two = pack[:part], pack[part + chans :]
        mains.append((jnp.where(upper, two, one), jnp.where(upper, one, two)))
        spreads.append(pack[part : part + chans])

    tokens = jnp.concatenate([ref[...] for ref in token_refs] + [own_ref[...]], 1)
    wide = tokens.astype(f32)
    spread = dot(jnp.concatenate(spreads, 0), jnp.concatenate([tokens, tokens], 0))
    row = lax.broadcasted_iota(jnp.int32, (part - chans, size + rows), 0)
    one = jnp.where(row == 0, 1.0, 0.0).astype(bf16)
    logits = []
    for slot, heads in enumerate(mains):
        product = spread[slot * chans : (slot + 1) * chans] * wide
        variance = jnp.maximum(jnp.sum(product, 0, keepdims=True), 0.0)
        normed = wide * lax.rsqrt(variance + norm_eps)
        high = normed.astype(bf16)
        low = (normed - high.astype(f32)).astype(bf16)
        features = jnp.concatenate([high, one, low, jnp.zeros_like(one)], 0)
        keys_ref[slot] = features[:, :size]
        own = features[:, size:]
        own_high = jnp.concatenate([own[:part], jnp.zeros((lanes - part, rows), bf16)], 0)
        for main in heads:
            ask = dot(jnp.concatenate([main, main], 0), own, (0, 0))[:chans].astype(bf16)
            shared = jnp.broadcast_to(dot(main[chans:], own_high)[1:2], (part - chans, rows))
            shared = jnp.where(row[:, :rows] == 0, shared, 0.0).astype(bf16)
            queries = jnp.concatenate([ask, shared, ask, jnp.zeros_like(shared)], 0)
            logits.append(dot(queries, keys_ref[slot], (0, 0)))

    total = None
    for place, scores in enumerate(logits):
        slot, head = divmod(place, 2)
        peak = jnp.broadcast_to(jnp.max(scores, 1, keepdims=True), (rows, lanes))
        if before:
            old_peak = refs[6 + count][place]
            peak = jnp.maximum(peak, old_peak)
        expo = jnp.exp2(scores - jnp.concatenate([peak] * (size // lanes), 1)).astype(bf16)
        mixed = dot(expo, keys_ref[slot], (1, 1))
        if before:
            factor = jnp.exp2(old_peak - peak)
            factor = jnp.concatenate([factor, factor[:, : 2 * part - lanes]], 1)
            mixed += refs[5 + count][place] * factor
        if last:
            mixed = (mixed / mixed[:, chans : chans + 1]).astype(bf16)
            main = jnp.concatenate([mains[slot][head]] * 2, 0)
            term = terms[slot][1] * dot(main, mixed, (0, 1))[chans:]
            total = term if total is None else total + term
        else:
            refs[-3][place] = mixed
            refs[-2][place] = peak
    if last:
        refs[-2][...] = total.astype(bf16)


def attend(terms, packs, own, tokens, state=(), last=True):
    rows = own.shape[1]
    count = len(tokens)
    pairs = 2 * count * rows * rows * len(terms)
    shape = [
        jax.ShapeDtypeStruct((2 * len(terms), rows, 2 * part), f32),
        jax.ShapeDtypeStruct((2 * len(terms), rows, lanes), f32),
    ]
    if last:
        shape = jax.ShapeDtypeStruct(own.shape, bf16)
    return pl.pallas_call(
        functools.partial(attend_kernel, terms, count, bool(state), last),
        out_shape=shape,
        scratch_shapes=[pltpu.VMEM((len(terms), 2 * part, count * rows), bf16)],
        compiler_params=pltpu.CompilerParams(vmem_limit_bytes=48 * 1024 * 1024),
        cost_estimate=pl.CostEstimate(
            flops=16 * pairs * lanes, bytes_accessed=1_000_000, transcendentals=pairs
        ),
        name="attend",
    )(*packs, own, *tokens, *state)


def swap(value, axis, flip, cross=0):
    axes = (axis, "tp")
    flip = 2 * flip + cross
    return lax.ppermute(value, axes, [(i, i ^ flip) for i in range(lax.axis_size(axes))])


def swap_all(value, axis, cross):
    one, three, two = (
        swap(value, axis, flip, crossed)
        for flip, crossed in ((1, cross[0]), (3, cross[2]), (2, cross[1]))
    )
    return [value, one, two, three]


def other_core(value):
    return lax.ppermute(value, "tp", [(0, 1), (1, 0)])


def add_over(value, axis):
    sent = lax.optimization_barrier(value.astype(bf16))
    parts = [part.astype(f32) for part in swap_all(sent, axis, (1, 0, 1))]
    return (parts[0] + parts[1]) + (parts[2] + parts[3])


def add_heads(value):
    return add_over(add_over(value, "y"), "x")


def shards(
    latent_noise, score_noise, gen_step, score_step, embed_weight, qkv_weight, mod_weight, head_out
):
    model = lax.axis_index("mp")
    gen_sigma = gen_step[0].astype(f32) / step_scale
    score_sigma = score_step[0].astype(f32) / step_scale
    latents, noise = latent_noise.T, score_noise.T
    odd = (lax.axis_index("x") + lax.axis_index("y")) % 2 == 1

    first = swap(latents, "mp", 1, 1)
    noise = jnp.where(odd, other_core(noise), noise)
    pack = fold_maps(
        gen_step, score_step, head_out[0, 0].T, embed_weight[0], mod_weight[0], qkv_weight[0, 0]
    )
    pack, first, noise = lax.optimization_barrier((pack, first, noise))
    other = swap(pack[:part], "zh", 1, 1)
    pair = swap(jnp.stack([latents, first]), "mp", 2, 1)
    packs = swap_all(jnp.concatenate([pack, other], 0), "mp", (1, 1, 1))
    near = [latents, first, pair[0], pair[1]]
    far = other_core(jnp.stack(near))

    latents = jnp.where(odd, far[0], latents)
    speed = add_heads(attend(((0, 1.0),), packs, latents, near + list(far)))
    clean = latents.astype(f32) - gen_sigma * speed
    noisy = (1.0 - score_sigma) * clean + score_sigma * noise.astype(f32)
    near = swap_all(noisy.astype(bf16), "mp", (1, 1, 1))
    far = other_core(jnp.stack(near))
    terms = ((1, 1.0), (2, -2.0), (3, 1.0))
    state = attend(terms, packs, near[0], near, last=False)
    grad = attend(terms, packs, near[0], list(far), state)
    grad = add_heads(grad) * -score_sigma
    grad = jnp.where(odd, other_core(grad), grad)
    clean = clean.astype(bf16)
    clean = jnp.where(odd, other_core(clean), clean)
    return (clean.T, grad.T)


def solution(mesh):
    models, heads, cores = mesh.devices.shape
    fine = Mesh(mesh.devices.reshape(models, 4, heads // 16, 4, cores), ("mp", "x", "zh", "y", "tp"))
    placed = (
        P(("mp", "tp"), None),
        P(("mp", "tp"), None),
        P(),
        P(),
        P("mp", None, None),
        P("mp", ("x", "zh", "y"), None, None),
        P("mp", None, None),
        P("mp", ("x", "zh", "y"), None, None),
    )
    return jax.shard_map(
        shards,
        mesh=fine,
        in_specs=placed,
        out_specs=(P(("mp", "tp"), None), P(("mp", "tp"), None)),
        check_vma=False,
    )
```

time: 1080 us -> 79.4 us (0.07)
  the two profiles are of different devices: /device:TPU:8 before, /device:TPU:1 now
where the time goes in v1:
time: 79.4 us; the launch traced here: 79.2 us
  starting transfers between devices  37.1 us (47%)
  waiting for transfers between devices  20.1 us (25%)
  Pallas kernels  17.6 us (22%)
  between operations  2.13 us (3%)
  other arithmetic  1.42 us (2%)
    ppermute x21, starting transfers between devices, swap(): lax.ppermute(value, axes, [(i, i ^ flip) for i in range(lax.axis_size(axe...  32.3 us
    ppermute x21, waiting for transfers between devices, swap(): lax.ppermute(value, axes, [(i, i ^ flip) for i in range(lax.axis_size(axe...  18.5 us
    pallas_call x3, Pallas kernels, attend(): pl.pallas_call(functools.partial(attend_kernel, terms, count, bool(state)...  11.8 us
    pallas_call x1, Pallas kernels, fold_maps(): pl.pallas_call(maps_kernel, in_specs=[pl.BlockSpec(memory_space=pltpu.SME...  5.81 us
    ppermute x5, starting transfers between devices, other_core(): return lax.ppermute(value, 'tp', [(0, 1), (1, 0)])  4.78 us
    ppermute x5, waiting for transfers between devices, other_core(): return lax.ppermute(value, 'tp', [(0, 1), (1, 0)])  1.6 us
  transfers between devices with their start and end apart: 26, of which 17 were waited for; matrix products, arithmetic and copies ran while one was open for 1% of the time, Pallas kernels for 12%

profile of v1, /device:TPU:1, one launch (start us, length us, event | category | flops | bytes accessed | tf_op | source)
XLA Modules:
  0.0 79.2 jit_solution(8720330307685866170)
XLA Ops:
  0.6 3.3 %collective-permute-start.1 = (bf16[64,256]{1,0:T(8,128)(2,1)}, bf16[64,256]{1,0:T(8,128)(2,1)S(1)}, u32[]{:S(2)}, u32[]{:S(2)}) collective-permute-start(bf16[64,256]{1,0:T(8,128)(2,1)} %bitcast.56), channel_id=1, source_target_pairs={{0,1},{1,0},{2,3},{3,2},{4,5},{5,4},{6,7},{7,6},{8,9},{9,8},{10,11... | collective-permute-start | bytes 98312 | tf_op jit(solution)/shard_map/ppermute | solution.py:281
  6.0 5.8 %fold_maps.1 = bf16[144,128]{1,0:T(8,128)(2,1)S(1)} custom-call(s32[1]{0:T(128)S(6)} %copy.11.gen_ref, s32[1]{0:T(128)S(6)} %copy.12.score_ref, bf16[64,5120]{1,0:T(8,128)(2,1)} %bitcast.59, bf16[64,128]{1,0:T(8,128)(2,1)S(1)} %bitcast.55, bf16[256,10240]{1,0:T(8,128)(2,1)} %bitcast.57, bf16[384,5120]{1,0:T(8,128)(2,1)} %bitcast.58), custom_call_target="tpu_custom_call" | custom-call | flops 6000000000 | bytes 10000000 | tf_op jit(solution)/shard_map/fold_maps/pallas_call | solution.py:157
  11.9 6.3 %collective-permute-start.4 = (bf16[80,128]{1,0:T(8,128)(2,1)S(1)}, bf16[80,128]{1,0:T(8,128)(2,1)S(1)}, u32[]{:S(2)}, u32[]{:S(2)}) collective-permute-start(bf16[80,128]{1,0:T(8,128)(2,1)S(1)} %slice.14), channel_id=1, source_target_pairs={{0,9},{1,8},{8,1},{9,0},{2,11},{3,10},{10,3},{11,2},{4,13},{5,12},... | collective-permute-start | bytes 61448 | tf_op jit(solution)/shard_map/ppermute | solution.py:269
  18.2 1.2 %collective-permute-start.2 = (bf16[2,64,256]{2,1,0:T(8,128)(2,1)S(1)}, bf16[2,64,256]{2,1,0:T(8,128)(2,1)S(1)}, u32[]{:S(2)}, u32[]{:S(2)}) collective-permute-start(bf16[2,64,256]{2,1,0:T(8,128)(2,1)S(1)} %pad_maximum_fusion.2), channel_id=1, source_target_pairs={{0,129},{1,128},{64,193},{65,192},{128,1},{129,0},{192,65},{193,64... | collective-permute-start | bytes 196616 | tf_op jit(solution)/shard_map/ppermute | solution.py:269
  19.8 2.1 %collective-permute-start.7 = (bf16[224,128]{1,0:T(8,128)(2,1)S(1)}, bf16[224,128]{1,0:T(8,128)(2,1)S(1)}, u32[]{:S(2)}, u32[]{:S(2)}) collective-permute-start(bf16[224,128]{1,0:T(8,128)(2,1)S(1)} %constant_dynamic-update-slice_fusion.refs_0_), channel_id=1, source_target_pairs={{0,193},{1,192},{64,129},{65,128},{128,65},{129,64},{192,1},{193,0... | collective-permute-start | bytes 172040 | tf_op jit(solution)/shard_map/ppermute | solution.py:269
  22.7 1.0 %collective-permute-start.5 = (bf16[224,128]{1,0:T(8,128)(2,1)S(1)}, bf16[224,128]{1,0:T(8,128)(2,1)S(1)}, u32[]{:S(2)}, u32[]{:S(2)}) collective-permute-start(bf16[224,128]{1,0:T(8,128)(2,1)S(1)} %constant_dynamic-update-slice_fusion.refs_0_), channel_id=1, source_target_pairs={{0,65},{1,64},{64,1},{65,0},{128,193},{129,192},{192,129},{193,128... | collective-permute-start | bytes 172040 | tf_op jit(solution)/shard_map/ppermute | solution.py:269
  23.7 3.3 %collective-permute-done.2 = bf16[2,64,256]{2,1,0:T(8,128)(2,1)S(1)} collective-permute-done((bf16[2,64,256]{2,1,0:T(8,128)(2,1)S(1)}, bf16[2,64,256]{2,1,0:T(8,128)(2,1)S(1)}, u32[]{:S(2)}, u32[]{:S(2)}) %collective-permute-start.2) | collective-permute-done | bytes 65568 | tf_op jit(solution)/shard_map/ppermute | solution.py:269
  27.1 1.3 %collective-permute-done.3 = bf16[4,64,256]{2,1,0:T(8,128)(2,1)S(1)} collective-permute-done((bf16[4,64,256]{2,1,0:T(8,128)(2,1)S(1)}, bf16[4,64,256]{2,1,0:T(8,128)(2,1)S(1)}, u32[]{:S(2)}, u32[]{:S(2)}) %collective-permute-start.3) | collective-permute-done | bytes 131104 | tf_op jit(solution)/shard_map/ppermute | solution.py:281
  29.3 2.9 %attend.3 = bf16[64,256]{1,0:T(8,128)(2,1)S(1)} custom-call(bf16[224,128]{1,0:T(8,128)(2,1)S(1)} %constant_dynamic-update-slice_fusion.refs_0_, bf16[224,128]{1,0:T(8,128)(2,1)S(1)} %collective-permute-done.5.refs_1_, bf16[224,128]{1,0:T(8,128)(2,1)S(1)} %collective-permute-done.6.refs_2_, bf16[224,128]{1,0:T(8,128)(2,1)S(1)} %collective-permute-done.7.refs_3_, ...), custom_call_target="tpu_custom_call" | custom-call | flops 2147483648 | bytes 1000000 | tf_op jit(solution)/shard_map/attend/pallas_call | solution.py:254
  32.2 2.9 %collective-permute-start.10 = (bf16[64,256]{1,0:T(8,128)(2,1)S(1)}, bf16[64,256]{1,0:T(8,128)(2,1)S(1)}, u32[]{:S(2)}, u32[]{:S(2)}) collective-permute-start(bf16[64,256]{1,0:T(8,128)(2,1)S(1)} %attend.3), channel_id=1, source_target_pairs={{0,7},{1,6},{2,5},{3,4},{4,3},{5,2},{6,1},{7,0},{8,15},{9,14},{10,... | collective-permute-start | bytes 98312 | tf_op jit(solution)/shard_map/ppermute | solution.py:269
  36.9 2.5 %collective-permute-done.9 = bf16[64,256]{1,0:T(8,128)(2,1)S(1)} collective-permute-done((bf16[64,256]{1,0:T(8,128)(2,1)S(1)}, bf16[64,256]{1,0:T(8,128)(2,1)S(1)}, u32[]{:S(2)}, u32[]{:S(2)}) %collective-permute-start.9) | collective-permute-done | bytes 32800 | tf_op jit(solution)/shard_map/ppermute | solution.py:269
  39.4 4.1 %collective-permute-start.13 = (bf16[64,256]{1,0:T(8,128)(2,1)S(1)}, bf16[64,256]{1,0:T(8,128)(2,1)S(1)}, u32[]{:S(2)}, u32[]{:S(2)}) collective-permute-start(bf16[64,256]{1,0:T(8,128)(2,1)S(1)} %add_convert_fusion.2), channel_id=1, source_target_pairs={{0,49},{1,48},{16,33},{17,32},{32,17},{33,16},{48,1},{49,0},{2,51}... | collective-permute-start | bytes 98312 | tf_op jit(solution)/shard_map/ppermute | solution.py:269
  45.6 2.2 %collective-permute-done.12 = bf16[64,256]{1,0:T(8,128)(2,1)S(1)} collective-permute-done((bf16[64,256]{1,0:T(8,128)(2,1)S(1)}, bf16[64,256]{1,0:T(8,128)(2,1)S(1)}, u32[]{:S(2)}, u32[]{:S(2)}) %collective-permute-start.12) | collective-permute-done | bytes 32800 | tf_op jit(solution)/shard_map/ppermute | solution.py:269
  47.8 2.1 %collective-permute-start.17 = (bf16[64,256]{1,0:T(8,128)(2,1)S(1)}, bf16[64,256]{1,0:T(8,128)(2,1)S(1)}, u32[]{:S(2)}, u32[]{:S(2)}) collective-permute-start(bf16[64,256]{1,0:T(8,128)(2,1)S(1)} %get-tuple-element.12.refs_4_.refs_5_), channel_id=1, source_target_pairs={{0,193},{1,192},{64,129},{65,128},{128,65},{129,64},{192,1},{193,0... | collective-permute-start | bytes 98312 | tf_op jit(solution)/shard_map/ppermute | solution.py:269
  49.9 1.8 %collective-permute-start.15 = (bf16[64,256]{1,0:T(8,128)(2,1)S(1)}, bf16[64,256]{1,0:T(8,128)(2,1)S(1)}, u32[]{:S(2)}, u32[]{:S(2)}) collective-permute-start(bf16[64,256]{1,0:T(8,128)(2,1)S(1)} %get-tuple-element.12.refs_4_.refs_5_), channel_id=1, source_target_pairs={{0,65},{1,64},{64,1},{65,0},{128,193},{129,192},{192,129},{193,128... | collective-permute-start | bytes 98312 | tf_op jit(solution)/shard_map/ppermute | solution.py:269
  51.8 1.5 %collective-permute-done.17.refs_8_ = bf16[64,256]{1,0:T(8,128)(2,1)S(1)} collective-permute-done((bf16[64,256]{1,0:T(8,128)(2,1)S(1)}, bf16[64,256]{1,0:T(8,128)(2,1)S(1)}, u32[]{:S(2)}, u32[]{:S(2)}) %collective-permute-start.17) | collective-permute-done | bytes 32800 | tf_op jit(solution)/shard_map/ppermute | solution.py:269
  53.2 1.1 %collective-permute-done.16.refs_7_ = bf16[64,256]{1,0:T(8,128)(2,1)S(1)} collective-permute-done((bf16[64,256]{1,0:T(8,128)(2,1)S(1)}, bf16[64,256]{1,0:T(8,128)(2,1)S(1)}, u32[]{:S(2)}, u32[]{:S(2)}) %collective-permute-start.16) | collective-permute-done | bytes 32800 | tf_op jit(solution)/shard_map/ppermute | solution.py:269
  55.2 3.7 %attend.4 = (f32[6,256,160]{2,1,0:T(8,128)S(1)}, f32[6,256,128]{2,1,0:T(8,128)S(1)}) custom-call(bf16[224,128]{1,0:T(8,128)(2,1)S(1)} %constant_dynamic-update-slice_fusion.refs_0_, bf16[224,128]{1,0:T(8,128)(2,1)S(1)} %collective-permute-done.5.refs_1_, bf16[224,128]{1,0:T(8,128)(2,1)S(1)} %collective-permute-done.6.refs_2_, ...), custom_call_target="tpu_custom_call" | custom-call | flops 3221225472 | bytes 1000000 | tf_op jit(solution)/shard_map/attend/pallas_call | solution.py:254
  58.9 5.2 %attend.5 = bf16[64,256]{1,0:T(8,128)(2,1)S(1)} custom-call(bf16[224,128]{1,0:T(8,128)(2,1)S(1)} %constant_dynamic-update-slice_fusion.refs_0_, bf16[224,128]{1,0:T(8,128)(2,1)S(1)} %collective-permute-done.5.refs_1_, bf16[224,128]{1,0:T(8,128)(2,1)S(1)} %collective-permute-done.6.refs_2_, bf16[224,128]{1,0:T(8,128)(2,1)S(1)} %collective-permute-done.7.refs_3_, ...), custom_call_target="tpu_custom_call" | custom-call | flops 3221225472 | bytes 1000000 | tf_op jit(solution)/shard_map/attend/pallas_call | solution.py:254
  64.1 1.3 %collective-permute-start.21 = (bf16[64,256]{1,0:T(8,128)(2,1)S(1)}, bf16[64,256]{1,0:T(8,128)(2,1)S(1)}, u32[]{:S(2)}, u32[]{:S(2)}) collective-permute-start(bf16[64,256]{1,0:T(8,128)(2,1)S(1)} %attend.5), channel_id=1, source_target_pairs={{0,7},{1,6},{2,5},{3,4},{4,3},{5,2},{6,1},{7,0},{8,15},{9,14},{10,... | collective-permute-start | bytes 98312 | tf_op jit(solution)/shard_map/ppermute | solution.py:269
  66.4 1.6 %collective-permute-start.19 = (bf16[64,256]{1,0:T(8,128)(2,1)S(1)}, bf16[64,256]{1,0:T(8,128)(2,1)S(1)}, u32[]{:S(2)}, u32[]{:S(2)}) collective-permute-start(bf16[64,256]{1,0:T(8,128)(2,1)S(1)} %attend.5), channel_id=1, source_target_pairs={{0,3},{1,2},{2,1},{3,0},{4,7},{5,6},{6,5},{7,4},{8,11},{9,10},{10,... | collective-permute-start | bytes 98312 | tf_op jit(solution)/shard_map/ppermute | solution.py:269
  70.5 1.7 %collective-permute-start.24 = (bf16[64,256]{1,0:T(8,128)(2,1)S(1)}, bf16[64,256]{1,0:T(8,128)(2,1)S(1)}, u32[]{:S(2)}, u32[]{:S(2)}) collective-permute-start(bf16[64,256]{1,0:T(8,128)(2,1)S(1)} %add_convert_fusion), channel_id=1, source_target_pairs={{0,49},{1,48},{16,33},{17,32},{32,17},{33,16},{48,1},{49,0},{2,51}... | collective-permute-start | bytes 98312 | tf_op jit(solution)/shard_map/ppermute | solution.py:269
  73.2 1.2 %collective-permute-start.22 = (bf16[64,256]{1,0:T(8,128)(2,1)S(1)}, bf16[64,256]{1,0:T(8,128)(2,1)S(1)}, u32[]{:S(2)}, u32[]{:S(2)}) collective-permute-start(bf16[64,256]{1,0:T(8,128)(2,1)S(1)} %add_convert_fusion), channel_id=1, source_target_pairs={{0,17},{1,16},{16,1},{17,0},{32,49},{33,48},{48,33},{49,32},{2,19}... | collective-permute-start | bytes 98312 | tf_op jit(solution)/shard_map/ppermute | solution.py:269
  75.2 1.7 %collective-permute-done.23 = bf16[64,256]{1,0:T(8,128)(2,1)S(1)} collective-permute-done((bf16[64,256]{1,0:T(8,128)(2,1)S(1)}, bf16[64,256]{1,0:T(8,128)(2,1)S(1)}, u32[]{:S(2)}, u32[]{:S(2)}) %collective-permute-start.23) | collective-permute-done | bytes 32800 | tf_op jit(solution)/shard_map/ppermute | solution.py:269
  (55 shorter events, 15.2 us)
Async XLA Ops:
  0.6 11.2 %collective-permute-start.1 = (bf16[64,256]{1,0:T(8,128)(2,1)}, bf16[64,256]{1,0:T(8,128)(2,1)S(1)}, u32[]{:S(2)}, u32[]{:S(2)}) collective-permute-start(bf16[64,256]{1,0:T(8,128)(2,1)} %bitcast.56), channel_id=1, source_target_pairs={{0,1},{1,0},{2,3},{3,2},{4,5},{5,4},{6,7},{7,6},{8,9},{9,8},{10,11... | collective-permute-start | bytes 98312 | tf_op jit(solution)/shard_map/ppermute | solution.py:281
  4.0 7.9 %collective-permute-start = (bf16[64,256]{1,0:T(8,128)(2,1)}, bf16[64,256]{1,0:T(8,128)(2,1)S(1)}, u32[]{:S(2)}, u32[]{:S(2)}) collective-permute-start(bf16[64,256]{1,0:T(8,128)(2,1)} %bitcast.45), channel_id=1, source_target_pairs={{0,65},{1,64},{64,1},{65,0},{128,193},{129,192},{192,129},{193,128... | collective-permute-start | bytes 98312 | tf_op jit(solution)/shard_map/ppermute | solution.py:269
  11.9 7.9 %collective-permute-start.4 = (bf16[80,128]{1,0:T(8,128)(2,1)S(1)}, bf16[80,128]{1,0:T(8,128)(2,1)S(1)}, u32[]{:S(2)}, u32[]{:S(2)}) collective-permute-start(bf16[80,128]{1,0:T(8,128)(2,1)S(1)} %slice.14), channel_id=1, source_target_pairs={{0,9},{1,8},{8,1},{9,0},{2,11},{3,10},{10,3},{11,2},{4,13},{5,12},... | collective-permute-start | bytes 61448 | tf_op jit(solution)/shard_map/ppermute | solution.py:269
  18.2 8.8 %collective-permute-start.2 = (bf16[2,64,256]{2,1,0:T(8,128)(2,1)S(1)}, bf16[2,64,256]{2,1,0:T(8,128)(2,1)S(1)}, u32[]{:S(2)}, u32[]{:S(2)}) collective-permute-start(bf16[2,64,256]{2,1,0:T(8,128)(2,1)S(1)} %pad_maximum_fusion.2), channel_id=1, source_target_pairs={{0,129},{1,128},{64,193},{65,192},{128,1},{129,0},{192,65},{193,64... | collective-permute-start | bytes 196616 | tf_op jit(solution)/shard_map/ppermute | solution.py:269
  19.8 8.7 %collective-permute-start.7 = (bf16[224,128]{1,0:T(8,128)(2,1)S(1)}, bf16[224,128]{1,0:T(8,128)(2,1)S(1)}, u32[]{:S(2)}, u32[]{:S(2)}) collective-permute-start(bf16[224,128]{1,0:T(8,128)(2,1)S(1)} %constant_dynamic-update-slice_fusion.refs_0_), channel_id=1, source_target_pairs={{0,193},{1,192},{64,129},{65,128},{128,65},{129,64},{192,1},{193,0... | collective-permute-start | bytes 172040 | tf_op jit(solution)/shard_map/ppermute | solution.py:269
  21.8 7.5 %collective-permute-start.6 = (bf16[224,128]{1,0:T(8,128)(2,1)S(1)}, bf16[224,128]{1,0:T(8,128)(2,1)S(1)}, u32[]{:S(2)}, u32[]{:S(2)}) collective-permute-start(bf16[224,128]{1,0:T(8,128)(2,1)S(1)} %constant_dynamic-update-slice_fusion.refs_0_), channel_id=1, source_target_pairs={{0,129},{1,128},{64,193},{65,192},{128,1},{129,0},{192,65},{193,64... | collective-permute-start | bytes 172040 | tf_op jit(solution)/shard_map/ppermute | solution.py:269
  22.7 6.6 %collective-permute-start.5 = (bf16[224,128]{1,0:T(8,128)(2,1)S(1)}, bf16[224,128]{1,0:T(8,128)(2,1)S(1)}, u32[]{:S(2)}, u32[]{:S(2)}) collective-permute-start(bf16[224,128]{1,0:T(8,128)(2,1)S(1)} %constant_dynamic-update-slice_fusion.refs_0_), channel_id=1, source_target_pairs={{0,65},{1,64},{64,1},{65,0},{128,193},{129,192},{192,129},{193,128... | collective-permute-start | bytes 172040 | tf_op jit(solution)/shard_map/ppermute | solution.py:269
  32.2 4.6 %collective-permute-start.10 = (bf16[64,256]{1,0:T(8,128)(2,1)S(1)}, bf16[64,256]{1,0:T(8,128)(2,1)S(1)}, u32[]{:S(2)}, u32[]{:S(2)}) collective-permute-start(bf16[64,256]{1,0:T(8,128)(2,1)S(1)} %attend.3), channel_id=1, source_target_pairs={{0,7},{1,6},{2,5},{3,4},{4,3},{5,2},{6,1},{7,0},{8,15},{9,14},{10,... | collective-permute-start | bytes 98312 | tf_op jit(solution)/shard_map/ppermute | solution.py:269
  35.1 4.3 %collective-permute-start.9 = (bf16[64,256]{1,0:T(8,128)(2,1)S(1)}, bf16[64,256]{1,0:T(8,128)(2,1)S(1)}, u32[]{:S(2)}, u32[]{:S(2)}) collective-permute-start(bf16[64,256]{1,0:T(8,128)(2,1)S(1)} %attend.3), channel_id=1, source_target_pairs={{0,4},{1,5},{2,6},{3,7},{4,0},{5,1},{6,2},{7,3},{8,12},{9,13},{10,... | collective-permute-start | bytes 98312 | tf_op jit(solution)/shard_map/ppermute | solution.py:269
  35.5 3.9 %collective-permute-start.8 = (bf16[64,256]{1,0:T(8,128)(2,1)S(1)}, bf16[64,256]{1,0:T(8,128)(2,1)S(1)}, u32[]{:S(2)}, u32[]{:S(2)}) collective-permute-start(bf16[64,256]{1,0:T(8,128)(2,1)S(1)} %attend.3), channel_id=1, source_target_pairs={{0,3},{1,2},{2,1},{3,0},{4,7},{5,6},{6,5},{7,4},{8,11},{9,10},{10,... | collective-permute-start | bytes 98312 | tf_op jit(solution)/shard_map/ppermute | solution.py:269
  39.4 6.1 %collective-permute-start.13 = (bf16[64,256]{1,0:T(8,128)(2,1)S(1)}, bf16[64,256]{1,0:T(8,128)(2,1)S(1)}, u32[]{:S(2)}, u32[]{:S(2)}) collective-permute-start(bf16[64,256]{1,0:T(8,128)(2,1)S(1)} %add_convert_fusion.2), channel_id=1, source_target_pairs={{0,49},{1,48},{16,33},{17,32},{32,17},{33,16},{48,1},{49,0},{2,51}... | collective-permute-start | bytes 98312 | tf_op jit(solution)/shard_map/ppermute | solution.py:269
  43.5 4.3 %collective-permute-start.12 = (bf16[64,256]{1,0:T(8,128)(2,1)S(1)}, bf16[64,256]{1,0:T(8,128)(2,1)S(1)}, u32[]{:S(2)}, u32[]{:S(2)}) collective-permute-start(bf16[64,256]{1,0:T(8,128)(2,1)S(1)} %add_convert_fusion.2), channel_id=1, source_target_pairs={{0,32},{1,33},{16,48},{17,49},{32,0},{33,1},{48,16},{49,17},{2,34}... | collective-permute-start | bytes 98312 | tf_op jit(solution)/shard_map/ppermute | solution.py:269
  44.1 3.7 %collective-permute-start.11 = (bf16[64,256]{1,0:T(8,128)(2,1)S(1)}, bf16[64,256]{1,0:T(8,128)(2,1)S(1)}, u32[]{:S(2)}, u32[]{:S(2)}) collective-permute-start(bf16[64,256]{1,0:T(8,128)(2,1)S(1)} %add_convert_fusion.2), channel_id=1, source_target_pairs={{0,17},{1,16},{16,1},{17,0},{32,49},{33,48},{48,33},{49,32},{2,19}... | collective-permute-start | bytes 98312 | tf_op jit(solution)/shard_map/ppermute | solution.py:269
  47.8 5.4 %collective-permute-start.17 = (bf16[64,256]{1,0:T(8,128)(2,1)S(1)}, bf16[64,256]{1,0:T(8,128)(2,1)S(1)}, u32[]{:S(2)}, u32[]{:S(2)}) collective-permute-start(bf16[64,256]{1,0:T(8,128)(2,1)S(1)} %get-tuple-element.12.refs_4_.refs_5_), channel_id=1, source_target_pairs={{0,193},{1,192},{64,129},{65,128},{128,65},{129,64},{192,1},{193,0... | collective-permute-start | bytes 98312 | tf_op jit(solution)/shard_map/ppermute | solution.py:269
  49.9 4.4 %collective-permute-start.16 = (bf16[64,256]{1,0:T(8,128)(2,1)S(1)}, bf16[64,256]{1,0:T(8,128)(2,1)S(1)}, u32[]{:S(2)}, u32[]{:S(2)}) collective-permute-start(bf16[64,256]{1,0:T(8,128)(2,1)S(1)} %get-tuple-element.12.refs_4_.refs_5_), channel_id=1, source_target_pairs={{0,129},{1,128},{64,193},{65,192},{128,1},{129,0},{192,65},{193,64... | collective-permute-start | bytes 98312 | tf_op jit(solution)/shard_map/ppermute | solution.py:269
  49.9 4.7 %collective-permute-start.15 = (bf16[64,256]{1,0:T(8,128)(2,1)S(1)}, bf16[64,256]{1,0:T(8,128)(2,1)S(1)}, u32[]{:S(2)}, u32[]{:S(2)}) collective-permute-start(bf16[64,256]{1,0:T(8,128)(2,1)S(1)} %get-tuple-element.12.refs_4_.refs_5_), channel_id=1, source_target_pairs={{0,65},{1,64},{64,1},{65,0},{128,193},{129,192},{192,129},{193,128... | collective-permute-start | bytes 98312 | tf_op jit(solution)/shard_map/ppermute | solution.py:269
  54.7 4.2 %collective-permute-start.18 = (bf16[4,64,256]{2,1,0:T(8,128)(2,1)S(1)}, bf16[4,64,256]{2,1,0:T(8,128)(2,1)S(1)}, u32[]{:S(2)}, u32[]{:S(2)}) collective-permute-start(bf16[4,64,256]{2,1,0:T(8,128)(2,1)S(1)} %pad_maximum_fusion.1), channel_id=1, source_target_pairs={{0,1},{1,0},{2,3},{3,2},{4,5},{5,4},{6,7},{7,6},{8,9},{9,8},{10,11... | collective-permute-start | bytes 393224 | tf_op jit(solution)/shard_map/ppermute | solution.py:281
  64.1 4.7 %collective-permute-start.21 = (bf16[64,256]{1,0:T(8,128)(2,1)S(1)}, bf16[64,256]{1,0:T(8,128)(2,1)S(1)}, u32[]{:S(2)}, u32[]{:S(2)}) collective-permute-start(bf16[64,256]{1,0:T(8,128)(2,1)S(1)} %attend.5), channel_id=1, source_target_pairs={{0,7},{1,6},{2,5},{3,4},{4,3},{5,2},{6,1},{7,0},{8,15},{9,14},{10,... | collective-permute-start | bytes 98312 | tf_op jit(solution)/shard_map/ppermute | solution.py:269
  65.4 4.3 %collective-permute-start.20 = (bf16[64,256]{1,0:T(8,128)(2,1)S(1)}, bf16[64,256]{1,0:T(8,128)(2,1)S(1)}, u32[]{:S(2)}, u32[]{:S(2)}) collective-permute-start(bf16[64,256]{1,0:T(8,128)(2,1)S(1)} %attend.5), channel_id=1, source_target_pairs={{0,4},{1,5},{2,6},{3,7},{4,0},{5,1},{6,2},{7,3},{8,12},{9,13},{10,... | collective-permute-start | bytes 98312 | tf_op jit(solution)/shard_map/ppermute | solution.py:269
  66.4 4.0 %collective-permute-start.19 = (bf16[64,256]{1,0:T(8,128)(2,1)S(1)}, bf16[64,256]{1,0:T(8,128)(2,1)S(1)}, u32[]{:S(2)}, u32[]{:S(2)}) collective-permute-start(bf16[64,256]{1,0:T(8,128)(2,1)S(1)} %attend.5), channel_id=1, source_target_pairs={{0,3},{1,2},{2,1},{3,0},{4,7},{5,6},{6,5},{7,4},{8,11},{9,10},{10,... | collective-permute-start | bytes 98312 | tf_op jit(solution)/shard_map/ppermute | solution.py:269
  70.5 4.7 %collective-permute-start.24 = (bf16[64,256]{1,0:T(8,128)(2,1)S(1)}, bf16[64,256]{1,0:T(8,128)(2,1)S(1)}, u32[]{:S(2)}, u32[]{:S(2)}) collective-permute-start(bf16[64,256]{1,0:T(8,128)(2,1)S(1)} %add_convert_fusion), channel_id=1, source_target_pairs={{0,49},{1,48},{16,33},{17,32},{32,17},{33,16},{48,1},{49,0},{2,51}... | collective-permute-start | bytes 98312 | tf_op jit(solution)/shard_map/ppermute | solution.py:269
  72.2 4.7 %collective-permute-start.23 = (bf16[64,256]{1,0:T(8,128)(2,1)S(1)}, bf16[64,256]{1,0:T(8,128)(2,1)S(1)}, u32[]{:S(2)}, u32[]{:S(2)}) collective-permute-start(bf16[64,256]{1,0:T(8,128)(2,1)S(1)} %add_convert_fusion), channel_id=1, source_target_pairs={{0,32},{1,33},{16,48},{17,49},{32,0},{33,1},{48,16},{49,17},{2,34}... | collective-permute-start | bytes 98312 | tf_op jit(solution)/shard_map/ppermute | solution.py:269
  73.2 3.6 %collective-permute-start.22 = (bf16[64,256]{1,0:T(8,128)(2,1)S(1)}, bf16[64,256]{1,0:T(8,128)(2,1)S(1)}, u32[]{:S(2)}, u32[]{:S(2)}) collective-permute-start(bf16[64,256]{1,0:T(8,128)(2,1)S(1)} %add_convert_fusion), channel_id=1, source_target_pairs={{0,17},{1,16},{16,1},{17,0},{32,49},{33,48},{48,33},{49,32},{2,19}... | collective-permute-start | bytes 98312 | tf_op jit(solution)/shard_map/ppermute | solution.py:269
  74.4 3.2 %collective-permute-start.14 = (bf16[64,256]{1,0:T(8,128)(2,1)S(1)}, bf16[64,256]{1,0:T(8,128)(2,1)S(1)}, u32[]{:S(2)}, u32[]{:S(2)}) collective-permute-start(bf16[64,256]{1,0:T(8,128)(2,1)S(1)} %get-tuple-element.13), channel_id=1, source_target_pairs={{0,1},{1,0},{2,3},{3,2},{4,5},{5,4},{6,7},{7,6},{8,9},{9,8},{10,11... | collective-permute-start | bytes 98312 | tf_op jit(solution)/shard_map/ppermute | solution.py:281
  (5 other events, 21.8 us)

commit v2 on v1

--- a/solution.py
+++ b/solution.py
@@ -193,7 +193,12 @@
         mains.append((jnp.where(upper, two, one), jnp.where(upper, one, two)))
         spreads.append(pack[part : part + chans])
 
-    tokens = jnp.concatenate([ref[...] for ref in token_refs] + [own_ref[...]], 1)
+    tokens = [
+        ref[at : at + chans] if ref.shape[1] == lanes else ref[:, 2 * at : 2 * at + lanes]
+        for ref in token_refs
+        for at in (0, chans)
+    ]
+    tokens = jnp.concatenate(tokens + [own_ref[...]], 1)
     wide = tokens.astype(f32)
     spread = dot(jnp.concatenate(spreads, 0), jnp.concatenate([tokens, tokens], 0))
     row = lax.broadcasted_iota(jnp.int32, (part - chans, size + rows), 0)
@@ -277,6 +282,10 @@
     return [value, one, two, three]
 
 
+def halve(tokens):
+    return jnp.concatenate([tokens[:, :lanes], tokens[:, lanes:]], 0)
+
+
 def other_core(value):
     return lax.ppermute(value, "tp", [(0, 1), (1, 0)])
 
@@ -294,26 +303,42 @@
 def shards(
     latent_noise, score_noise, gen_step, score_step, embed_weight, qkv_weight, mod_weight, head_out
 ):
-    model = lax.axis_index("mp")
+    chans = latent_noise.shape[1]
     gen_sigma = gen_step[0].astype(f32) / step_scale
     score_sigma = score_step[0].astype(f32) / step_scale
     latents, noise = latent_noise.T, score_noise.T
     odd = (lax.axis_index("x") + lax.axis_index("y")) % 2 == 1
 
-    first = swap(latents, "mp", 1, 1)
+    one = swap(latents, "mp", 1, 1)
     noise = jnp.where(odd, other_core(noise), noise)
     pack = fold_maps(
         gen_step, score_step, head_out[0, 0].T, embed_weight[0], mod_weight[0], qkv_weight[0, 0]
     )
-    pack, first, noise = lax.optimization_barrier((pack, first, noise))
-    other = swap(pack[:part], "zh", 1, 1)
-    pair = swap(jnp.stack([latents, first]), "mp", 2, 1)
-    packs = swap_all(jnp.concatenate([pack, other], 0), "mp", (1, 1, 1))
-    near = [latents, first, pair[0], pair[1]]
-    far = other_core(jnp.stack(near))
-
-    latents = jnp.where(odd, far[0], latents)
-    speed = add_heads(attend(((0, 1.0),), packs, latents, near + list(far)))
+    pack, latents, one, noise = lax.optimization_barrier((pack, latents, one, noise))
+    pack = jnp.concatenate([pack, swap(pack[:part], "zh", 1, 1)], 0)
+    two = halve(swap(latents, "mp", 2, 1))
+    second = lax.axis_index("tp") == 1
+    rows = pack.shape[0] // 2
+    half = jnp.where(second, pack[rows:], pack[:rows])
+    others = [
+        swap(jnp.concatenate([half, two], 0), "mp", 1, 1),
+        swap(half, "mp", 2, 1),
+        swap(half, "mp", 3, 1),
+    ]
+    others = lax.optimization_barrier(others)
+    near = [halve(latents), halve(one), two, others[0][rows:]]
+    mine = jnp.concatenate(near + [other[:rows] for other in others], 0)
+    theirs = other_core(mine)
+    far = [theirs[at : at + lanes] for at in range(0, 4 * lanes, lanes)]
+    packs = [pack]
+    for at in range(4 * lanes, mine.shape[0], rows):
+        here, there = mine[at : at + rows], theirs[at : at + rows]
+        packs.append(
+            jnp.concatenate([jnp.where(second, here, there), jnp.where(second, there, here)], 0)
+        )
+
+    latents = jnp.where(odd, jnp.concatenate([far[0][:chans], far[0][chans:]], 1), latents)
+    speed = add_heads(attend(((0, 1.0),), packs, latents, near + far))
     clean = latents.astype(f32) - gen_sigma * speed
     noisy = (1.0 - score_sigma) * clean + score_sigma * noise.astype(f32)
     near = swap_all(noisy.astype(bf16), "mp", (1, 1, 1))

time: 79.4 us -> 81.5 us (1.026)
  waiting for transfers between devices: 20.1 us -> 21.5 us
    ppermute x21, starting transfers between devices: 32.3 us -> 35.2 us  [swap(): lax.ppermute(value, axes, [(i, i ^ flip) for i in range(lax.axis_size(axe...]
    ppermute x5, starting transfers between devices: 4.78 us -> 2.45 us  [other_core(): return lax.ppermute(value, 'tp', [(0, 1), (1, 0)])]
    ppermute x21, waiting for transfers between devices: 18.5 us -> 20.2 us  [swap(): lax.ppermute(value, axes, [(i, i ^ flip) for i in range(lax.axis_size(axe...]
  transfers between devices with their start and end apart: 26 -> 26, of which waited for: 17 -> 18; matrix products, arithmetic and copies ran while one was open for 1% -> 1% of each run, Pallas kernels for 12% -> 12%
where the time goes in v2:
time: 81.5 us; the launch traced here: 81.3 us
  starting transfers between devices  37.7 us (46%)
  waiting for transfers between devices  21.5 us (26%)
  Pallas kernels  17.6 us (22%)
  between operations  2.17 us (3%)
  other arithmetic  1.47 us (2%)
  local copies, waits for them, and re-layouts  0.87 us (1%)
    ppermute x21, starting transfers between devices, swap(): lax.ppermute(value, axes, [(i, i ^ flip) for i in range(lax.axis_size(axe...  35.2 us
    ppermute x21, waiting for transfers between devices, swap(): lax.ppermute(value, axes, [(i, i ^ flip) for i in range(lax.axis_size(axe...  20.2 us
    pallas_call x3, Pallas kernels, attend(): pl.pallas_call(functools.partial(attend_kernel, terms, count, bool(state)...  11.8 us
    pallas_call x1, Pallas kernels, fold_maps(): pl.pallas_call(maps_kernel, in_specs=[pl.BlockSpec(memory_space=pltpu.SME...  5.81 us
    ppermute x5, starting transfers between devices, other_core(): return lax.ppermute(value, 'tp', [(0, 1), (1, 0)])  2.45 us
  transfers between devices with their start and end apart: 26, of which 18 were waited for; matrix products, arithmetic and copies ran while one was open for 1% of the time, Pallas kernels for 12%

profile of v2, /device:TPU:1, one launch (start us, length us, event | category | flops | bytes accessed | tf_op | source)
XLA Modules:
  0.0 81.3 jit_solution(4695261788145845375)
XLA Ops:
  0.6 3.1 %collective-permute-start = (bf16[64,256]{1,0:T(8,128)(2,1)}, bf16[64,256]{1,0:T(8,128)(2,1)S(1)}, u32[]{:S(2)}, u32[]{:S(2)}) collective-permute-start(bf16[64,256]{1,0:T(8,128)(2,1)} %bitcast.32), channel_id=1, source_target_pairs={{0,65},{1,64},{64,1},{65,0},{128,193},{129,192},{192,129},{193,128... | collective-permute-start | bytes 98312 | tf_op jit(solution)/shard_map/ppermute | solution.py:274
  6.1 5.8 %fold_maps.1 = bf16[144,128]{1,0:T(8,128)(2,1)S(1)} custom-call(s32[1]{0:T(128)S(6)} %copy.20.gen_ref, s32[1]{0:T(128)S(6)} %copy.21.score_ref, bf16[64,5120]{1,0:T(8,128)(2,1)} %bitcast.40, bf16[64,128]{1,0:T(8,128)(2,1)S(1)} %bitcast.31, bf16[256,10240]{1,0:T(8,128)(2,1)} %bitcast.38, bf16[384,5120]{1,0:T(8,128)(2,1)} %bitcast.39), custom_call_target="tpu_custom_call" | custom-call | flops 6000000000 | bytes 10000000 | tf_op jit(solution)/shard_map/fold_maps/pallas_call | solution.py:157
  12.0 3.2 %collective-permute-start.2 = (bf16[64,256]{1,0:T(8,128)(2,1)S(1)}, bf16[64,256]{1,0:T(8,128)(2,1)S(1)}, u32[]{:S(2)}, u32[]{:S(2)}) collective-permute-start(bf16[64,256]{1,0:T(8,128)(2,1)S(1)} %bitcast.33), channel_id=1, source_target_pairs={{0,129},{1,128},{64,193},{65,192},{128,1},{129,0},{192,65},{193,64... | collective-permute-start | bytes 98312 | tf_op jit(solution)/shard_map/ppermute | solution.py:274
  15.2 4.2 %collective-permute-start.3 = (bf16[80,128]{1,0:T(8,128)(2,1)S(1)}, bf16[80,128]{1,0:T(8,128)(2,1)S(1)}, u32[]{:S(2)}, u32[]{:S(2)}) collective-permute-start(bf16[80,128]{1,0:T(8,128)(2,1)S(1)} %slice.68), channel_id=1, source_target_pairs={{0,9},{1,8},{8,1},{9,0},{2,11},{3,10},{10,3},{11,2},{4,13},{5,12},... | collective-permute-start | bytes 61448 | tf_op jit(solution)/shard_map/ppermute | solution.py:274
  19.4 3.0 %collective-permute-done.3 = bf16[80,128]{1,0:T(8,128)(2,1)S(1)} collective-permute-done((bf16[80,128]{1,0:T(8,128)(2,1)S(1)}, bf16[80,128]{1,0:T(8,128)(2,1)S(1)}, u32[]{:S(2)}, u32[]{:S(2)}) %collective-permute-start.3) | collective-permute-done | bytes 20512 | tf_op jit(solution)/shard_map/ppermute | solution.py:274
  22.4 1.3 %collective-permute-start.6 = (bf16[112,128]{1,0:T(8,128)(2,1)S(1)}, bf16[112,128]{1,0:T(8,128)(2,1)S(1)}, u32[]{:S(2)}, u32[]{:S(2)}) collective-permute-start(bf16[112,128]{1,0:T(8,128)(2,1)S(1)} %slice_select_fusion), channel_id=1, source_target_pairs={{0,193},{1,192},{64,129},{65,128},{128,65},{129,64},{192,1},{193,0... | collective-permute-start | bytes 86024 | tf_op jit(solution)/shard_map/ppermute | solution.py:274
  24.3 2.0 %collective-permute-start.4 = (bf16[240,128]{1,0:T(8,128)(2,1)S(1)}, bf16[240,128]{1,0:T(8,128)(2,1)S(1)}, u32[]{:S(2)}, u32[]{:S(2)}) collective-permute-start(bf16[240,128]{1,0:T(8,128)(2,1)S(1)} %pad_maximum_fusion.1), channel_id=1, source_target_pairs={{0,65},{1,64},{64,1},{65,0},{128,193},{129,192},{192,129},{193,128... | collective-permute-start | bytes 184328 | tf_op jit(solution)/shard_map/ppermute | solution.py:274
  26.3 1.3 %collective-permute-done.6 = bf16[112,128]{1,0:T(8,128)(2,1)S(1)} collective-permute-done((bf16[112,128]{1,0:T(8,128)(2,1)S(1)}, bf16[112,128]{1,0:T(8,128)(2,1)S(1)}, u32[]{:S(2)}, u32[]{:S(2)}) %collective-permute-start.6) | collective-permute-done | bytes 28704 | tf_op jit(solution)/shard_map/ppermute | solution.py:274
  28.6 1.1 %collective-permute-done.4 = bf16[240,128]{1,0:T(8,128)(2,1)S(1)} collective-permute-done((bf16[240,128]{1,0:T(8,128)(2,1)S(1)}, bf16[240,128]{1,0:T(8,128)(2,1)S(1)}, u32[]{:S(2)}, u32[]{:S(2)}) %collective-permute-start.4) | collective-permute-done | bytes 61472 | tf_op jit(solution)/shard_map/ppermute | solution.py:274
  30.2 1.1 %collective-permute-done.7 = bf16[848,128]{1,0:T(8,128)(2,1)S(1)} collective-permute-done((bf16[848,128]{1,0:T(8,128)(2,1)S(1)}, bf16[848,128]{1,0:T(8,128)(2,1)S(1)}, u32[]{:S(2)}, u32[]{:S(2)}) %collective-permute-start.7) | collective-permute-done | bytes 217120 | tf_op jit(solution)/shard_map/ppermute | solution.py:290
  31.4 2.9 %attend.3 = bf16[64,256]{1,0:T(8,128)(2,1)S(1)} custom-call(bf16[224,128]{1,0:T(8,128)(2,1)S(1)} %constant_dynamic-update-slice_fusion.refs_0_, bf16[224,128]{1,0:T(8,128)(2,1)S(1)} %get-tuple-element.53.refs_1_, bf16[224,128]{1,0:T(8,128)(2,1)S(1)} %get-tuple-element.54.refs_2_, bf16[224,128]{1,0:T(8,128)(2,1)S(1)} %pad_maximum_fusion.4.refs_3_, ...), custom_call_target="tpu_custom_call" | custom-call | flops 2147483648 | bytes 1000000 | tf_op jit(solution)/shard_map/attend/pallas_call | solution.py:259
  34.4 3.1 %collective-permute-start.10 = (bf16[64,256]{1,0:T(8,128)(2,1)S(1)}, bf16[64,256]{1,0:T(8,128)(2,1)S(1)}, u32[]{:S(2)}, u32[]{:S(2)}) collective-permute-start(bf16[64,256]{1,0:T(8,128)(2,1)S(1)} %attend.3), channel_id=1, source_target_pairs={{0,7},{1,6},{2,5},{3,4},{4,3},{5,2},{6,1},{7,0},{8,15},{9,14},{10,... | collective-permute-start | bytes 98312 | tf_op jit(solution)/shard_map/ppermute | solution.py:274
  39.1 2.7 %collective-permute-done.9 = bf16[64,256]{1,0:T(8,128)(2,1)S(1)} collective-permute-done((bf16[64,256]{1,0:T(8,128)(2,1)S(1)}, bf16[64,256]{1,0:T(8,128)(2,1)S(1)}, u32[]{:S(2)}, u32[]{:S(2)}) %collective-permute-start.9) | collective-permute-done | bytes 32800 | tf_op jit(solution)/shard_map/ppermute | solution.py:274
  41.7 3.9 %collective-permute-start.13 = (bf16[64,256]{1,0:T(8,128)(2,1)S(1)}, bf16[64,256]{1,0:T(8,128)(2,1)S(1)}, u32[]{:S(2)}, u32[]{:S(2)}) collective-permute-start(bf16[64,256]{1,0:T(8,128)(2,1)S(1)} %add_convert_fusion.2), channel_id=1, source_target_pairs={{0,49},{1,48},{16,33},{17,32},{32,17},{33,16},{48,1},{49,0},{2,51}... | collective-permute-start | bytes 98312 | tf_op jit(solution)/shard_map/ppermute | solution.py:274
  47.7 2.2 %collective-permute-done.12 = bf16[64,256]{1,0:T(8,128)(2,1)S(1)} collective-permute-done((bf16[64,256]{1,0:T(8,128)(2,1)S(1)}, bf16[64,256]{1,0:T(8,128)(2,1)S(1)}, u32[]{:S(2)}, u32[]{:S(2)}) %collective-permute-start.12) | collective-permute-done | bytes 32800 | tf_op jit(solution)/shard_map/ppermute | solution.py:274
  51.9 2.1 %collective-permute-start.15 = (bf16[64,256]{1,0:T(8,128)(2,1)S(1)}, bf16[64,256]{1,0:T(8,128)(2,1)S(1)}, u32[]{:S(2)}, u32[]{:S(2)}) collective-permute-start(bf16[64,256]{1,0:T(8,128)(2,1)S(1)} %get-tuple-element.36.refs_4_.refs_5_), channel_id=1, source_target_pairs={{0,65},{1,64},{64,1},{65,0},{128,193},{129,192},{192,129},{193,128... | collective-permute-start | bytes 98312 | tf_op jit(solution)/shard_map/ppermute | solution.py:274
  54.0 1.5 %collective-permute-done.17.refs_8_ = bf16[64,256]{1,0:T(8,128)(2,1)S(1)} collective-permute-done((bf16[64,256]{1,0:T(8,128)(2,1)S(1)}, bf16[64,256]{1,0:T(8,128)(2,1)S(1)}, u32[]{:S(2)}, u32[]{:S(2)}) %collective-permute-start.17) | collective-permute-done | bytes 32800 | tf_op jit(solution)/shard_map/ppermute | solution.py:274
  55.5 1.2 %collective-permute-done.16.refs_7_ = bf16[64,256]{1,0:T(8,128)(2,1)S(1)} collective-permute-done((bf16[64,256]{1,0:T(8,128)(2,1)S(1)}, bf16[64,256]{1,0:T(8,128)(2,1)S(1)}, u32[]{:S(2)}, u32[]{:S(2)}) %collective-permute-start.16) | collective-permute-done | bytes 32800 | tf_op jit(solution)/shard_map/ppermute | solution.py:274
  57.3 3.7 %attend.4 = (f32[6,256,160]{2,1,0:T(8,128)S(1)}, f32[6,256,128]{2,1,0:T(8,128)S(1)}) custom-call(bf16[224,128]{1,0:T(8,128)(2,1)S(1)} %constant_dynamic-update-slice_fusion.refs_0_, bf16[224,128]{1,0:T(8,128)(2,1)S(1)} %get-tuple-element.53.refs_1_, bf16[224,128]{1,0:T(8,128)(2,1)S(1)} %get-tuple-element.54.refs_2_, ...), custom_call_target="tpu_custom_call" | custom-call | flops 3221225472 | bytes 1000000 | tf_op jit(solution)/shard_map/attend/pallas_call | solution.py:259
  61.0 5.2 %attend.5 = bf16[64,256]{1,0:T(8,128)(2,1)S(1)} custom-call(bf16[224,128]{1,0:T(8,128)(2,1)S(1)} %constant_dynamic-update-slice_fusion.refs_0_, bf16[224,128]{1,0:T(8,128)(2,1)S(1)} %get-tuple-element.53.refs_1_, bf16[224,128]{1,0:T(8,128)(2,1)S(1)} %get-tuple-element.54.refs_2_, bf16[224,128]{1,0:T(8,128)(2,1)S(1)} %pad_maximum_fusion.4.refs_3_, ...), custom_call_target="tpu_custom_call" | custom-call | flops 3221225472 | bytes 1000000 | tf_op jit(solution)/shard_map/attend/pallas_call | solution.py:259
  68.0 2.1 %collective-permute-start.19 = (bf16[64,256]{1,0:T(8,128)(2,1)S(1)}, bf16[64,256]{1,0:T(8,128)(2,1)S(1)}, u32[]{:S(2)}, u32[]{:S(2)}) collective-permute-start(bf16[64,256]{1,0:T(8,128)(2,1)S(1)} %attend.5), channel_id=1, source_target_pairs={{0,3},{1,2},{2,1},{3,0},{4,7},{5,6},{6,5},{7,4},{8,11},{9,10},{10,... | collective-permute-start | bytes 98312 | tf_op jit(solution)/shard_map/ppermute | solution.py:274
  72.3 1.9 %collective-permute-start.24 = (bf16[64,256]{1,0:T(8,128)(2,1)S(1)}, bf16[64,256]{1,0:T(8,128)(2,1)S(1)}, u32[]{:S(2)}, u32[]{:S(2)}) collective-permute-start(bf16[64,256]{1,0:T(8,128)(2,1)S(1)} %add_convert_fusion), channel_id=1, source_target_pairs={{0,49},{1,48},{16,33},{17,32},{32,17},{33,16},{48,1},{49,0},{2,51}... | collective-permute-start | bytes 98312 | tf_op jit(solution)/shard_map/ppermute | solution.py:274
  74.8 1.4 %collective-permute-start.22 = (bf16[64,256]{1,0:T(8,128)(2,1)S(1)}, bf16[64,256]{1,0:T(8,128)(2,1)S(1)}, u32[]{:S(2)}, u32[]{:S(2)}) collective-permute-start(bf16[64,256]{1,0:T(8,128)(2,1)S(1)} %add_convert_fusion), channel_id=1, source_target_pairs={{0,17},{1,16},{16,1},{17,0},{32,49},{33,48},{48,33},{49,32},{2,19}... | collective-permute-start | bytes 98312 | tf_op jit(solution)/shard_map/ppermute | solution.py:274
  77.0 1.5 %collective-permute-done.23 = bf16[64,256]{1,0:T(8,128)(2,1)S(1)} collective-permute-done((bf16[64,256]{1,0:T(8,128)(2,1)S(1)}, bf16[64,256]{1,0:T(8,128)(2,1)S(1)}, u32[]{:S(2)}, u32[]{:S(2)}) %collective-permute-start.23) | collective-permute-done | bytes 32800 | tf_op jit(solution)/shard_map/ppermute | solution.py:274
  (70 shorter events, 17.7 us)
Async XLA Ops:
  0.6 11.3 %collective-permute-start = (bf16[64,256]{1,0:T(8,128)(2,1)}, bf16[64,256]{1,0:T(8,128)(2,1)S(1)}, u32[]{:S(2)}, u32[]{:S(2)}) collective-permute-start(bf16[64,256]{1,0:T(8,128)(2,1)} %bitcast.32), channel_id=1, source_target_pairs={{0,65},{1,64},{64,1},{65,0},{128,193},{129,192},{192,129},{193,128... | collective-permute-start | bytes 98312 | tf_op jit(solution)/shard_map/ppermute | solution.py:274
  3.7 8.2 %collective-permute-start.1 = (bf16[64,256]{1,0:T(8,128)(2,1)}, bf16[64,256]{1,0:T(8,128)(2,1)S(1)}, u32[]{:S(2)}, u32[]{:S(2)}) collective-permute-start(bf16[64,256]{1,0:T(8,128)(2,1)} %bitcast.37), channel_id=1, source_target_pairs={{0,1},{1,0},{2,3},{3,2},{4,5},{5,4},{6,7},{7,6},{8,9},{9,8},{10,11... | collective-permute-start | bytes 98312 | tf_op jit(solution)/shard_map/ppermute | solution.py:290
  12.0 12.3 %collective-permute-start.2 = (bf16[64,256]{1,0:T(8,128)(2,1)S(1)}, bf16[64,256]{1,0:T(8,128)(2,1)S(1)}, u32[]{:S(2)}, u32[]{:S(2)}) collective-permute-start(bf16[64,256]{1,0:T(8,128)(2,1)S(1)} %bitcast.33), channel_id=1, source_target_pairs={{0,129},{1,128},{64,193},{65,192},{128,1},{129,0},{192,65},{193,64... | collective-permute-start | bytes 98312 | tf_op jit(solution)/shard_map/ppermute | solution.py:274
  15.2 7.2 %collective-permute-start.3 = (bf16[80,128]{1,0:T(8,128)(2,1)S(1)}, bf16[80,128]{1,0:T(8,128)(2,1)S(1)}, u32[]{:S(2)}, u32[]{:S(2)}) collective-permute-start(bf16[80,128]{1,0:T(8,128)(2,1)S(1)} %slice.68), channel_id=1, source_target_pairs={{0,9},{1,8},{8,1},{9,0},{2,11},{3,10},{10,3},{11,2},{4,13},{5,12},... | collective-permute-start | bytes 61448 | tf_op jit(solution)/shard_map/ppermute | solution.py:274
  22.4 5.2 %collective-permute-start.6 = (bf16[112,128]{1,0:T(8,128)(2,1)S(1)}, bf16[112,128]{1,0:T(8,128)(2,1)S(1)}, u32[]{:S(2)}, u32[]{:S(2)}) collective-permute-start(bf16[112,128]{1,0:T(8,128)(2,1)S(1)} %slice_select_fusion), channel_id=1, source_target_pairs={{0,193},{1,192},{64,129},{65,128},{128,65},{129,64},{192,1},{193,0... | collective-permute-start | bytes 86024 | tf_op jit(solution)/shard_map/ppermute | solution.py:274
  23.6 5.0 %collective-permute-start.5 = (bf16[112,128]{1,0:T(8,128)(2,1)S(1)}, bf16[112,128]{1,0:T(8,128)(2,1)S(1)}, u32[]{:S(2)}, u32[]{:S(2)}) collective-permute-start(bf16[112,128]{1,0:T(8,128)(2,1)S(1)} %slice_select_fusion), channel_id=1, source_target_pairs={{0,129},{1,128},{64,193},{65,192},{128,1},{129,0},{192,65},{193,64... | collective-permute-start | bytes 86024 | tf_op jit(solution)/shard_map/ppermute | solution.py:274
  24.3 5.4 %collective-permute-start.4 = (bf16[240,128]{1,0:T(8,128)(2,1)S(1)}, bf16[240,128]{1,0:T(8,128)(2,1)S(1)}, u32[]{:S(2)}, u32[]{:S(2)}) collective-permute-start(bf16[240,128]{1,0:T(8,128)(2,1)S(1)} %pad_maximum_fusion.1), channel_id=1, source_target_pairs={{0,65},{1,64},{64,1},{65,0},{128,193},{129,192},{192,129},{193,128... | collective-permute-start | bytes 184328 | tf_op jit(solution)/shard_map/ppermute | solution.py:274
  34.4 4.7 %collective-permute-start.10 = (bf16[64,256]{1,0:T(8,128)(2,1)S(1)}, bf16[64,256]{1,0:T(8,128)(2,1)S(1)}, u32[]{:S(2)}, u32[]{:S(2)}) collective-permute-start(bf16[64,256]{1,0:T(8,128)(2,1)S(1)} %attend.3), channel_id=1, source_target_pairs={{0,7},{1,6},{2,5},{3,4},{4,3},{5,2},{6,1},{7,0},{8,15},{9,14},{10,... | collective-permute-start | bytes 98312 | tf_op jit(solution)/shard_map/ppermute | solution.py:274
  37.5 4.3 %collective-permute-start.9 = (bf16[64,256]{1,0:T(8,128)(2,1)S(1)}, bf16[64,256]{1,0:T(8,128)(2,1)S(1)}, u32[]{:S(2)}, u32[]{:S(2)}) collective-permute-start(bf16[64,256]{1,0:T(8,128)(2,1)S(1)} %attend.3), channel_id=1, source_target_pairs={{0,4},{1,5},{2,6},{3,7},{4,0},{5,1},{6,2},{7,3},{8,12},{9,13},{10,... | collective-permute-start | bytes 98312 | tf_op jit(solution)/shard_map/ppermute | solution.py:274
  37.8 3.9 %collective-permute-start.8 = (bf16[64,256]{1,0:T(8,128)(2,1)S(1)}, bf16[64,256]{1,0:T(8,128)(2,1)S(1)}, u32[]{:S(2)}, u32[]{:S(2)}) collective-permute-start(bf16[64,256]{1,0:T(8,128)(2,1)S(1)} %attend.3), channel_id=1, source_target_pairs={{0,3},{1,2},{2,1},{3,0},{4,7},{5,6},{6,5},{7,4},{8,11},{9,10},{10,... | collective-permute-start | bytes 98312 | tf_op jit(solution)/shard_map/ppermute | solution.py:274
  41.7 6.0 %collective-permute-start.13 = (bf16[64,256]{1,0:T(8,128)(2,1)S(1)}, bf16[64,256]{1,0:T(8,128)(2,1)S(1)}, u32[]{:S(2)}, u32[]{:S(2)}) collective-permute-start(bf16[64,256]{1,0:T(8,128)(2,1)S(1)} %add_convert_fusion.2), channel_id=1, source_target_pairs={{0,49},{1,48},{16,33},{17,32},{32,17},{33,16},{48,1},{49,0},{2,51}... | collective-permute-start | bytes 98312 | tf_op jit(solution)/shard_map/ppermute | solution.py:274
  45.7 4.3 %collective-permute-start.12 = (bf16[64,256]{1,0:T(8,128)(2,1)S(1)}, bf16[64,256]{1,0:T(8,128)(2,1)S(1)}, u32[]{:S(2)}, u32[]{:S(2)}) collective-permute-start(bf16[64,256]{1,0:T(8,128)(2,1)S(1)} %add_convert_fusion.2), channel_id=1, source_target_pairs={{0,32},{1,33},{16,48},{17,49},{32,0},{33,1},{48,16},{49,17},{2,34}... | collective-permute-start | bytes 98312 | tf_op jit(solution)/shard_map/ppermute | solution.py:274
  46.2 3.8 %collective-permute-start.11 = (bf16[64,256]{1,0:T(8,128)(2,1)S(1)}, bf16[64,256]{1,0:T(8,128)(2,1)S(1)}, u32[]{:S(2)}, u32[]{:S(2)}) collective-permute-start(bf16[64,256]{1,0:T(8,128)(2,1)S(1)} %add_convert_fusion.2), channel_id=1, source_target_pairs={{0,17},{1,16},{16,1},{17,0},{32,49},{33,48},{48,33},{49,32},{2,19}... | collective-permute-start | bytes 98312 | tf_op jit(solution)/shard_map/ppermute | solution.py:274
  50.0 5.5 %collective-permute-start.17 = (bf16[64,256]{1,0:T(8,128)(2,1)S(1)}, bf16[64,256]{1,0:T(8,128)(2,1)S(1)}, u32[]{:S(2)}, u32[]{:S(2)}) collective-permute-start(bf16[64,256]{1,0:T(8,128)(2,1)S(1)} %get-tuple-element.36.refs_4_.refs_5_), channel_id=1, source_target_pairs={{0,193},{1,192},{64,129},{65,128},{128,65},{129,64},{192,1},{193,0... | collective-permute-start | bytes 98312 | tf_op jit(solution)/shard_map/ppermute | solution.py:274
  50.9 5.8 %collective-permute-start.16 = (bf16[64,256]{1,0:T(8,128)(2,1)S(1)}, bf16[64,256]{1,0:T(8,128)(2,1)S(1)}, u32[]{:S(2)}, u32[]{:S(2)}) collective-permute-start(bf16[64,256]{1,0:T(8,128)(2,1)S(1)} %get-tuple-element.36.refs_4_.refs_5_), channel_id=1, source_target_pairs={{0,129},{1,128},{64,193},{65,192},{128,1},{129,0},{192,65},{193,64... | collective-permute-start | bytes 98312 | tf_op jit(solution)/shard_map/ppermute | solution.py:274
  51.9 4.9 %collective-permute-start.15 = (bf16[64,256]{1,0:T(8,128)(2,1)S(1)}, bf16[64,256]{1,0:T(8,128)(2,1)S(1)}, u32[]{:S(2)}, u32[]{:S(2)}) collective-permute-start(bf16[64,256]{1,0:T(8,128)(2,1)S(1)} %get-tuple-element.36.refs_4_.refs_5_), channel_id=1, source_target_pairs={{0,65},{1,64},{64,1},{65,0},{128,193},{129,192},{192,129},{193,128... | collective-permute-start | bytes 98312 | tf_op jit(solution)/shard_map/ppermute | solution.py:274
  56.8 4.2 %collective-permute-start.18 = (bf16[4,64,256]{2,1,0:T(8,128)(2,1)S(1)}, bf16[4,64,256]{2,1,0:T(8,128)(2,1)S(1)}, u32[]{:S(2)}, u32[]{:S(2)}) collective-permute-start(bf16[4,64,256]{2,1,0:T(8,128)(2,1)S(1)} %pad_maximum_fusion), channel_id=1, source_target_pairs={{0,1},{1,0},{2,3},{3,2},{4,5},{5,4},{6,7},{7,6},{8,9},{9,8},{10,11... | collective-permute-start | bytes 393224 | tf_op jit(solution)/shard_map/ppermute | solution.py:290
  66.2 4.6 %collective-permute-start.21 = (bf16[64,256]{1,0:T(8,128)(2,1)S(1)}, bf16[64,256]{1,0:T(8,128)(2,1)S(1)}, u32[]{:S(2)}, u32[]{:S(2)}) collective-permute-start(bf16[64,256]{1,0:T(8,128)(2,1)S(1)} %attend.5), channel_id=1, source_target_pairs={{0,7},{1,6},{2,5},{3,4},{4,3},{5,2},{6,1},{7,0},{8,15},{9,14},{10,... | collective-permute-start | bytes 98312 | tf_op jit(solution)/shard_map/ppermute | solution.py:274
  67.3 4.3 %collective-permute-start.20 = (bf16[64,256]{1,0:T(8,128)(2,1)S(1)}, bf16[64,256]{1,0:T(8,128)(2,1)S(1)}, u32[]{:S(2)}, u32[]{:S(2)}) collective-permute-start(bf16[64,256]{1,0:T(8,128)(2,1)S(1)} %attend.5), channel_id=1, source_target_pairs={{0,4},{1,5},{2,6},{3,7},{4,0},{5,1},{6,2},{7,3},{8,12},{9,13},{10,... | collective-permute-start | bytes 98312 | tf_op jit(solution)/shard_map/ppermute | solution.py:274
  68.0 4.3 %collective-permute-start.19 = (bf16[64,256]{1,0:T(8,128)(2,1)S(1)}, bf16[64,256]{1,0:T(8,128)(2,1)S(1)}, u32[]{:S(2)}, u32[]{:S(2)}) collective-permute-start(bf16[64,256]{1,0:T(8,128)(2,1)S(1)} %attend.5), channel_id=1, source_target_pairs={{0,3},{1,2},{2,1},{3,0},{4,7},{5,6},{6,5},{7,4},{8,11},{9,10},{10,... | collective-permute-start | bytes 98312 | tf_op jit(solution)/shard_map/ppermute | solution.py:274
  72.3 4.7 %collective-permute-start.24 = (bf16[64,256]{1,0:T(8,128)(2,1)S(1)}, bf16[64,256]{1,0:T(8,128)(2,1)S(1)}, u32[]{:S(2)}, u32[]{:S(2)}) collective-permute-start(bf16[64,256]{1,0:T(8,128)(2,1)S(1)} %add_convert_fusion), channel_id=1, source_target_pairs={{0,49},{1,48},{16,33},{17,32},{32,17},{33,16},{48,1},{49,0},{2,51}... | collective-permute-start | bytes 98312 | tf_op jit(solution)/shard_map/ppermute | solution.py:274
  74.2 4.3 %collective-permute-start.23 = (bf16[64,256]{1,0:T(8,128)(2,1)S(1)}, bf16[64,256]{1,0:T(8,128)(2,1)S(1)}, u32[]{:S(2)}, u32[]{:S(2)}) collective-permute-start(bf16[64,256]{1,0:T(8,128)(2,1)S(1)} %add_convert_fusion), channel_id=1, source_target_pairs={{0,32},{1,33},{16,48},{17,49},{32,0},{33,1},{48,16},{49,17},{2,34}... | collective-permute-start | bytes 98312 | tf_op jit(solution)/shard_map/ppermute | solution.py:274
  74.8 4.0 %collective-permute-start.22 = (bf16[64,256]{1,0:T(8,128)(2,1)S(1)}, bf16[64,256]{1,0:T(8,128)(2,1)S(1)}, u32[]{:S(2)}, u32[]{:S(2)}) collective-permute-start(bf16[64,256]{1,0:T(8,128)(2,1)S(1)} %add_convert_fusion), channel_id=1, source_target_pairs={{0,17},{1,16},{16,1},{17,0},{32,49},{33,48},{48,33},{49,32},{2,19}... | collective-permute-start | bytes 98312 | tf_op jit(solution)/shard_map/ppermute | solution.py:274
  76.2 3.6 %collective-permute-start.14 = (bf16[64,256]{1,0:T(8,128)(2,1)S(1)}, bf16[64,256]{1,0:T(8,128)(2,1)S(1)}, u32[]{:S(2)}, u32[]{:S(2)}) collective-permute-start(bf16[64,256]{1,0:T(8,128)(2,1)S(1)} %get-tuple-element.37), channel_id=1, source_target_pairs={{0,1},{1,0},{2,3},{3,2},{4,5},{5,4},{6,7},{7,6},{8,9},{9,8},{10,11... | collective-permute-start | bytes 98312 | tf_op jit(solution)/shard_map/ppermute | solution.py:290
  (5 other events, 15.9 us)

commit v3 on v1

--- a/solution.py
+++ b/solution.py
@@ -217,6 +217,9 @@
             logits.append(dot(queries, keys_ref[slot], (0, 0)))
 
     total = None
+    unit = lax.broadcasted_iota(jnp.int32, (part, lanes), 1) == 0
+    pick = lax.broadcasted_iota(jnp.int32, (part, lanes), 0) == chans
+    pick = jnp.where(pick, 1.0, 0.0).astype(bf16)
     for place, scores in enumerate(logits):
         slot, head = divmod(place, 2)
         peak = jnp.broadcast_to(jnp.max(scores, 1, keepdims=True), (rows, lanes))
@@ -230,9 +233,9 @@
             factor = jnp.concatenate([factor, factor[:, : 2 * part - lanes]], 1)
             mixed += refs[5 + count][place] * factor
         if last:
-            mixed = (mixed / mixed[:, chans : chans + 1]).astype(bf16)
-            main = jnp.concatenate([mains[slot][head]] * 2, 0)
-            term = terms[slot][1] * dot(main, mixed, (0, 1))[chans:]
+            main = jnp.concatenate([jnp.where(unit, pick, mains[slot][head])] * 2, 0)
+            term = dot(main, mixed.astype(bf16), (0, 1))
+            term = term[chans:] * (terms[slot][1] / term[:1])
             total = term if total is None else total + term
         else:
             refs[-3][place] = mixed

time: 79.4 us -> 79.2 us (level)
  no operation moved by 1% of the time
where the time goes in v3:
time: 79.2 us; the launch traced here: 79 us
  starting transfers between devices  37.1 us (47%)
  waiting for transfers between devices  20.2 us (26%)
  Pallas kernels  17.5 us (22%)
  between operations  2.13 us (3%)
  other arithmetic  1.42 us (2%)
    ppermute x21, starting transfers between devices, swap(): lax.ppermute(value, axes, [(i, i ^ flip) for i in range(lax.axis_size(axe...  32.4 us
    ppermute x21, waiting for transfers between devices, swap(): lax.ppermute(value, axes, [(i, i ^ flip) for i in range(lax.axis_size(axe...  18.6 us
    pallas_call x3, Pallas kernels, attend(): pl.pallas_call(functools.partial(attend_kernel, terms, count, bool(state)...  11.7 us
    pallas_call x1, Pallas kernels, fold_maps(): pl.pallas_call(maps_kernel, in_specs=[pl.BlockSpec(memory_space=pltpu.SME...  5.81 us
    ppermute x5, starting transfers between devices, other_core(): return lax.ppermute(value, 'tp', [(0, 1), (1, 0)])  4.73 us
    ppermute x5, waiting for transfers between devices, other_core(): return lax.ppermute(value, 'tp', [(0, 1), (1, 0)])  1.6 us
  transfers between devices with their start and end apart: 26, of which 17 were waited for; matrix products, arithmetic and copies ran while one was open for 1% of the time, Pallas kernels for 12%

profile of v3, /device:TPU:1, one launch (start us, length us, event | category | flops | bytes accessed | tf_op | source)
XLA Modules:
  0.0 79.0 jit_solution(14426068082745807211)
XLA Ops:
  0.6 3.3 %collective-permute-start.1 = (bf16[64,256]{1,0:T(8,128)(2,1)}, bf16[64,256]{1,0:T(8,128)(2,1)S(1)}, u32[]{:S(2)}, u32[]{:S(2)}) collective-permute-start(bf16[64,256]{1,0:T(8,128)(2,1)} %bitcast.56), channel_id=1, source_target_pairs={{0,1},{1,0},{2,3},{3,2},{4,5},{5,4},{6,7},{7,6},{8,9},{9,8},{10,11... | collective-permute-start | bytes 98312 | tf_op jit(solution)/shard_map/ppermute | solution.py:284
  6.0 5.8 %fold_maps.1 = bf16[144,128]{1,0:T(8,128)(2,1)S(1)} custom-call(s32[1]{0:T(128)S(6)} %copy.11.gen_ref, s32[1]{0:T(128)S(6)} %copy.12.score_ref, bf16[64,5120]{1,0:T(8,128)(2,1)} %bitcast.59, bf16[64,128]{1,0:T(8,128)(2,1)S(1)} %bitcast.55, bf16[256,10240]{1,0:T(8,128)(2,1)} %bitcast.57, bf16[384,5120]{1,0:T(8,128)(2,1)} %bitcast.58), custom_call_target="tpu_custom_call" | custom-call | flops 6000000000 | bytes 10000000 | tf_op jit(solution)/shard_map/fold_maps/pallas_call | solution.py:157
  11.9 6.3 %collective-permute-start.4 = (bf16[80,128]{1,0:T(8,128)(2,1)S(1)}, bf16[80,128]{1,0:T(8,128)(2,1)S(1)}, u32[]{:S(2)}, u32[]{:S(2)}) collective-permute-start(bf16[80,128]{1,0:T(8,128)(2,1)S(1)} %slice.14), channel_id=1, source_target_pairs={{0,9},{1,8},{8,1},{9,0},{2,11},{3,10},{10,3},{11,2},{4,13},{5,12},... | collective-permute-start | bytes 61448 | tf_op jit(solution)/shard_map/ppermute | solution.py:272
  18.2 1.2 %collective-permute-start.2 = (bf16[2,64,256]{2,1,0:T(8,128)(2,1)S(1)}, bf16[2,64,256]{2,1,0:T(8,128)(2,1)S(1)}, u32[]{:S(2)}, u32[]{:S(2)}) collective-permute-start(bf16[2,64,256]{2,1,0:T(8,128)(2,1)S(1)} %pad_maximum_fusion.2), channel_id=1, source_target_pairs={{0,129},{1,128},{64,193},{65,192},{128,1},{129,0},{192,65},{193,64... | collective-permute-start | bytes 196616 | tf_op jit(solution)/shard_map/ppermute | solution.py:272
  19.8 2.1 %collective-permute-start.7 = (bf16[224,128]{1,0:T(8,128)(2,1)S(1)}, bf16[224,128]{1,0:T(8,128)(2,1)S(1)}, u32[]{:S(2)}, u32[]{:S(2)}) collective-permute-start(bf16[224,128]{1,0:T(8,128)(2,1)S(1)} %constant_dynamic-update-slice_fusion.refs_0_), channel_id=1, source_target_pairs={{0,193},{1,192},{64,129},{65,128},{128,65},{129,64},{192,1},{193,0... | collective-permute-start | bytes 172040 | tf_op jit(solution)/shard_map/ppermute | solution.py:272
  22.7 1.0 %collective-permute-start.5 = (bf16[224,128]{1,0:T(8,128)(2,1)S(1)}, bf16[224,128]{1,0:T(8,128)(2,1)S(1)}, u32[]{:S(2)}, u32[]{:S(2)}) collective-permute-start(bf16[224,128]{1,0:T(8,128)(2,1)S(1)} %constant_dynamic-update-slice_fusion.refs_0_), channel_id=1, source_target_pairs={{0,65},{1,64},{64,1},{65,0},{128,193},{129,192},{192,129},{193,128... | collective-permute-start | bytes 172040 | tf_op jit(solution)/shard_map/ppermute | solution.py:272
  23.7 3.3 %collective-permute-done.2 = bf16[2,64,256]{2,1,0:T(8,128)(2,1)S(1)} collective-permute-done((bf16[2,64,256]{2,1,0:T(8,128)(2,1)S(1)}, bf16[2,64,256]{2,1,0:T(8,128)(2,1)S(1)}, u32[]{:S(2)}, u32[]{:S(2)}) %collective-permute-start.2) | collective-permute-done | bytes 65568 | tf_op jit(solution)/shard_map/ppermute | solution.py:272
  27.1 1.3 %collective-permute-done.3 = bf16[4,64,256]{2,1,0:T(8,128)(2,1)S(1)} collective-permute-done((bf16[4,64,256]{2,1,0:T(8,128)(2,1)S(1)}, bf16[4,64,256]{2,1,0:T(8,128)(2,1)S(1)}, u32[]{:S(2)}, u32[]{:S(2)}) %collective-permute-start.3) | collective-permute-done | bytes 131104 | tf_op jit(solution)/shard_map/ppermute | solution.py:284
  29.3 2.8 %attend.3 = bf16[64,256]{1,0:T(8,128)(2,1)S(1)} custom-call(bf16[224,128]{1,0:T(8,128)(2,1)S(1)} %constant_dynamic-update-slice_fusion.refs_0_, bf16[224,128]{1,0:T(8,128)(2,1)S(1)} %collective-permute-done.5.refs_1_, bf16[224,128]{1,0:T(8,128)(2,1)S(1)} %collective-permute-done.6.refs_2_, bf16[224,128]{1,0:T(8,128)(2,1)S(1)} %collective-permute-done.7.refs_3_, ...), custom_call_target="tpu_custom_call" | custom-call | flops 2147483648 | bytes 1000000 | tf_op jit(solution)/shard_map/attend/pallas_call | solution.py:257
  32.1 2.9 %collective-permute-start.10 = (bf16[64,256]{1,0:T(8,128)(2,1)S(1)}, bf16[64,256]{1,0:T(8,128)(2,1)S(1)}, u32[]{:S(2)}, u32[]{:S(2)}) collective-permute-start(bf16[64,256]{1,0:T(8,128)(2,1)S(1)} %attend.3), channel_id=1, source_target_pairs={{0,7},{1,6},{2,5},{3,4},{4,3},{5,2},{6,1},{7,0},{8,15},{9,14},{10,... | collective-permute-start | bytes 98312 | tf_op jit(solution)/shard_map/ppermute | solution.py:272
  36.7 2.6 %collective-permute-done.9 = bf16[64,256]{1,0:T(8,128)(2,1)S(1)} collective-permute-done((bf16[64,256]{1,0:T(8,128)(2,1)S(1)}, bf16[64,256]{1,0:T(8,128)(2,1)S(1)}, u32[]{:S(2)}, u32[]{:S(2)}) %collective-permute-start.9) | collective-permute-done | bytes 32800 | tf_op jit(solution)/shard_map/ppermute | solution.py:272
  39.3 4.1 %collective-permute-start.13 = (bf16[64,256]{1,0:T(8,128)(2,1)S(1)}, bf16[64,256]{1,0:T(8,128)(2,1)S(1)}, u32[]{:S(2)}, u32[]{:S(2)}) collective-permute-start(bf16[64,256]{1,0:T(8,128)(2,1)S(1)} %add_convert_fusion.2), channel_id=1, source_target_pairs={{0,49},{1,48},{16,33},{17,32},{32,17},{33,16},{48,1},{49,0},{2,51}... | collective-permute-start | bytes 98312 | tf_op jit(solution)/shard_map/ppermute | solution.py:272
  45.4 2.2 %collective-permute-done.12 = bf16[64,256]{1,0:T(8,128)(2,1)S(1)} collective-permute-done((bf16[64,256]{1,0:T(8,128)(2,1)S(1)}, bf16[64,256]{1,0:T(8,128)(2,1)S(1)}, u32[]{:S(2)}, u32[]{:S(2)}) %collective-permute-start.12) | collective-permute-done | bytes 32800 | tf_op jit(solution)/shard_map/ppermute | solution.py:272
  47.7 2.1 %collective-permute-start.17 = (bf16[64,256]{1,0:T(8,128)(2,1)S(1)}, bf16[64,256]{1,0:T(8,128)(2,1)S(1)}, u32[]{:S(2)}, u32[]{:S(2)}) collective-permute-start(bf16[64,256]{1,0:T(8,128)(2,1)S(1)} %get-tuple-element.12.refs_4_.refs_5_), channel_id=1, source_target_pairs={{0,193},{1,192},{64,129},{65,128},{128,65},{129,64},{192,1},{193,0... | collective-permute-start | bytes 98312 | tf_op jit(solution)/shard_map/ppermute | solution.py:272
  49.8 1.9 %collective-permute-start.15 = (bf16[64,256]{1,0:T(8,128)(2,1)S(1)}, bf16[64,256]{1,0:T(8,128)(2,1)S(1)}, u32[]{:S(2)}, u32[]{:S(2)}) collective-permute-start(bf16[64,256]{1,0:T(8,128)(2,1)S(1)} %get-tuple-element.12.refs_4_.refs_5_), channel_id=1, source_target_pairs={{0,65},{1,64},{64,1},{65,0},{128,193},{129,192},{192,129},{193,128... | collective-permute-start | bytes 98312 | tf_op jit(solution)/shard_map/ppermute | solution.py:272
  51.7 1.4 %collective-permute-done.17.refs_8_ = bf16[64,256]{1,0:T(8,128)(2,1)S(1)} collective-permute-done((bf16[64,256]{1,0:T(8,128)(2,1)S(1)}, bf16[64,256]{1,0:T(8,128)(2,1)S(1)}, u32[]{:S(2)}, u32[]{:S(2)}) %collective-permute-start.17) | collective-permute-done | bytes 32800 | tf_op jit(solution)/shard_map/ppermute | solution.py:272
  53.1 1.1 %collective-permute-done.16.refs_7_ = bf16[64,256]{1,0:T(8,128)(2,1)S(1)} collective-permute-done((bf16[64,256]{1,0:T(8,128)(2,1)S(1)}, bf16[64,256]{1,0:T(8,128)(2,1)S(1)}, u32[]{:S(2)}, u32[]{:S(2)}) %collective-permute-start.16) | collective-permute-done | bytes 32800 | tf_op jit(solution)/shard_map/ppermute | solution.py:272
  54.7 3.7 %attend.4 = (f32[6,256,160]{2,1,0:T(8,128)S(1)}, f32[6,256,128]{2,1,0:T(8,128)S(1)}) custom-call(bf16[224,128]{1,0:T(8,128)(2,1)S(1)} %constant_dynamic-update-slice_fusion.refs_0_, bf16[224,128]{1,0:T(8,128)(2,1)S(1)} %collective-permute-done.5.refs_1_, bf16[224,128]{1,0:T(8,128)(2,1)S(1)} %collective-permute-done.6.refs_2_, ...), custom_call_target="tpu_custom_call" | custom-call | flops 3221225472 | bytes 1000000 | tf_op jit(solution)/shard_map/attend/pallas_call | solution.py:257
  58.5 5.2 %attend.5 = bf16[64,256]{1,0:T(8,128)(2,1)S(1)} custom-call(bf16[224,128]{1,0:T(8,128)(2,1)S(1)} %constant_dynamic-update-slice_fusion.refs_0_, bf16[224,128]{1,0:T(8,128)(2,1)S(1)} %collective-permute-done.5.refs_1_, bf16[224,128]{1,0:T(8,128)(2,1)S(1)} %collective-permute-done.6.refs_2_, bf16[224,128]{1,0:T(8,128)(2,1)S(1)} %collective-permute-done.7.refs_3_, ...), custom_call_target="tpu_custom_call" | custom-call | flops 3221225472 | bytes 1000000 | tf_op jit(solution)/shard_map/attend/pallas_call | solution.py:257
  63.7 1.6 %collective-permute-start.21 = (bf16[64,256]{1,0:T(8,128)(2,1)S(1)}, bf16[64,256]{1,0:T(8,128)(2,1)S(1)}, u32[]{:S(2)}, u32[]{:S(2)}) collective-permute-start(bf16[64,256]{1,0:T(8,128)(2,1)S(1)} %attend.5), channel_id=1, source_target_pairs={{0,7},{1,6},{2,5},{3,4},{4,3},{5,2},{6,1},{7,0},{8,15},{9,14},{10,... | collective-permute-start | bytes 98312 | tf_op jit(solution)/shard_map/ppermute | solution.py:272
  66.3 1.3 %collective-permute-start.19 = (bf16[64,256]{1,0:T(8,128)(2,1)S(1)}, bf16[64,256]{1,0:T(8,128)(2,1)S(1)}, u32[]{:S(2)}, u32[]{:S(2)}) collective-permute-start(bf16[64,256]{1,0:T(8,128)(2,1)S(1)} %attend.5), channel_id=1, source_target_pairs={{0,3},{1,2},{2,1},{3,0},{4,7},{5,6},{6,5},{7,4},{8,11},{9,10},{10,... | collective-permute-start | bytes 98312 | tf_op jit(solution)/shard_map/ppermute | solution.py:272
  68.3 1.2 %collective-permute-done.20 = bf16[64,256]{1,0:T(8,128)(2,1)S(1)} collective-permute-done((bf16[64,256]{1,0:T(8,128)(2,1)S(1)}, bf16[64,256]{1,0:T(8,128)(2,1)S(1)}, u32[]{:S(2)}, u32[]{:S(2)}) %collective-permute-start.20) | collective-permute-done | bytes 32800 | tf_op jit(solution)/shard_map/ppermute | solution.py:272
  70.2 1.9 %collective-permute-start.24 = (bf16[64,256]{1,0:T(8,128)(2,1)S(1)}, bf16[64,256]{1,0:T(8,128)(2,1)S(1)}, u32[]{:S(2)}, u32[]{:S(2)}) collective-permute-start(bf16[64,256]{1,0:T(8,128)(2,1)S(1)} %add_convert_fusion), channel_id=1, source_target_pairs={{0,49},{1,48},{16,33},{17,32},{32,17},{33,16},{48,1},{49,0},{2,51}... | collective-permute-start | bytes 98312 | tf_op jit(solution)/shard_map/ppermute | solution.py:272
  75.1 1.7 %collective-permute-done.23 = bf16[64,256]{1,0:T(8,128)(2,1)S(1)} collective-permute-done((bf16[64,256]{1,0:T(8,128)(2,1)S(1)}, bf16[64,256]{1,0:T(8,128)(2,1)S(1)}, u32[]{:S(2)}, u32[]{:S(2)}) %collective-permute-start.23) | collective-permute-done | bytes 32800 | tf_op jit(solution)/shard_map/ppermute | solution.py:272
  (55 shorter events, 15.0 us)
Async XLA Ops:
  0.6 11.2 %collective-permute-start.1 = (bf16[64,256]{1,0:T(8,128)(2,1)}, bf16[64,256]{1,0:T(8,128)(2,1)S(1)}, u32[]{:S(2)}, u32[]{:S(2)}) collective-permute-start(bf16[64,256]{1,0:T(8,128)(2,1)} %bitcast.56), channel_id=1, source_target_pairs={{0,1},{1,0},{2,3},{3,2},{4,5},{5,4},{6,7},{7,6},{8,9},{9,8},{10,11... | collective-permute-start | bytes 98312 | tf_op jit(solution)/shard_map/ppermute | solution.py:284
  4.0 7.9 %collective-permute-start = (bf16[64,256]{1,0:T(8,128)(2,1)}, bf16[64,256]{1,0:T(8,128)(2,1)S(1)}, u32[]{:S(2)}, u32[]{:S(2)}) collective-permute-start(bf16[64,256]{1,0:T(8,128)(2,1)} %bitcast.45), channel_id=1, source_target_pairs={{0,65},{1,64},{64,1},{65,0},{128,193},{129,192},{192,129},{193,128... | collective-permute-start | bytes 98312 | tf_op jit(solution)/shard_map/ppermute | solution.py:272
  11.9 7.9 %collective-permute-start.4 = (bf16[80,128]{1,0:T(8,128)(2,1)S(1)}, bf16[80,128]{1,0:T(8,128)(2,1)S(1)}, u32[]{:S(2)}, u32[]{:S(2)}) collective-permute-start(bf16[80,128]{1,0:T(8,128)(2,1)S(1)} %slice.14), channel_id=1, source_target_pairs={{0,9},{1,8},{8,1},{9,0},{2,11},{3,10},{10,3},{11,2},{4,13},{5,12},... | collective-permute-start | bytes 61448 | tf_op jit(solution)/shard_map/ppermute | solution.py:272
  18.2 8.8 %collective-permute-start.2 = (bf16[2,64,256]{2,1,0:T(8,128)(2,1)S(1)}, bf16[2,64,256]{2,1,0:T(8,128)(2,1)S(1)}, u32[]{:S(2)}, u32[]{:S(2)}) collective-permute-start(bf16[2,64,256]{2,1,0:T(8,128)(2,1)S(1)} %pad_maximum_fusion.2), channel_id=1, source_target_pairs={{0,129},{1,128},{64,193},{65,192},{128,1},{129,0},{192,65},{193,64... | collective-permute-start | bytes 196616 | tf_op jit(solution)/shard_map/ppermute | solution.py:272
  19.8 8.7 %collective-permute-start.7 = (bf16[224,128]{1,0:T(8,128)(2,1)S(1)}, bf16[224,128]{1,0:T(8,128)(2,1)S(1)}, u32[]{:S(2)}, u32[]{:S(2)}) collective-permute-start(bf16[224,128]{1,0:T(8,128)(2,1)S(1)} %constant_dynamic-update-slice_fusion.refs_0_), channel_id=1, source_target_pairs={{0,193},{1,192},{64,129},{65,128},{128,65},{129,64},{192,1},{193,0... | collective-permute-start | bytes 172040 | tf_op jit(solution)/shard_map/ppermute | solution.py:272
  21.8 7.5 %collective-permute-start.6 = (bf16[224,128]{1,0:T(8,128)(2,1)S(1)}, bf16[224,128]{1,0:T(8,128)(2,1)S(1)}, u32[]{:S(2)}, u32[]{:S(2)}) collective-permute-start(bf16[224,128]{1,0:T(8,128)(2,1)S(1)} %constant_dynamic-update-slice_fusion.refs_0_), channel_id=1, source_target_pairs={{0,129},{1,128},{64,193},{65,192},{128,1},{129,0},{192,65},{193,64... | collective-permute-start | bytes 172040 | tf_op jit(solution)/shard_map/ppermute | solution.py:272
  22.7 6.6 %collective-permute-start.5 = (bf16[224,128]{1,0:T(8,128)(2,1)S(1)}, bf16[224,128]{1,0:T(8,128)(2,1)S(1)}, u32[]{:S(2)}, u32[]{:S(2)}) collective-permute-start(bf16[224,128]{1,0:T(8,128)(2,1)S(1)} %constant_dynamic-update-slice_fusion.refs_0_), channel_id=1, source_target_pairs={{0,65},{1,64},{64,1},{65,0},{128,193},{129,192},{192,129},{193,128... | collective-permute-start | bytes 172040 | tf_op jit(solution)/shard_map/ppermute | solution.py:272
  32.1 4.6 %collective-permute-start.10 = (bf16[64,256]{1,0:T(8,128)(2,1)S(1)}, bf16[64,256]{1,0:T(8,128)(2,1)S(1)}, u32[]{:S(2)}, u32[]{:S(2)}) collective-permute-start(bf16[64,256]{1,0:T(8,128)(2,1)S(1)} %attend.3), channel_id=1, source_target_pairs={{0,7},{1,6},{2,5},{3,4},{4,3},{5,2},{6,1},{7,0},{8,15},{9,14},{10,... | collective-permute-start | bytes 98312 | tf_op jit(solution)/shard_map/ppermute | solution.py:272
  35.0 4.3 %collective-permute-start.9 = (bf16[64,256]{1,0:T(8,128)(2,1)S(1)}, bf16[64,256]{1,0:T(8,128)(2,1)S(1)}, u32[]{:S(2)}, u32[]{:S(2)}) collective-permute-start(bf16[64,256]{1,0:T(8,128)(2,1)S(1)} %attend.3), channel_id=1, source_target_pairs={{0,4},{1,5},{2,6},{3,7},{4,0},{5,1},{6,2},{7,3},{8,12},{9,13},{10,... | collective-permute-start | bytes 98312 | tf_op jit(solution)/shard_map/ppermute | solution.py:272
  35.4 3.9 %collective-permute-start.8 = (bf16[64,256]{1,0:T(8,128)(2,1)S(1)}, bf16[64,256]{1,0:T(8,128)(2,1)S(1)}, u32[]{:S(2)}, u32[]{:S(2)}) collective-permute-start(bf16[64,256]{1,0:T(8,128)(2,1)S(1)} %attend.3), channel_id=1, source_target_pairs={{0,3},{1,2},{2,1},{3,0},{4,7},{5,6},{6,5},{7,4},{8,11},{9,10},{10,... | collective-permute-start | bytes 98312 | tf_op jit(solution)/shard_map/ppermute | solution.py:272
  39.3 6.1 %collective-permute-start.13 = (bf16[64,256]{1,0:T(8,128)(2,1)S(1)}, bf16[64,256]{1,0:T(8,128)(2,1)S(1)}, u32[]{:S(2)}, u32[]{:S(2)}) collective-permute-start(bf16[64,256]{1,0:T(8,128)(2,1)S(1)} %add_convert_fusion.2), channel_id=1, source_target_pairs={{0,49},{1,48},{16,33},{17,32},{32,17},{33,16},{48,1},{49,0},{2,51}... | collective-permute-start | bytes 98312 | tf_op jit(solution)/shard_map/ppermute | solution.py:272
  43.4 4.3 %collective-permute-start.12 = (bf16[64,256]{1,0:T(8,128)(2,1)S(1)}, bf16[64,256]{1,0:T(8,128)(2,1)S(1)}, u32[]{:S(2)}, u32[]{:S(2)}) collective-permute-start(bf16[64,256]{1,0:T(8,128)(2,1)S(1)} %add_convert_fusion.2), channel_id=1, source_target_pairs={{0,32},{1,33},{16,48},{17,49},{32,0},{33,1},{48,16},{49,17},{2,34}... | collective-permute-start | bytes 98312 | tf_op jit(solution)/shard_map/ppermute | solution.py:272
  43.9 3.7 %collective-permute-start.11 = (bf16[64,256]{1,0:T(8,128)(2,1)S(1)}, bf16[64,256]{1,0:T(8,128)(2,1)S(1)}, u32[]{:S(2)}, u32[]{:S(2)}) collective-permute-start(bf16[64,256]{1,0:T(8,128)(2,1)S(1)} %add_convert_fusion.2), channel_id=1, source_target_pairs={{0,17},{1,16},{16,1},{17,0},{32,49},{33,48},{48,33},{49,32},{2,19}... | collective-permute-start | bytes 98312 | tf_op jit(solution)/shard_map/ppermute | solution.py:272
  47.7 5.4 %collective-permute-start.17 = (bf16[64,256]{1,0:T(8,128)(2,1)S(1)}, bf16[64,256]{1,0:T(8,128)(2,1)S(1)}, u32[]{:S(2)}, u32[]{:S(2)}) collective-permute-start(bf16[64,256]{1,0:T(8,128)(2,1)S(1)} %get-tuple-element.12.refs_4_.refs_5_), channel_id=1, source_target_pairs={{0,193},{1,192},{64,129},{65,128},{128,65},{129,64},{192,1},{193,0... | collective-permute-start | bytes 98312 | tf_op jit(solution)/shard_map/ppermute | solution.py:272
  49.8 4.4 %collective-permute-start.16 = (bf16[64,256]{1,0:T(8,128)(2,1)S(1)}, bf16[64,256]{1,0:T(8,128)(2,1)S(1)}, u32[]{:S(2)}, u32[]{:S(2)}) collective-permute-start(bf16[64,256]{1,0:T(8,128)(2,1)S(1)} %get-tuple-element.12.refs_4_.refs_5_), channel_id=1, source_target_pairs={{0,129},{1,128},{64,193},{65,192},{128,1},{129,0},{192,65},{193,64... | collective-permute-start | bytes 98312 | tf_op jit(solution)/shard_map/ppermute | solution.py:272
  49.8 4.5 %collective-permute-start.15 = (bf16[64,256]{1,0:T(8,128)(2,1)S(1)}, bf16[64,256]{1,0:T(8,128)(2,1)S(1)}, u32[]{:S(2)}, u32[]{:S(2)}) collective-permute-start(bf16[64,256]{1,0:T(8,128)(2,1)S(1)} %get-tuple-element.12.refs_4_.refs_5_), channel_id=1, source_target_pairs={{0,65},{1,64},{64,1},{65,0},{128,193},{129,192},{192,129},{193,128... | collective-permute-start | bytes 98312 | tf_op jit(solution)/shard_map/ppermute | solution.py:272
  54.3 4.1 %collective-permute-start.18 = (bf16[4,64,256]{2,1,0:T(8,128)(2,1)S(1)}, bf16[4,64,256]{2,1,0:T(8,128)(2,1)S(1)}, u32[]{:S(2)}, u32[]{:S(2)}) collective-permute-start(bf16[4,64,256]{2,1,0:T(8,128)(2,1)S(1)} %pad_maximum_fusion.1), channel_id=1, source_target_pairs={{0,1},{1,0},{2,3},{3,2},{4,5},{5,4},{6,7},{7,6},{8,9},{9,8},{10,11... | collective-permute-start | bytes 393224 | tf_op jit(solution)/shard_map/ppermute | solution.py:284
  63.7 4.6 %collective-permute-start.21 = (bf16[64,256]{1,0:T(8,128)(2,1)S(1)}, bf16[64,256]{1,0:T(8,128)(2,1)S(1)}, u32[]{:S(2)}, u32[]{:S(2)}) collective-permute-start(bf16[64,256]{1,0:T(8,128)(2,1)S(1)} %attend.5), channel_id=1, source_target_pairs={{0,7},{1,6},{2,5},{3,4},{4,3},{5,2},{6,1},{7,0},{8,15},{9,14},{10,... | collective-permute-start | bytes 98312 | tf_op jit(solution)/shard_map/ppermute | solution.py:272
  65.3 4.3 %collective-permute-start.20 = (bf16[64,256]{1,0:T(8,128)(2,1)S(1)}, bf16[64,256]{1,0:T(8,128)(2,1)S(1)}, u32[]{:S(2)}, u32[]{:S(2)}) collective-permute-start(bf16[64,256]{1,0:T(8,128)(2,1)S(1)} %attend.5), channel_id=1, source_target_pairs={{0,4},{1,5},{2,6},{3,7},{4,0},{5,1},{6,2},{7,3},{8,12},{9,13},{10,... | collective-permute-start | bytes 98312 | tf_op jit(solution)/shard_map/ppermute | solution.py:272
  66.3 3.9 %collective-permute-start.19 = (bf16[64,256]{1,0:T(8,128)(2,1)S(1)}, bf16[64,256]{1,0:T(8,128)(2,1)S(1)}, u32[]{:S(2)}, u32[]{:S(2)}) collective-permute-start(bf16[64,256]{1,0:T(8,128)(2,1)S(1)} %attend.5), channel_id=1, source_target_pairs={{0,3},{1,2},{2,1},{3,0},{4,7},{5,6},{6,5},{7,4},{8,11},{9,10},{10,... | collective-permute-start | bytes 98312 | tf_op jit(solution)/shard_map/ppermute | solution.py:272
  70.2 4.9 %collective-permute-start.24 = (bf16[64,256]{1,0:T(8,128)(2,1)S(1)}, bf16[64,256]{1,0:T(8,128)(2,1)S(1)}, u32[]{:S(2)}, u32[]{:S(2)}) collective-permute-start(bf16[64,256]{1,0:T(8,128)(2,1)S(1)} %add_convert_fusion), channel_id=1, source_target_pairs={{0,49},{1,48},{16,33},{17,32},{32,17},{33,16},{48,1},{49,0},{2,51}... | collective-permute-start | bytes 98312 | tf_op jit(solution)/shard_map/ppermute | solution.py:272
  72.1 4.7 %collective-permute-start.23 = (bf16[64,256]{1,0:T(8,128)(2,1)S(1)}, bf16[64,256]{1,0:T(8,128)(2,1)S(1)}, u32[]{:S(2)}, u32[]{:S(2)}) collective-permute-start(bf16[64,256]{1,0:T(8,128)(2,1)S(1)} %add_convert_fusion), channel_id=1, source_target_pairs={{0,32},{1,33},{16,48},{17,49},{32,0},{33,1},{48,16},{49,17},{2,34}... | collective-permute-start | bytes 98312 | tf_op jit(solution)/shard_map/ppermute | solution.py:272
  73.1 3.7 %collective-permute-start.22 = (bf16[64,256]{1,0:T(8,128)(2,1)S(1)}, bf16[64,256]{1,0:T(8,128)(2,1)S(1)}, u32[]{:S(2)}, u32[]{:S(2)}) collective-permute-start(bf16[64,256]{1,0:T(8,128)(2,1)S(1)} %add_convert_fusion), channel_id=1, source_target_pairs={{0,17},{1,16},{16,1},{17,0},{32,49},{33,48},{48,33},{49,32},{2,19}... | collective-permute-start | bytes 98312 | tf_op jit(solution)/shard_map/ppermute | solution.py:272
  74.1 3.4 %collective-permute-start.14 = (bf16[64,256]{1,0:T(8,128)(2,1)S(1)}, bf16[64,256]{1,0:T(8,128)(2,1)S(1)}, u32[]{:S(2)}, u32[]{:S(2)}) collective-permute-start(bf16[64,256]{1,0:T(8,128)(2,1)S(1)} %get-tuple-element.13), channel_id=1, source_target_pairs={{0,1},{1,0},{2,3},{3,2},{4,5},{5,4},{6,7},{7,6},{8,9},{9,8},{10,11... | collective-permute-start | bytes 98312 | tf_op jit(solution)/shard_map/ppermute | solution.py:284
  (5 other events, 21.8 us)

commit v4 on v3

--- a/solution.py
+++ b/solution.py
@@ -217,7 +217,6 @@
             logits.append(dot(queries, keys_ref[slot], (0, 0)))
 
     total = None
-    unit = lax.broadcasted_iota(jnp.int32, (part, lanes), 1) == 0
     pick = lax.broadcasted_iota(jnp.int32, (part, lanes), 0) == chans
     pick = jnp.where(pick, 1.0, 0.0).astype(bf16)
     for place, scores in enumerate(logits):
@@ -233,15 +232,15 @@
             factor = jnp.concatenate([factor, factor[:, : 2 * part - lanes]], 1)
             mixed += refs[5 + count][place] * factor
         if last:
-            main = jnp.concatenate([jnp.where(unit, pick, mains[slot][head])] * 2, 0)
-            term = dot(main, mixed.astype(bf16), (0, 1))
-            term = term[chans:] * (terms[slot][1] / term[:1])
+            main = jnp.concatenate([jnp.concatenate([mains[slot][head], pick], 1)] * 2, 0)
+            term = dot(mixed.astype(bf16), main)
+            term = term[:, :lanes] * (terms[slot][1] / term[:, lanes:])
             total = term if total is None else total + term
         else:
             refs[-3][place] = mixed
             refs[-2][place] = peak
     if last:
-        refs[-2][...] = total.astype(bf16)
+        refs[-2][...] = total.T[chans:].astype(bf16)
 
 
 def attend(terms, packs, own, tokens, state=(), last=True):

time: 79.2 us -> 79 us (level)
  no operation moved by 1% of the time
where the time goes in v4:
time: 79 us; the launch traced here: 78.8 us
  starting transfers between devices  37.5 us (47%)
  waiting for transfers between devices  19.7 us (25%)
  Pallas kernels  17.3 us (22%)
  between operations  2.13 us (3%)
  other arithmetic  1.42 us (2%)
    ppermute x21, starting transfers between devices, swap(): lax.ppermute(value, axes, [(i, i ^ flip) for i in range(lax.axis_size(axe...  32.4 us
    ppermute x21, waiting for transfers between devices, swap(): lax.ppermute(value, axes, [(i, i ^ flip) for i in range(lax.axis_size(axe...  18.1 us
    pallas_call x3, Pallas kernels, attend(): pl.pallas_call(functools.partial(attend_kernel, terms, count, bool(state)...  11.5 us
    pallas_call x1, Pallas kernels, fold_maps(): pl.pallas_call(maps_kernel, in_specs=[pl.BlockSpec(memory_space=pltpu.SME...  5.81 us
    ppermute x5, starting transfers between devices, other_core(): return lax.ppermute(value, 'tp', [(0, 1), (1, 0)])  5.09 us
    ppermute x5, waiting for transfers between devices, other_core(): return lax.ppermute(value, 'tp', [(0, 1), (1, 0)])  1.6 us
  transfers between devices with their start and end apart: 26, of which 17 were waited for; matrix products, arithmetic and copies ran while one was open for 1% of the time, Pallas kernels for 12%

profile of v4, /device:TPU:1, one launch (start us, length us, event | category | flops | bytes accessed | tf_op | source)
XLA Modules:
  0.0 78.8 jit_solution(11293498371012475391)
XLA Ops:
  0.6 3.3 %collective-permute-start.1 = (bf16[64,256]{1,0:T(8,128)(2,1)}, bf16[64,256]{1,0:T(8,128)(2,1)S(1)}, u32[]{:S(2)}, u32[]{:S(2)}) collective-permute-start(bf16[64,256]{1,0:T(8,128)(2,1)} %bitcast.56), channel_id=1, source_target_pairs={{0,1},{1,0},{2,3},{3,2},{4,5},{5,4},{6,7},{7,6},{8,9},{9,8},{10,11... | collective-permute-start | bytes 98312 | tf_op jit(solution)/shard_map/ppermute | solution.py:283
  6.0 5.8 %fold_maps.1 = bf16[144,128]{1,0:T(8,128)(2,1)S(1)} custom-call(s32[1]{0:T(128)S(6)} %copy.11.gen_ref, s32[1]{0:T(128)S(6)} %copy.12.score_ref, bf16[64,5120]{1,0:T(8,128)(2,1)} %bitcast.59, bf16[64,128]{1,0:T(8,128)(2,1)S(1)} %bitcast.55, bf16[256,10240]{1,0:T(8,128)(2,1)} %bitcast.57, bf16[384,5120]{1,0:T(8,128)(2,1)} %bitcast.58), custom_call_target="tpu_custom_call" | custom-call | flops 6000000000 | bytes 10000000 | tf_op jit(solution)/shard_map/fold_maps/pallas_call | solution.py:157
  11.9 6.3 %collective-permute-start.4 = (bf16[80,128]{1,0:T(8,128)(2,1)S(1)}, bf16[80,128]{1,0:T(8,128)(2,1)S(1)}, u32[]{:S(2)}, u32[]{:S(2)}) collective-permute-start(bf16[80,128]{1,0:T(8,128)(2,1)S(1)} %slice.14), channel_id=1, source_target_pairs={{0,9},{1,8},{8,1},{9,0},{2,11},{3,10},{10,3},{11,2},{4,13},{5,12},... | collective-permute-start | bytes 61448 | tf_op jit(solution)/shard_map/ppermute | solution.py:271
  18.2 1.2 %collective-permute-start.2 = (bf16[2,64,256]{2,1,0:T(8,128)(2,1)S(1)}, bf16[2,64,256]{2,1,0:T(8,128)(2,1)S(1)}, u32[]{:S(2)}, u32[]{:S(2)}) collective-permute-start(bf16[2,64,256]{2,1,0:T(8,128)(2,1)S(1)} %pad_maximum_fusion.2), channel_id=1, source_target_pairs={{0,129},{1,128},{64,193},{65,192},{128,1},{129,0},{192,65},{193,64... | collective-permute-start | bytes 196616 | tf_op jit(solution)/shard_map/ppermute | solution.py:271
  19.8 2.1 %collective-permute-start.7 = (bf16[224,128]{1,0:T(8,128)(2,1)S(1)}, bf16[224,128]{1,0:T(8,128)(2,1)S(1)}, u32[]{:S(2)}, u32[]{:S(2)}) collective-permute-start(bf16[224,128]{1,0:T(8,128)(2,1)S(1)} %constant_dynamic-update-slice_fusion.refs_0_), channel_id=1, source_target_pairs={{0,193},{1,192},{64,129},{65,128},{128,65},{129,64},{192,1},{193,0... | collective-permute-start | bytes 172040 | tf_op jit(solution)/shard_map/ppermute | solution.py:271
  22.7 1.0 %collective-permute-start.5 = (bf16[224,128]{1,0:T(8,128)(2,1)S(1)}, bf16[224,128]{1,0:T(8,128)(2,1)S(1)}, u32[]{:S(2)}, u32[]{:S(2)}) collective-permute-start(bf16[224,128]{1,0:T(8,128)(2,1)S(1)} %constant_dynamic-update-slice_fusion.refs_0_), channel_id=1, source_target_pairs={{0,65},{1,64},{64,1},{65,0},{128,193},{129,192},{192,129},{193,128... | collective-permute-start | bytes 172040 | tf_op jit(solution)/shard_map/ppermute | solution.py:271
  23.7 3.3 %collective-permute-done.2 = bf16[2,64,256]{2,1,0:T(8,128)(2,1)S(1)} collective-permute-done((bf16[2,64,256]{2,1,0:T(8,128)(2,1)S(1)}, bf16[2,64,256]{2,1,0:T(8,128)(2,1)S(1)}, u32[]{:S(2)}, u32[]{:S(2)}) %collective-permute-start.2) | collective-permute-done | bytes 65568 | tf_op jit(solution)/shard_map/ppermute | solution.py:271
  27.1 1.3 %collective-permute-done.3 = bf16[4,64,256]{2,1,0:T(8,128)(2,1)S(1)} collective-permute-done((bf16[4,64,256]{2,1,0:T(8,128)(2,1)S(1)}, bf16[4,64,256]{2,1,0:T(8,128)(2,1)S(1)}, u32[]{:S(2)}, u32[]{:S(2)}) %collective-permute-start.3) | collective-permute-done | bytes 131104 | tf_op jit(solution)/shard_map/ppermute | solution.py:283
  29.3 2.8 %attend.3 = bf16[64,256]{1,0:T(8,128)(2,1)S(1)} custom-call(bf16[224,128]{1,0:T(8,128)(2,1)S(1)} %constant_dynamic-update-slice_fusion.refs_0_, bf16[224,128]{1,0:T(8,128)(2,1)S(1)} %collective-permute-done.5.refs_1_, bf16[224,128]{1,0:T(8,128)(2,1)S(1)} %collective-permute-done.6.refs_2_, bf16[224,128]{1,0:T(8,128)(2,1)S(1)} %collective-permute-done.7.refs_3_, ...), custom_call_target="tpu_custom_call" | custom-call | flops 2147483648 | bytes 1000000 | tf_op jit(solution)/shard_map/attend/pallas_call | solution.py:256
  32.1 2.9 %collective-permute-start.10 = (bf16[64,256]{1,0:T(8,128)(2,1)S(1)}, bf16[64,256]{1,0:T(8,128)(2,1)S(1)}, u32[]{:S(2)}, u32[]{:S(2)}) collective-permute-start(bf16[64,256]{1,0:T(8,128)(2,1)S(1)} %attend.3), channel_id=1, source_target_pairs={{0,7},{1,6},{2,5},{3,4},{4,3},{5,2},{6,1},{7,0},{8,15},{9,14},{10,... | collective-permute-start | bytes 98312 | tf_op jit(solution)/shard_map/ppermute | solution.py:271
  36.8 2.5 %collective-permute-done.9 = bf16[64,256]{1,0:T(8,128)(2,1)S(1)} collective-permute-done((bf16[64,256]{1,0:T(8,128)(2,1)S(1)}, bf16[64,256]{1,0:T(8,128)(2,1)S(1)}, u32[]{:S(2)}, u32[]{:S(2)}) %collective-permute-start.9) | collective-permute-done | bytes 32800 | tf_op jit(solution)/shard_map/ppermute | solution.py:271
  39.3 4.1 %collective-permute-start.13 = (bf16[64,256]{1,0:T(8,128)(2,1)S(1)}, bf16[64,256]{1,0:T(8,128)(2,1)S(1)}, u32[]{:S(2)}, u32[]{:S(2)}) collective-permute-start(bf16[64,256]{1,0:T(8,128)(2,1)S(1)} %add_convert_fusion.2), channel_id=1, source_target_pairs={{0,49},{1,48},{16,33},{17,32},{32,17},{33,16},{48,1},{49,0},{2,51}... | collective-permute-start | bytes 98312 | tf_op jit(solution)/shard_map/ppermute | solution.py:271
  45.4 2.3 %collective-permute-done.12 = bf16[64,256]{1,0:T(8,128)(2,1)S(1)} collective-permute-done((bf16[64,256]{1,0:T(8,128)(2,1)S(1)}, bf16[64,256]{1,0:T(8,128)(2,1)S(1)}, u32[]{:S(2)}, u32[]{:S(2)}) %collective-permute-start.12) | collective-permute-done | bytes 32800 | tf_op jit(solution)/shard_map/ppermute | solution.py:271
  47.7 2.0 %collective-permute-start.17 = (bf16[64,256]{1,0:T(8,128)(2,1)S(1)}, bf16[64,256]{1,0:T(8,128)(2,1)S(1)}, u32[]{:S(2)}, u32[]{:S(2)}) collective-permute-start(bf16[64,256]{1,0:T(8,128)(2,1)S(1)} %get-tuple-element.12.refs_4_.refs_5_), channel_id=1, source_target_pairs={{0,193},{1,192},{64,129},{65,128},{128,65},{129,64},{192,1},{193,0... | collective-permute-start | bytes 98312 | tf_op jit(solution)/shard_map/ppermute | solution.py:271
  49.8 1.9 %collective-permute-start.15 = (bf16[64,256]{1,0:T(8,128)(2,1)S(1)}, bf16[64,256]{1,0:T(8,128)(2,1)S(1)}, u32[]{:S(2)}, u32[]{:S(2)}) collective-permute-start(bf16[64,256]{1,0:T(8,128)(2,1)S(1)} %get-tuple-element.12.refs_4_.refs_5_), channel_id=1, source_target_pairs={{0,65},{1,64},{64,1},{65,0},{128,193},{129,192},{192,129},{193,128... | collective-permute-start | bytes 98312 | tf_op jit(solution)/shard_map/ppermute | solution.py:271
  51.7 1.4 %collective-permute-done.17.refs_8_ = bf16[64,256]{1,0:T(8,128)(2,1)S(1)} collective-permute-done((bf16[64,256]{1,0:T(8,128)(2,1)S(1)}, bf16[64,256]{1,0:T(8,128)(2,1)S(1)}, u32[]{:S(2)}, u32[]{:S(2)}) %collective-permute-start.17) | collective-permute-done | bytes 32800 | tf_op jit(solution)/shard_map/ppermute | solution.py:271
  53.1 1.1 %collective-permute-done.16.refs_7_ = bf16[64,256]{1,0:T(8,128)(2,1)S(1)} collective-permute-done((bf16[64,256]{1,0:T(8,128)(2,1)S(1)}, bf16[64,256]{1,0:T(8,128)(2,1)S(1)}, u32[]{:S(2)}, u32[]{:S(2)}) %collective-permute-start.16) | collective-permute-done | bytes 32800 | tf_op jit(solution)/shard_map/ppermute | solution.py:271
  54.8 3.7 %attend.4 = (f32[6,256,160]{2,1,0:T(8,128)S(1)}, f32[6,256,128]{2,1,0:T(8,128)S(1)}) custom-call(bf16[224,128]{1,0:T(8,128)(2,1)S(1)} %constant_dynamic-update-slice_fusion.refs_0_, bf16[224,128]{1,0:T(8,128)(2,1)S(1)} %collective-permute-done.5.refs_1_, bf16[224,128]{1,0:T(8,128)(2,1)S(1)} %collective-permute-done.6.refs_2_, ...), custom_call_target="tpu_custom_call" | custom-call | flops 3221225472 | bytes 1000000 | tf_op jit(solution)/shard_map/attend/pallas_call | solution.py:256
  58.5 5.0 %attend.5 = bf16[64,256]{1,0:T(8,128)(2,1)S(1)} custom-call(bf16[224,128]{1,0:T(8,128)(2,1)S(1)} %constant_dynamic-update-slice_fusion.refs_0_, bf16[224,128]{1,0:T(8,128)(2,1)S(1)} %collective-permute-done.5.refs_1_, bf16[224,128]{1,0:T(8,128)(2,1)S(1)} %collective-permute-done.6.refs_2_, bf16[224,128]{1,0:T(8,128)(2,1)S(1)} %collective-permute-done.7.refs_3_, ...), custom_call_target="tpu_custom_call" | custom-call | flops 3221225472 | bytes 1000000 | tf_op jit(solution)/shard_map/attend/pallas_call | solution.py:256
  63.6 1.6 %collective-permute-start.21 = (bf16[64,256]{1,0:T(8,128)(2,1)S(1)}, bf16[64,256]{1,0:T(8,128)(2,1)S(1)}, u32[]{:S(2)}, u32[]{:S(2)}) collective-permute-start(bf16[64,256]{1,0:T(8,128)(2,1)S(1)} %attend.5), channel_id=1, source_target_pairs={{0,7},{1,6},{2,5},{3,4},{4,3},{5,2},{6,1},{7,0},{8,15},{9,14},{10,... | collective-permute-start | bytes 98312 | tf_op jit(solution)/shard_map/ppermute | solution.py:271
  65.9 1.6 %collective-permute-start.19 = (bf16[64,256]{1,0:T(8,128)(2,1)S(1)}, bf16[64,256]{1,0:T(8,128)(2,1)S(1)}, u32[]{:S(2)}, u32[]{:S(2)}) collective-permute-start(bf16[64,256]{1,0:T(8,128)(2,1)S(1)} %attend.5), channel_id=1, source_target_pairs={{0,3},{1,2},{2,1},{3,0},{4,7},{5,6},{6,5},{7,4},{8,11},{9,10},{10,... | collective-permute-start | bytes 98312 | tf_op jit(solution)/shard_map/ppermute | solution.py:271
  68.2 1.2 %collective-permute-done.20 = bf16[64,256]{1,0:T(8,128)(2,1)S(1)} collective-permute-done((bf16[64,256]{1,0:T(8,128)(2,1)S(1)}, bf16[64,256]{1,0:T(8,128)(2,1)S(1)}, u32[]{:S(2)}, u32[]{:S(2)}) %collective-permute-start.20) | collective-permute-done | bytes 32800 | tf_op jit(solution)/shard_map/ppermute | solution.py:271
  69.8 2.0 %collective-permute-start.24 = (bf16[64,256]{1,0:T(8,128)(2,1)S(1)}, bf16[64,256]{1,0:T(8,128)(2,1)S(1)}, u32[]{:S(2)}, u32[]{:S(2)}) collective-permute-start(bf16[64,256]{1,0:T(8,128)(2,1)S(1)} %add_convert_fusion), channel_id=1, source_target_pairs={{0,49},{1,48},{16,33},{17,32},{32,17},{33,16},{48,1},{49,0},{2,51}... | collective-permute-start | bytes 98312 | tf_op jit(solution)/shard_map/ppermute | solution.py:271
  75.0 1.5 %collective-permute-done.23 = bf16[64,256]{1,0:T(8,128)(2,1)S(1)} collective-permute-done((bf16[64,256]{1,0:T(8,128)(2,1)S(1)}, bf16[64,256]{1,0:T(8,128)(2,1)S(1)}, u32[]{:S(2)}, u32[]{:S(2)}) %collective-permute-start.23) | collective-permute-done | bytes 32800 | tf_op jit(solution)/shard_map/ppermute | solution.py:271
  (55 shorter events, 14.6 us)
Async XLA Ops:
  0.6 11.2 %collective-permute-start.1 = (bf16[64,256]{1,0:T(8,128)(2,1)}, bf16[64,256]{1,0:T(8,128)(2,1)S(1)}, u32[]{:S(2)}, u32[]{:S(2)}) collective-permute-start(bf16[64,256]{1,0:T(8,128)(2,1)} %bitcast.56), channel_id=1, source_target_pairs={{0,1},{1,0},{2,3},{3,2},{4,5},{5,4},{6,7},{7,6},{8,9},{9,8},{10,11... | collective-permute-start | bytes 98312 | tf_op jit(solution)/shard_map/ppermute | solution.py:283
  4.0 7.9 %collective-permute-start = (bf16[64,256]{1,0:T(8,128)(2,1)}, bf16[64,256]{1,0:T(8,128)(2,1)S(1)}, u32[]{:S(2)}, u32[]{:S(2)}) collective-permute-start(bf16[64,256]{1,0:T(8,128)(2,1)} %bitcast.45), channel_id=1, source_target_pairs={{0,65},{1,64},{64,1},{65,0},{128,193},{129,192},{192,129},{193,128... | collective-permute-start | bytes 98312 | tf_op jit(solution)/shard_map/ppermute | solution.py:271
  11.9 7.9 %collective-permute-start.4 = (bf16[80,128]{1,0:T(8,128)(2,1)S(1)}, bf16[80,128]{1,0:T(8,128)(2,1)S(1)}, u32[]{:S(2)}, u32[]{:S(2)}) collective-permute-start(bf16[80,128]{1,0:T(8,128)(2,1)S(1)} %slice.14), channel_id=1, source_target_pairs={{0,9},{1,8},{8,1},{9,0},{2,11},{3,10},{10,3},{11,2},{4,13},{5,12},... | collective-permute-start | bytes 61448 | tf_op jit(solution)/shard_map/ppermute | solution.py:271
  18.2 8.8 %collective-permute-start.2 = (bf16[2,64,256]{2,1,0:T(8,128)(2,1)S(1)}, bf16[2,64,256]{2,1,0:T(8,128)(2,1)S(1)}, u32[]{:S(2)}, u32[]{:S(2)}) collective-permute-start(bf16[2,64,256]{2,1,0:T(8,128)(2,1)S(1)} %pad_maximum_fusion.2), channel_id=1, source_target_pairs={{0,129},{1,128},{64,193},{65,192},{128,1},{129,0},{192,65},{193,64... | collective-permute-start | bytes 196616 | tf_op jit(solution)/shard_map/ppermute | solution.py:271
  19.8 8.7 %collective-permute-start.7 = (bf16[224,128]{1,0:T(8,128)(2,1)S(1)}, bf16[224,128]{1,0:T(8,128)(2,1)S(1)}, u32[]{:S(2)}, u32[]{:S(2)}) collective-permute-start(bf16[224,128]{1,0:T(8,128)(2,1)S(1)} %constant_dynamic-update-slice_fusion.refs_0_), channel_id=1, source_target_pairs={{0,193},{1,192},{64,129},{65,128},{128,65},{129,64},{192,1},{193,0... | collective-permute-start | bytes 172040 | tf_op jit(solution)/shard_map/ppermute | solution.py:271
  21.8 7.5 %collective-permute-start.6 = (bf16[224,128]{1,0:T(8,128)(2,1)S(1)}, bf16[224,128]{1,0:T(8,128)(2,1)S(1)}, u32[]{:S(2)}, u32[]{:S(2)}) collective-permute-start(bf16[224,128]{1,0:T(8,128)(2,1)S(1)} %constant_dynamic-update-slice_fusion.refs_0_), channel_id=1, source_target_pairs={{0,129},{1,128},{64,193},{65,192},{128,1},{129,0},{192,65},{193,64... | collective-permute-start | bytes 172040 | tf_op jit(solution)/shard_map/ppermute | solution.py:271
  22.7 6.6 %collective-permute-start.5 = (bf16[224,128]{1,0:T(8,128)(2,1)S(1)}, bf16[224,128]{1,0:T(8,128)(2,1)S(1)}, u32[]{:S(2)}, u32[]{:S(2)}) collective-permute-start(bf16[224,128]{1,0:T(8,128)(2,1)S(1)} %constant_dynamic-update-slice_fusion.refs_0_), channel_id=1, source_target_pairs={{0,65},{1,64},{64,1},{65,0},{128,193},{129,192},{192,129},{193,128... | collective-permute-start | bytes 172040 | tf_op jit(solution)/shard_map/ppermute | solution.py:271
  32.1 4.6 %collective-permute-start.10 = (bf16[64,256]{1,0:T(8,128)(2,1)S(1)}, bf16[64,256]{1,0:T(8,128)(2,1)S(1)}, u32[]{:S(2)}, u32[]{:S(2)}) collective-permute-start(bf16[64,256]{1,0:T(8,128)(2,1)S(1)} %attend.3), channel_id=1, source_target_pairs={{0,7},{1,6},{2,5},{3,4},{4,3},{5,2},{6,1},{7,0},{8,15},{9,14},{10,... | collective-permute-start | bytes 98312 | tf_op jit(solution)/shard_map/ppermute | solution.py:271
  35.0 4.3 %collective-permute-start.9 = (bf16[64,256]{1,0:T(8,128)(2,1)S(1)}, bf16[64,256]{1,0:T(8,128)(2,1)S(1)}, u32[]{:S(2)}, u32[]{:S(2)}) collective-permute-start(bf16[64,256]{1,0:T(8,128)(2,1)S(1)} %attend.3), channel_id=1, source_target_pairs={{0,4},{1,5},{2,6},{3,7},{4,0},{5,1},{6,2},{7,3},{8,12},{9,13},{10,... | collective-permute-start | bytes 98312 | tf_op jit(solution)/shard_map/ppermute | solution.py:271
  35.4 3.9 %collective-permute-start.8 = (bf16[64,256]{1,0:T(8,128)(2,1)S(1)}, bf16[64,256]{1,0:T(8,128)(2,1)S(1)}, u32[]{:S(2)}, u32[]{:S(2)}) collective-permute-start(bf16[64,256]{1,0:T(8,128)(2,1)S(1)} %attend.3), channel_id=1, source_target_pairs={{0,3},{1,2},{2,1},{3,0},{4,7},{5,6},{6,5},{7,4},{8,11},{9,10},{10,... | collective-permute-start | bytes 98312 | tf_op jit(solution)/shard_map/ppermute | solution.py:271
  39.3 6.1 %collective-permute-start.13 = (bf16[64,256]{1,0:T(8,128)(2,1)S(1)}, bf16[64,256]{1,0:T(8,128)(2,1)S(1)}, u32[]{:S(2)}, u32[]{:S(2)}) collective-permute-start(bf16[64,256]{1,0:T(8,128)(2,1)S(1)} %add_convert_fusion.2), channel_id=1, source_target_pairs={{0,49},{1,48},{16,33},{17,32},{32,17},{33,16},{48,1},{49,0},{2,51}... | collective-permute-start | bytes 98312 | tf_op jit(solution)/shard_map/ppermute | solution.py:271
  43.4 4.3 %collective-permute-start.12 = (bf16[64,256]{1,0:T(8,128)(2,1)S(1)}, bf16[64,256]{1,0:T(8,128)(2,1)S(1)}, u32[]{:S(2)}, u32[]{:S(2)}) collective-permute-start(bf16[64,256]{1,0:T(8,128)(2,1)S(1)} %add_convert_fusion.2), channel_id=1, source_target_pairs={{0,32},{1,33},{16,48},{17,49},{32,0},{33,1},{48,16},{49,17},{2,34}... | collective-permute-start | bytes 98312 | tf_op jit(solution)/shard_map/ppermute | solution.py:271
  43.9 3.7 %collective-permute-start.11 = (bf16[64,256]{1,0:T(8,128)(2,1)S(1)}, bf16[64,256]{1,0:T(8,128)(2,1)S(1)}, u32[]{:S(2)}, u32[]{:S(2)}) collective-permute-start(bf16[64,256]{1,0:T(8,128)(2,1)S(1)} %add_convert_fusion.2), channel_id=1, source_target_pairs={{0,17},{1,16},{16,1},{17,0},{32,49},{33,48},{48,33},{49,32},{2,19}... | collective-permute-start | bytes 98312 | tf_op jit(solution)/shard_map/ppermute | solution.py:271
  47.7 5.4 %collective-permute-start.17 = (bf16[64,256]{1,0:T(8,128)(2,1)S(1)}, bf16[64,256]{1,0:T(8,128)(2,1)S(1)}, u32[]{:S(2)}, u32[]{:S(2)}) collective-permute-start(bf16[64,256]{1,0:T(8,128)(2,1)S(1)} %get-tuple-element.12.refs_4_.refs_5_), channel_id=1, source_target_pairs={{0,193},{1,192},{64,129},{65,128},{128,65},{129,64},{192,1},{193,0... | collective-permute-start | bytes 98312 | tf_op jit(solution)/shard_map/ppermute | solution.py:271
  49.8 4.5 %collective-permute-start.16 = (bf16[64,256]{1,0:T(8,128)(2,1)S(1)}, bf16[64,256]{1,0:T(8,128)(2,1)S(1)}, u32[]{:S(2)}, u32[]{:S(2)}) collective-permute-start(bf16[64,256]{1,0:T(8,128)(2,1)S(1)} %get-tuple-element.12.refs_4_.refs_5_), channel_id=1, source_target_pairs={{0,129},{1,128},{64,193},{65,192},{128,1},{129,0},{192,65},{193,64... | collective-permute-start | bytes 98312 | tf_op jit(solution)/shard_map/ppermute | solution.py:271
  49.8 4.6 %collective-permute-start.15 = (bf16[64,256]{1,0:T(8,128)(2,1)S(1)}, bf16[64,256]{1,0:T(8,128)(2,1)S(1)}, u32[]{:S(2)}, u32[]{:S(2)}) collective-permute-start(bf16[64,256]{1,0:T(8,128)(2,1)S(1)} %get-tuple-element.12.refs_4_.refs_5_), channel_id=1, source_target_pairs={{0,65},{1,64},{64,1},{65,0},{128,193},{129,192},{192,129},{193,128... | collective-permute-start | bytes 98312 | tf_op jit(solution)/shard_map/ppermute | solution.py:271
  54.4 4.1 %collective-permute-start.18 = (bf16[4,64,256]{2,1,0:T(8,128)(2,1)S(1)}, bf16[4,64,256]{2,1,0:T(8,128)(2,1)S(1)}, u32[]{:S(2)}, u32[]{:S(2)}) collective-permute-start(bf16[4,64,256]{2,1,0:T(8,128)(2,1)S(1)} %pad_maximum_fusion.1), channel_id=1, source_target_pairs={{0,1},{1,0},{2,3},{3,2},{4,5},{5,4},{6,7},{7,6},{8,9},{9,8},{10,11... | collective-permute-start | bytes 393224 | tf_op jit(solution)/shard_map/ppermute | solution.py:283
  63.6 4.6 %collective-permute-start.21 = (bf16[64,256]{1,0:T(8,128)(2,1)S(1)}, bf16[64,256]{1,0:T(8,128)(2,1)S(1)}, u32[]{:S(2)}, u32[]{:S(2)}) collective-permute-start(bf16[64,256]{1,0:T(8,128)(2,1)S(1)} %attend.5), channel_id=1, source_target_pairs={{0,7},{1,6},{2,5},{3,4},{4,3},{5,2},{6,1},{7,0},{8,15},{9,14},{10,... | collective-permute-start | bytes 98312 | tf_op jit(solution)/shard_map/ppermute | solution.py:271
  65.1 4.3 %collective-permute-start.20 = (bf16[64,256]{1,0:T(8,128)(2,1)S(1)}, bf16[64,256]{1,0:T(8,128)(2,1)S(1)}, u32[]{:S(2)}, u32[]{:S(2)}) collective-permute-start(bf16[64,256]{1,0:T(8,128)(2,1)S(1)} %attend.5), channel_id=1, source_target_pairs={{0,4},{1,5},{2,6},{3,7},{4,0},{5,1},{6,2},{7,3},{8,12},{9,13},{10,... | collective-permute-start | bytes 98312 | tf_op jit(solution)/shard_map/ppermute | solution.py:271
  65.9 4.0 %collective-permute-start.19 = (bf16[64,256]{1,0:T(8,128)(2,1)S(1)}, bf16[64,256]{1,0:T(8,128)(2,1)S(1)}, u32[]{:S(2)}, u32[]{:S(2)}) collective-permute-start(bf16[64,256]{1,0:T(8,128)(2,1)S(1)} %attend.5), channel_id=1, source_target_pairs={{0,3},{1,2},{2,1},{3,0},{4,7},{5,6},{6,5},{7,4},{8,11},{9,10},{10,... | collective-permute-start | bytes 98312 | tf_op jit(solution)/shard_map/ppermute | solution.py:271
  69.8 5.2 %collective-permute-start.24 = (bf16[64,256]{1,0:T(8,128)(2,1)S(1)}, bf16[64,256]{1,0:T(8,128)(2,1)S(1)}, u32[]{:S(2)}, u32[]{:S(2)}) collective-permute-start(bf16[64,256]{1,0:T(8,128)(2,1)S(1)} %add_convert_fusion), channel_id=1, source_target_pairs={{0,49},{1,48},{16,33},{17,32},{32,17},{33,16},{48,1},{49,0},{2,51}... | collective-permute-start | bytes 98312 | tf_op jit(solution)/shard_map/ppermute | solution.py:271
  71.9 4.6 %collective-permute-start.23 = (bf16[64,256]{1,0:T(8,128)(2,1)S(1)}, bf16[64,256]{1,0:T(8,128)(2,1)S(1)}, u32[]{:S(2)}, u32[]{:S(2)}) collective-permute-start(bf16[64,256]{1,0:T(8,128)(2,1)S(1)} %add_convert_fusion), channel_id=1, source_target_pairs={{0,32},{1,33},{16,48},{17,49},{32,0},{33,1},{48,16},{49,17},{2,34}... | collective-permute-start | bytes 98312 | tf_op jit(solution)/shard_map/ppermute | solution.py:271
  72.9 3.6 %collective-permute-start.22 = (bf16[64,256]{1,0:T(8,128)(2,1)S(1)}, bf16[64,256]{1,0:T(8,128)(2,1)S(1)}, u32[]{:S(2)}, u32[]{:S(2)}) collective-permute-start(bf16[64,256]{1,0:T(8,128)(2,1)S(1)} %add_convert_fusion), channel_id=1, source_target_pairs={{0,17},{1,16},{16,1},{17,0},{32,49},{33,48},{48,33},{49,32},{2,19}... | collective-permute-start | bytes 98312 | tf_op jit(solution)/shard_map/ppermute | solution.py:271
  73.7 3.6 %collective-permute-start.14 = (bf16[64,256]{1,0:T(8,128)(2,1)S(1)}, bf16[64,256]{1,0:T(8,128)(2,1)S(1)}, u32[]{:S(2)}, u32[]{:S(2)}) collective-permute-start(bf16[64,256]{1,0:T(8,128)(2,1)S(1)} %get-tuple-element.13), channel_id=1, source_target_pairs={{0,1},{1,0},{2,3},{3,2},{4,5},{5,4},{6,7},{7,6},{8,9},{9,8},{10,11... | collective-permute-start | bytes 98312 | tf_op jit(solution)/shard_map/ppermute | solution.py:283
  (5 other events, 21.8 us)

commit v5 on v4

--- a/solution.py
+++ b/solution.py
@@ -255,6 +255,8 @@
         shape = jax.ShapeDtypeStruct(own.shape, bf16)
     return pl.pallas_call(
         functools.partial(attend_kernel, terms, count, bool(state), last),
+        in_specs=[pl.BlockSpec(memory_space=pltpu.VMEM)] * (5 + count + len(state)),
+        out_specs=jax.tree.map(lambda _: pl.BlockSpec(memory_space=pltpu.VMEM), shape),
         out_shape=shape,
         scratch_shapes=[pltpu.VMEM((len(terms), 2 * part, count * rows), bf16)],
         compiler_params=pltpu.CompilerParams(vmem_limit_bytes=48 * 1024 * 1024),

time: 79 us -> 79 us (level)
  no operation moved by 1% of the time
where the time goes in v5:
time: 79 us; the launch traced here: 78.8 us
  starting transfers between devices  37.5 us (47%)
  waiting for transfers between devices  19.7 us (25%)
  Pallas kernels  17.3 us (22%)
  between operations  2.13 us (3%)
  other arithmetic  1.42 us (2%)
    ppermute x21, starting transfers between devices, swap(): lax.ppermute(value, axes, [(i, i ^ flip) for i in range(lax.axis_size(axe...  32.4 us
    ppermute x21, waiting for transfers between devices, swap(): lax.ppermute(value, axes, [(i, i ^ flip) for i in range(lax.axis_size(axe...  18.1 us
    pallas_call x3, Pallas kernels, attend(): pl.pallas_call(functools.partial(attend_kernel, terms, count, bool(state)...  11.5 us
    pallas_call x1, Pallas kernels, fold_maps(): pl.pallas_call(maps_kernel, in_specs=[pl.BlockSpec(memory_space=pltpu.SME...  5.81 us
    ppermute x5, starting transfers between devices, other_core(): return lax.ppermute(value, 'tp', [(0, 1), (1, 0)])  5.09 us
    ppermute x5, waiting for transfers between devices, other_core(): return lax.ppermute(value, 'tp', [(0, 1), (1, 0)])  1.6 us
  transfers between devices with their start and end apart: 26, of which 17 were waited for; matrix products, arithmetic and copies ran while one was open for 1% of the time, Pallas kernels for 12%

profile of v5, /device:TPU:1, one launch (start us, length us, event | category | flops | bytes accessed | tf_op | source)
XLA Modules:
  0.0 78.8 jit_solution(11293498371012475391)
XLA Ops:
  0.6 3.3 %collective-permute-start.1 = (bf16[64,256]{1,0:T(8,128)(2,1)}, bf16[64,256]{1,0:T(8,128)(2,1)S(1)}, u32[]{:S(2)}, u32[]{:S(2)}) collective-permute-start(bf16[64,256]{1,0:T(8,128)(2,1)} %bitcast.56), channel_id=1, source_target_pairs={{0,1},{1,0},{2,3},{3,2},{4,5},{5,4},{6,7},{7,6},{8,9},{9,8},{10,11... | collective-permute-start | bytes 98312 | tf_op jit(solution)/shard_map/ppermute | solution.py:285
  6.0 5.8 %fold_maps.1 = bf16[144,128]{1,0:T(8,128)(2,1)S(1)} custom-call(s32[1]{0:T(128)S(6)} %copy.11.gen_ref, s32[1]{0:T(128)S(6)} %copy.12.score_ref, bf16[64,5120]{1,0:T(8,128)(2,1)} %bitcast.59, bf16[64,128]{1,0:T(8,128)(2,1)S(1)} %bitcast.55, bf16[256,10240]{1,0:T(8,128)(2,1)} %bitcast.57, bf16[384,5120]{1,0:T(8,128)(2,1)} %bitcast.58), custom_call_target="tpu_custom_call" | custom-call | flops 6000000000 | bytes 10000000 | tf_op jit(solution)/shard_map/fold_maps/pallas_call | solution.py:157
  11.9 6.3 %collective-permute-start.4 = (bf16[80,128]{1,0:T(8,128)(2,1)S(1)}, bf16[80,128]{1,0:T(8,128)(2,1)S(1)}, u32[]{:S(2)}, u32[]{:S(2)}) collective-permute-start(bf16[80,128]{1,0:T(8,128)(2,1)S(1)} %slice.14), channel_id=1, source_target_pairs={{0,9},{1,8},{8,1},{9,0},{2,11},{3,10},{10,3},{11,2},{4,13},{5,12},... | collective-permute-start | bytes 61448 | tf_op jit(solution)/shard_map/ppermute | solution.py:273
  18.2 1.2 %collective-permute-start.2 = (bf16[2,64,256]{2,1,0:T(8,128)(2,1)S(1)}, bf16[2,64,256]{2,1,0:T(8,128)(2,1)S(1)}, u32[]{:S(2)}, u32[]{:S(2)}) collective-permute-start(bf16[2,64,256]{2,1,0:T(8,128)(2,1)S(1)} %pad_maximum_fusion.2), channel_id=1, source_target_pairs={{0,129},{1,128},{64,193},{65,192},{128,1},{129,0},{192,65},{193,64... | collective-permute-start | bytes 196616 | tf_op jit(solution)/shard_map/ppermute | solution.py:273
  19.8 2.1 %collective-permute-start.7 = (bf16[224,128]{1,0:T(8,128)(2,1)S(1)}, bf16[224,128]{1,0:T(8,128)(2,1)S(1)}, u32[]{:S(2)}, u32[]{:S(2)}) collective-permute-start(bf16[224,128]{1,0:T(8,128)(2,1)S(1)} %constant_dynamic-update-slice_fusion.refs_0_), channel_id=1, source_target_pairs={{0,193},{1,192},{64,129},{65,128},{128,65},{129,64},{192,1},{193,0... | collective-permute-start | bytes 172040 | tf_op jit(solution)/shard_map/ppermute | solution.py:273
  22.7 1.0 %collective-permute-start.5 = (bf16[224,128]{1,0:T(8,128)(2,1)S(1)}, bf16[224,128]{1,0:T(8,128)(2,1)S(1)}, u32[]{:S(2)}, u32[]{:S(2)}) collective-permute-start(bf16[224,128]{1,0:T(8,128)(2,1)S(1)} %constant_dynamic-update-slice_fusion.refs_0_), channel_id=1, source_target_pairs={{0,65},{1,64},{64,1},{65,0},{128,193},{129,192},{192,129},{193,128... | collective-permute-start | bytes 172040 | tf_op jit(solution)/shard_map/ppermute | solution.py:273
  23.7 3.3 %collective-permute-done.2 = bf16[2,64,256]{2,1,0:T(8,128)(2,1)S(1)} collective-permute-done((bf16[2,64,256]{2,1,0:T(8,128)(2,1)S(1)}, bf16[2,64,256]{2,1,0:T(8,128)(2,1)S(1)}, u32[]{:S(2)}, u32[]{:S(2)}) %collective-permute-start.2) | collective-permute-done | bytes 65568 | tf_op jit(solution)/shard_map/ppermute | solution.py:273
  27.1 1.3 %collective-permute-done.3 = bf16[4,64,256]{2,1,0:T(8,128)(2,1)S(1)} collective-permute-done((bf16[4,64,256]{2,1,0:T(8,128)(2,1)S(1)}, bf16[4,64,256]{2,1,0:T(8,128)(2,1)S(1)}, u32[]{:S(2)}, u32[]{:S(2)}) %collective-permute-start.3) | collective-permute-done | bytes 131104 | tf_op jit(solution)/shard_map/ppermute | solution.py:285
  29.3 2.8 %attend.3 = bf16[64,256]{1,0:T(8,128)(2,1)S(1)} custom-call(bf16[224,128]{1,0:T(8,128)(2,1)S(1)} %constant_dynamic-update-slice_fusion.refs_0_, bf16[224,128]{1,0:T(8,128)(2,1)S(1)} %collective-permute-done.5.refs_1_, bf16[224,128]{1,0:T(8,128)(2,1)S(1)} %collective-permute-done.6.refs_2_, bf16[224,128]{1,0:T(8,128)(2,1)S(1)} %collective-permute-done.7.refs_3_, ...), custom_call_target="tpu_custom_call" | custom-call | flops 2147483648 | bytes 1000000 | tf_op jit(solution)/shard_map/attend/pallas_call | solution.py:256
  32.1 2.9 %collective-permute-start.10 = (bf16[64,256]{1,0:T(8,128)(2,1)S(1)}, bf16[64,256]{1,0:T(8,128)(2,1)S(1)}, u32[]{:S(2)}, u32[]{:S(2)}) collective-permute-start(bf16[64,256]{1,0:T(8,128)(2,1)S(1)} %attend.3), channel_id=1, source_target_pairs={{0,7},{1,6},{2,5},{3,4},{4,3},{5,2},{6,1},{7,0},{8,15},{9,14},{10,... | collective-permute-start | bytes 98312 | tf_op jit(solution)/shard_map/ppermute | solution.py:273
  36.8 2.5 %collective-permute-done.9 = bf16[64,256]{1,0:T(8,128)(2,1)S(1)} collective-permute-done((bf16[64,256]{1,0:T(8,128)(2,1)S(1)}, bf16[64,256]{1,0:T(8,128)(2,1)S(1)}, u32[]{:S(2)}, u32[]{:S(2)}) %collective-permute-start.9) | collective-permute-done | bytes 32800 | tf_op jit(solution)/shard_map/ppermute | solution.py:273
  39.3 4.1 %collective-permute-start.13 = (bf16[64,256]{1,0:T(8,128)(2,1)S(1)}, bf16[64,256]{1,0:T(8,128)(2,1)S(1)}, u32[]{:S(2)}, u32[]{:S(2)}) collective-permute-start(bf16[64,256]{1,0:T(8,128)(2,1)S(1)} %add_convert_fusion.2), channel_id=1, source_target_pairs={{0,49},{1,48},{16,33},{17,32},{32,17},{33,16},{48,1},{49,0},{2,51}... | collective-permute-start | bytes 98312 | tf_op jit(solution)/shard_map/ppermute | solution.py:273
  45.4 2.3 %collective-permute-done.12 = bf16[64,256]{1,0:T(8,128)(2,1)S(1)} collective-permute-done((bf16[64,256]{1,0:T(8,128)(2,1)S(1)}, bf16[64,256]{1,0:T(8,128)(2,1)S(1)}, u32[]{:S(2)}, u32[]{:S(2)}) %collective-permute-start.12) | collective-permute-done | bytes 32800 | tf_op jit(solution)/shard_map/ppermute | solution.py:273
  47.7 2.0 %collective-permute-start.17 = (bf16[64,256]{1,0:T(8,128)(2,1)S(1)}, bf16[64,256]{1,0:T(8,128)(2,1)S(1)}, u32[]{:S(2)}, u32[]{:S(2)}) collective-permute-start(bf16[64,256]{1,0:T(8,128)(2,1)S(1)} %get-tuple-element.12.refs_4_.refs_5_), channel_id=1, source_target_pairs={{0,193},{1,192},{64,129},{65,128},{128,65},{129,64},{192,1},{193,0... | collective-permute-start | bytes 98312 | tf_op jit(solution)/shard_map/ppermute | solution.py:273
  49.8 1.9 %collective-permute-start.15 = (bf16[64,256]{1,0:T(8,128)(2,1)S(1)}, bf16[64,256]{1,0:T(8,128)(2,1)S(1)}, u32[]{:S(2)}, u32[]{:S(2)}) collective-permute-start(bf16[64,256]{1,0:T(8,128)(2,1)S(1)} %get-tuple-element.12.refs_4_.refs_5_), channel_id=1, source_target_pairs={{0,65},{1,64},{64,1},{65,0},{128,193},{129,192},{192,129},{193,128... | collective-permute-start | bytes 98312 | tf_op jit(solution)/shard_map/ppermute | solution.py:273
  51.7 1.4 %collective-permute-done.17.refs_8_ = bf16[64,256]{1,0:T(8,128)(2,1)S(1)} collective-permute-done((bf16[64,256]{1,0:T(8,128)(2,1)S(1)}, bf16[64,256]{1,0:T(8,128)(2,1)S(1)}, u32[]{:S(2)}, u32[]{:S(2)}) %collective-permute-start.17) | collective-permute-done | bytes 32800 | tf_op jit(solution)/shard_map/ppermute | solution.py:273
  53.1 1.1 %collective-permute-done.16.refs_7_ = bf16[64,256]{1,0:T(8,128)(2,1)S(1)} collective-permute-done((bf16[64,256]{1,0:T(8,128)(2,1)S(1)}, bf16[64,256]{1,0:T(8,128)(2,1)S(1)}, u32[]{:S(2)}, u32[]{:S(2)}) %collective-permute-start.16) | collective-permute-done | bytes 32800 | tf_op jit(solution)/shard_map/ppermute | solution.py:273
  54.8 3.7 %attend.4 = (f32[6,256,160]{2,1,0:T(8,128)S(1)}, f32[6,256,128]{2,1,0:T(8,128)S(1)}) custom-call(bf16[224,128]{1,0:T(8,128)(2,1)S(1)} %constant_dynamic-update-slice_fusion.refs_0_, bf16[224,128]{1,0:T(8,128)(2,1)S(1)} %collective-permute-done.5.refs_1_, bf16[224,128]{1,0:T(8,128)(2,1)S(1)} %collective-permute-done.6.refs_2_, ...), custom_call_target="tpu_custom_call" | custom-call | flops 3221225472 | bytes 1000000 | tf_op jit(solution)/shard_map/attend/pallas_call | solution.py:256
  58.5 5.0 %attend.5 = bf16[64,256]{1,0:T(8,128)(2,1)S(1)} custom-call(bf16[224,128]{1,0:T(8,128)(2,1)S(1)} %constant_dynamic-update-slice_fusion.refs_0_, bf16[224,128]{1,0:T(8,128)(2,1)S(1)} %collective-permute-done.5.refs_1_, bf16[224,128]{1,0:T(8,128)(2,1)S(1)} %collective-permute-done.6.refs_2_, bf16[224,128]{1,0:T(8,128)(2,1)S(1)} %collective-permute-done.7.refs_3_, ...), custom_call_target="tpu_custom_call" | custom-call | flops 3221225472 | bytes 1000000 | tf_op jit(solution)/shard_map/attend/pallas_call | solution.py:256
  63.6 1.6 %collective-permute-start.21 = (bf16[64,256]{1,0:T(8,128)(2,1)S(1)}, bf16[64,256]{1,0:T(8,128)(2,1)S(1)}, u32[]{:S(2)}, u32[]{:S(2)}) collective-permute-start(bf16[64,256]{1,0:T(8,128)(2,1)S(1)} %attend.5), channel_id=1, source_target_pairs={{0,7},{1,6},{2,5},{3,4},{4,3},{5,2},{6,1},{7,0},{8,15},{9,14},{10,... | collective-permute-start | bytes 98312 | tf_op jit(solution)/shard_map/ppermute | solution.py:273
  65.9 1.6 %collective-permute-start.19 = (bf16[64,256]{1,0:T(8,128)(2,1)S(1)}, bf16[64,256]{1,0:T(8,128)(2,1)S(1)}, u32[]{:S(2)}, u32[]{:S(2)}) collective-permute-start(bf16[64,256]{1,0:T(8,128)(2,1)S(1)} %attend.5), channel_id=1, source_target_pairs={{0,3},{1,2},{2,1},{3,0},{4,7},{5,6},{6,5},{7,4},{8,11},{9,10},{10,... | collective-permute-start | bytes 98312 | tf_op jit(solution)/shard_map/ppermute | solution.py:273
  68.2 1.2 %collective-permute-done.20 = bf16[64,256]{1,0:T(8,128)(2,1)S(1)} collective-permute-done((bf16[64,256]{1,0:T(8,128)(2,1)S(1)}, bf16[64,256]{1,0:T(8,128)(2,1)S(1)}, u32[]{:S(2)}, u32[]{:S(2)}) %collective-permute-start.20) | collective-permute-done | bytes 32800 | tf_op jit(solution)/shard_map/ppermute | solution.py:273
  69.8 2.0 %collective-permute-start.24 = (bf16[64,256]{1,0:T(8,128)(2,1)S(1)}, bf16[64,256]{1,0:T(8,128)(2,1)S(1)}, u32[]{:S(2)}, u32[]{:S(2)}) collective-permute-start(bf16[64,256]{1,0:T(8,128)(2,1)S(1)} %add_convert_fusion), channel_id=1, source_target_pairs={{0,49},{1,48},{16,33},{17,32},{32,17},{33,16},{48,1},{49,0},{2,51}... | collective-permute-start | bytes 98312 | tf_op jit(solution)/shard_map/ppermute | solution.py:273
  75.0 1.5 %collective-permute-done.23 = bf16[64,256]{1,0:T(8,128)(2,1)S(1)} collective-permute-done((bf16[64,256]{1,0:T(8,128)(2,1)S(1)}, bf16[64,256]{1,0:T(8,128)(2,1)S(1)}, u32[]{:S(2)}, u32[]{:S(2)}) %collective-permute-start.23) | collective-permute-done | bytes 32800 | tf_op jit(solution)/shard_map/ppermute | solution.py:273
  (55 shorter events, 14.6 us)
Async XLA Ops:
  0.6 11.2 %collective-permute-start.1 = (bf16[64,256]{1,0:T(8,128)(2,1)}, bf16[64,256]{1,0:T(8,128)(2,1)S(1)}, u32[]{:S(2)}, u32[]{:S(2)}) collective-permute-start(bf16[64,256]{1,0:T(8,128)(2,1)} %bitcast.56), channel_id=1, source_target_pairs={{0,1},{1,0},{2,3},{3,2},{4,5},{5,4},{6,7},{7,6},{8,9},{9,8},{10,11... | collective-permute-start | bytes 98312 | tf_op jit(solution)/shard_map/ppermute | solution.py:285
  4.0 7.9 %collective-permute-start = (bf16[64,256]{1,0:T(8,128)(2,1)}, bf16[64,256]{1,0:T(8,128)(2,1)S(1)}, u32[]{:S(2)}, u32[]{:S(2)}) collective-permute-start(bf16[64,256]{1,0:T(8,128)(2,1)} %bitcast.45), channel_id=1, source_target_pairs={{0,65},{1,64},{64,1},{65,0},{128,193},{129,192},{192,129},{193,128... | collective-permute-start | bytes 98312 | tf_op jit(solution)/shard_map/ppermute | solution.py:273
  11.9 7.9 %collective-permute-start.4 = (bf16[80,128]{1,0:T(8,128)(2,1)S(1)}, bf16[80,128]{1,0:T(8,128)(2,1)S(1)}, u32[]{:S(2)}, u32[]{:S(2)}) collective-permute-start(bf16[80,128]{1,0:T(8,128)(2,1)S(1)} %slice.14), channel_id=1, source_target_pairs={{0,9},{1,8},{8,1},{9,0},{2,11},{3,10},{10,3},{11,2},{4,13},{5,12},... | collective-permute-start | bytes 61448 | tf_op jit(solution)/shard_map/ppermute | solution.py:273
  18.2 8.8 %collective-permute-start.2 = (bf16[2,64,256]{2,1,0:T(8,128)(2,1)S(1)}, bf16[2,64,256]{2,1,0:T(8,128)(2,1)S(1)}, u32[]{:S(2)}, u32[]{:S(2)}) collective-permute-start(bf16[2,64,256]{2,1,0:T(8,128)(2,1)S(1)} %pad_maximum_fusion.2), channel_id=1, source_target_pairs={{0,129},{1,128},{64,193},{65,192},{128,1},{129,0},{192,65},{193,64... | collective-permute-start | bytes 196616 | tf_op jit(solution)/shard_map/ppermute | solution.py:273
  19.8 8.7 %collective-permute-start.7 = (bf16[224,128]{1,0:T(8,128)(2,1)S(1)}, bf16[224,128]{1,0:T(8,128)(2,1)S(1)}, u32[]{:S(2)}, u32[]{:S(2)}) collective-permute-start(bf16[224,128]{1,0:T(8,128)(2,1)S(1)} %constant_dynamic-update-slice_fusion.refs_0_), channel_id=1, source_target_pairs={{0,193},{1,192},{64,129},{65,128},{128,65},{129,64},{192,1},{193,0... | collective-permute-start | bytes 172040 | tf_op jit(solution)/shard_map/ppermute | solution.py:273
  21.8 7.5 %collective-permute-start.6 = (bf16[224,128]{1,0:T(8,128)(2,1)S(1)}, bf16[224,128]{1,0:T(8,128)(2,1)S(1)}, u32[]{:S(2)}, u32[]{:S(2)}) collective-permute-start(bf16[224,128]{1,0:T(8,128)(2,1)S(1)} %constant_dynamic-update-slice_fusion.refs_0_), channel_id=1, source_target_pairs={{0,129},{1,128},{64,193},{65,192},{128,1},{129,0},{192,65},{193,64... | collective-permute-start | bytes 172040 | tf_op jit(solution)/shard_map/ppermute | solution.py:273
  22.7 6.6 %collective-permute-start.5 = (bf16[224,128]{1,0:T(8,128)(2,1)S(1)}, bf16[224,128]{1,0:T(8,128)(2,1)S(1)}, u32[]{:S(2)}, u32[]{:S(2)}) collective-permute-start(bf16[224,128]{1,0:T(8,128)(2,1)S(1)} %constant_dynamic-update-slice_fusion.refs_0_), channel_id=1, source_target_pairs={{0,65},{1,64},{64,1},{65,0},{128,193},{129,192},{192,129},{193,128... | collective-permute-start | bytes 172040 | tf_op jit(solution)/shard_map/ppermute | solution.py:273
  32.1 4.6 %collective-permute-start.10 = (bf16[64,256]{1,0:T(8,128)(2,1)S(1)}, bf16[64,256]{1,0:T(8,128)(2,1)S(1)}, u32[]{:S(2)}, u32[]{:S(2)}) collective-permute-start(bf16[64,256]{1,0:T(8,128)(2,1)S(1)} %attend.3), channel_id=1, source_target_pairs={{0,7},{1,6},{2,5},{3,4},{4,3},{5,2},{6,1},{7,0},{8,15},{9,14},{10,... | collective-permute-start | bytes 98312 | tf_op jit(solution)/shard_map/ppermute | solution.py:273
  35.0 4.3 %collective-permute-start.9 = (bf16[64,256]{1,0:T(8,128)(2,1)S(1)}, bf16[64,256]{1,0:T(8,128)(2,1)S(1)}, u32[]{:S(2)}, u32[]{:S(2)}) collective-permute-start(bf16[64,256]{1,0:T(8,128)(2,1)S(1)} %attend.3), channel_id=1, source_target_pairs={{0,4},{1,5},{2,6},{3,7},{4,0},{5,1},{6,2},{7,3},{8,12},{9,13},{10,... | collective-permute-start | bytes 98312 | tf_op jit(solution)/shard_map/ppermute | solution.py:273
  35.4 3.9 %collective-permute-start.8 = (bf16[64,256]{1,0:T(8,128)(2,1)S(1)}, bf16[64,256]{1,0:T(8,128)(2,1)S(1)}, u32[]{:S(2)}, u32[]{:S(2)}) collective-permute-start(bf16[64,256]{1,0:T(8,128)(2,1)S(1)} %attend.3), channel_id=1, source_target_pairs={{0,3},{1,2},{2,1},{3,0},{4,7},{5,6},{6,5},{7,4},{8,11},{9,10},{10,... | collective-permute-start | bytes 98312 | tf_op jit(solution)/shard_map/ppermute | solution.py:273
  39.3 6.1 %collective-permute-start.13 = (bf16[64,256]{1,0:T(8,128)(2,1)S(1)}, bf16[64,256]{1,0:T(8,128)(2,1)S(1)}, u32[]{:S(2)}, u32[]{:S(2)}) collective-permute-start(bf16[64,256]{1,0:T(8,128)(2,1)S(1)} %add_convert_fusion.2), channel_id=1, source_target_pairs={{0,49},{1,48},{16,33},{17,32},{32,17},{33,16},{48,1},{49,0},{2,51}... | collective-permute-start | bytes 98312 | tf_op jit(solution)/shard_map/ppermute | solution.py:273
  43.4 4.3 %collective-permute-start.12 = (bf16[64,256]{1,0:T(8,128)(2,1)S(1)}, bf16[64,256]{1,0:T(8,128)(2,1)S(1)}, u32[]{:S(2)}, u32[]{:S(2)}) collective-permute-start(bf16[64,256]{1,0:T(8,128)(2,1)S(1)} %add_convert_fusion.2), channel_id=1, source_target_pairs={{0,32},{1,33},{16,48},{17,49},{32,0},{33,1},{48,16},{49,17},{2,34}... | collective-permute-start | bytes 98312 | tf_op jit(solution)/shard_map/ppermute | solution.py:273
  43.9 3.7 %collective-permute-start.11 = (bf16[64,256]{1,0:T(8,128)(2,1)S(1)}, bf16[64,256]{1,0:T(8,128)(2,1)S(1)}, u32[]{:S(2)}, u32[]{:S(2)}) collective-permute-start(bf16[64,256]{1,0:T(8,128)(2,1)S(1)} %add_convert_fusion.2), channel_id=1, source_target_pairs={{0,17},{1,16},{16,1},{17,0},{32,49},{33,48},{48,33},{49,32},{2,19}... | collective-permute-start | bytes 98312 | tf_op jit(solution)/shard_map/ppermute | solution.py:273
  47.7 5.4 %collective-permute-start.17 = (bf16[64,256]{1,0:T(8,128)(2,1)S(1)}, bf16[64,256]{1,0:T(8,128)(2,1)S(1)}, u32[]{:S(2)}, u32[]{:S(2)}) collective-permute-start(bf16[64,256]{1,0:T(8,128)(2,1)S(1)} %get-tuple-element.12.refs_4_.refs_5_), channel_id=1, source_target_pairs={{0,193},{1,192},{64,129},{65,128},{128,65},{129,64},{192,1},{193,0... | collective-permute-start | bytes 98312 | tf_op jit(solution)/shard_map/ppermute | solution.py:273
  49.8 4.5 %collective-permute-start.16 = (bf16[64,256]{1,0:T(8,128)(2,1)S(1)}, bf16[64,256]{1,0:T(8,128)(2,1)S(1)}, u32[]{:S(2)}, u32[]{:S(2)}) collective-permute-start(bf16[64,256]{1,0:T(8,128)(2,1)S(1)} %get-tuple-element.12.refs_4_.refs_5_), channel_id=1, source_target_pairs={{0,129},{1,128},{64,193},{65,192},{128,1},{129,0},{192,65},{193,64... | collective-permute-start | bytes 98312 | tf_op jit(solution)/shard_map/ppermute | solution.py:273
  49.8 4.6 %collective-permute-start.15 = (bf16[64,256]{1,0:T(8,128)(2,1)S(1)}, bf16[64,256]{1,0:T(8,128)(2,1)S(1)}, u32[]{:S(2)}, u32[]{:S(2)}) collective-permute-start(bf16[64,256]{1,0:T(8,128)(2,1)S(1)} %get-tuple-element.12.refs_4_.refs_5_), channel_id=1, source_target_pairs={{0,65},{1,64},{64,1},{65,0},{128,193},{129,192},{192,129},{193,128... | collective-permute-start | bytes 98312 | tf_op jit(solution)/shard_map/ppermute | solution.py:273
  54.4 4.1 %collective-permute-start.18 = (bf16[4,64,256]{2,1,0:T(8,128)(2,1)S(1)}, bf16[4,64,256]{2,1,0:T(8,128)(2,1)S(1)}, u32[]{:S(2)}, u32[]{:S(2)}) collective-permute-start(bf16[4,64,256]{2,1,0:T(8,128)(2,1)S(1)} %pad_maximum_fusion.1), channel_id=1, source_target_pairs={{0,1},{1,0},{2,3},{3,2},{4,5},{5,4},{6,7},{7,6},{8,9},{9,8},{10,11... | collective-permute-start | bytes 393224 | tf_op jit(solution)/shard_map/ppermute | solution.py:285
  63.6 4.6 %collective-permute-start.21 = (bf16[64,256]{1,0:T(8,128)(2,1)S(1)}, bf16[64,256]{1,0:T(8,128)(2,1)S(1)}, u32[]{:S(2)}, u32[]{:S(2)}) collective-permute-start(bf16[64,256]{1,0:T(8,128)(2,1)S(1)} %attend.5), channel_id=1, source_target_pairs={{0,7},{1,6},{2,5},{3,4},{4,3},{5,2},{6,1},{7,0},{8,15},{9,14},{10,... | collective-permute-start | bytes 98312 | tf_op jit(solution)/shard_map/ppermute | solution.py:273
  65.1 4.3 %collective-permute-start.20 = (bf16[64,256]{1,0:T(8,128)(2,1)S(1)}, bf16[64,256]{1,0:T(8,128)(2,1)S(1)}, u32[]{:S(2)}, u32[]{:S(2)}) collective-permute-start(bf16[64,256]{1,0:T(8,128)(2,1)S(1)} %attend.5), channel_id=1, source_target_pairs={{0,4},{1,5},{2,6},{3,7},{4,0},{5,1},{6,2},{7,3},{8,12},{9,13},{10,... | collective-permute-start | bytes 98312 | tf_op jit(solution)/shard_map/ppermute | solution.py:273
  65.9 4.0 %collective-permute-start.19 = (bf16[64,256]{1,0:T(8,128)(2,1)S(1)}, bf16[64,256]{1,0:T(8,128)(2,1)S(1)}, u32[]{:S(2)}, u32[]{:S(2)}) collective-permute-start(bf16[64,256]{1,0:T(8,128)(2,1)S(1)} %attend.5), channel_id=1, source_target_pairs={{0,3},{1,2},{2,1},{3,0},{4,7},{5,6},{6,5},{7,4},{8,11},{9,10},{10,... | collective-permute-start | bytes 98312 | tf_op jit(solution)/shard_map/ppermute | solution.py:273
  69.8 5.2 %collective-permute-start.24 = (bf16[64,256]{1,0:T(8,128)(2,1)S(1)}, bf16[64,256]{1,0:T(8,128)(2,1)S(1)}, u32[]{:S(2)}, u32[]{:S(2)}) collective-permute-start(bf16[64,256]{1,0:T(8,128)(2,1)S(1)} %add_convert_fusion), channel_id=1, source_target_pairs={{0,49},{1,48},{16,33},{17,32},{32,17},{33,16},{48,1},{49,0},{2,51}... | collective-permute-start | bytes 98312 | tf_op jit(solution)/shard_map/ppermute | solution.py:273
  71.9 4.6 %collective-permute-start.23 = (bf16[64,256]{1,0:T(8,128)(2,1)S(1)}, bf16[64,256]{1,0:T(8,128)(2,1)S(1)}, u32[]{:S(2)}, u32[]{:S(2)}) collective-permute-start(bf16[64,256]{1,0:T(8,128)(2,1)S(1)} %add_convert_fusion), channel_id=1, source_target_pairs={{0,32},{1,33},{16,48},{17,49},{32,0},{33,1},{48,16},{49,17},{2,34}... | collective-permute-start | bytes 98312 | tf_op jit(solution)/shard_map/ppermute | solution.py:273
  72.9 3.6 %collective-permute-start.22 = (bf16[64,256]{1,0:T(8,128)(2,1)S(1)}, bf16[64,256]{1,0:T(8,128)(2,1)S(1)}, u32[]{:S(2)}, u32[]{:S(2)}) collective-permute-start(bf16[64,256]{1,0:T(8,128)(2,1)S(1)} %add_convert_fusion), channel_id=1, source_target_pairs={{0,17},{1,16},{16,1},{17,0},{32,49},{33,48},{48,33},{49,32},{2,19}... | collective-permute-start | bytes 98312 | tf_op jit(solution)/shard_map/ppermute | solution.py:273
  73.7 3.6 %collective-permute-start.14 = (bf16[64,256]{1,0:T(8,128)(2,1)S(1)}, bf16[64,256]{1,0:T(8,128)(2,1)S(1)}, u32[]{:S(2)}, u32[]{:S(2)}) collective-permute-start(bf16[64,256]{1,0:T(8,128)(2,1)S(1)} %get-tuple-element.13), channel_id=1, source_target_pairs={{0,1},{1,0},{2,3},{3,2},{4,5},{5,4},{6,7},{7,6},{8,9},{9,8},{10,11... | collective-permute-start | bytes 98312 | tf_op jit(solution)/shard_map/ppermute | solution.py:285
  (5 other events, 21.8 us)

commit v6 on v5

--- a/solution.py
+++ b/solution.py
@@ -287,7 +287,7 @@
 
 def add_over(value, axis):
     sent = lax.optimization_barrier(value.astype(bf16))
-    parts = [part.astype(f32) for part in swap_all(sent, axis, (1, 0, 1))]
+    parts = [part.astype(f32) for part in swap_all(sent, axis, (0, 1, 1))]
     return (parts[0] + parts[1]) + (parts[2] + parts[3])
 
 
@@ -302,7 +302,7 @@
     gen_sigma = gen_step[0].astype(f32) / step_scale
     score_sigma = score_step[0].astype(f32) / step_scale
     latents, noise = latent_noise.T, score_noise.T
-    odd = (lax.axis_index("x") + lax.axis_index("y")) % 2 == 1
+    odd = (lax.axis_index("x") // 2 + lax.axis_index("y") // 2) % 2 == 1
 
     first = swap(latents, "mp", 1, 1)
     noise = jnp.where(odd, other_core(noise), noise)

time: 79 us -> 78.6 us (level)
  starting transfers between devices: 37.5 us -> 35 us
  waiting for transfers between devices: 19.7 us -> 21.7 us
    ppermute x21, starting transfers between devices: 32.4 us -> 30.1 us  [swap(): lax.ppermute(value, axes, [(i, i ^ flip) for i in range(lax.axis_size(axe...]
    ppermute x21, waiting for transfers between devices: 18.1 us -> 20 us  [swap(): lax.ppermute(value, axes, [(i, i ^ flip) for i in range(lax.axis_size(axe...]
  transfers between devices with their start and end apart: 26 -> 26, of which waited for: 17 -> 15; matrix products, arithmetic and copies ran while one was open for 1% -> 1% of each run, Pallas kernels for 12% -> 12%
where the time goes in v6:
time: 78.6 us; the launch traced here: 78.4 us
  starting transfers between devices  35 us (45%)
  waiting for transfers between devices  21.7 us (28%)
  Pallas kernels  17.3 us (22%)
  between operations  2.16 us (3%)
  other arithmetic  1.42 us (2%)
    ppermute x21, starting transfers between devices, swap(): lax.ppermute(value, axes, [(i, i ^ flip) for i in range(lax.axis_size(axe...  30.1 us
    ppermute x21, waiting for transfers between devices, swap(): lax.ppermute(value, axes, [(i, i ^ flip) for i in range(lax.axis_size(axe...  20 us
    pallas_call x3, Pallas kernels, attend(): pl.pallas_call(functools.partial(attend_kernel, terms, count, bool(state)...  11.5 us
    pallas_call x1, Pallas kernels, fold_maps(): pl.pallas_call(maps_kernel, in_specs=[pl.BlockSpec(memory_space=pltpu.SME...  5.81 us
    ppermute x5, starting transfers between devices, other_core(): return lax.ppermute(value, 'tp', [(0, 1), (1, 0)])  4.97 us
    ppermute x5, waiting for transfers between devices, other_core(): return lax.ppermute(value, 'tp', [(0, 1), (1, 0)])  1.6 us
  transfers between devices with their start and end apart: 26, of which 15 were waited for; matrix products, arithmetic and copies ran while one was open for 1% of the time, Pallas kernels for 12%

profile of v6, /device:TPU:1, one launch (start us, length us, event | category | flops | bytes accessed | tf_op | source)
XLA Modules:
  0.0 78.4 jit_solution(10154335306693670942)
XLA Ops:
  0.6 3.3 %collective-permute-start.1 = (bf16[64,256]{1,0:T(8,128)(2,1)}, bf16[64,256]{1,0:T(8,128)(2,1)S(1)}, u32[]{:S(2)}, u32[]{:S(2)}) collective-permute-start(bf16[64,256]{1,0:T(8,128)(2,1)} %bitcast.56), channel_id=1, source_target_pairs={{0,1},{1,0},{2,3},{3,2},{4,5},{5,4},{6,7},{7,6},{8,9},{9,8},{10,11... | collective-permute-start | bytes 98312 | tf_op jit(solution)/shard_map/ppermute | solution.py:285
  6.0 5.8 %fold_maps.1 = bf16[144,128]{1,0:T(8,128)(2,1)S(1)} custom-call(s32[1]{0:T(128)S(6)} %copy.11.gen_ref, s32[1]{0:T(128)S(6)} %copy.12.score_ref, bf16[64,5120]{1,0:T(8,128)(2,1)} %bitcast.59, bf16[64,128]{1,0:T(8,128)(2,1)S(1)} %bitcast.55, bf16[256,10240]{1,0:T(8,128)(2,1)} %bitcast.57, bf16[384,5120]{1,0:T(8,128)(2,1)} %bitcast.58), custom_call_target="tpu_custom_call" | custom-call | flops 6000000000 | bytes 10000000 | tf_op jit(solution)/shard_map/fold_maps/pallas_call | solution.py:157
  11.9 6.3 %collective-permute-start.4 = (bf16[80,128]{1,0:T(8,128)(2,1)S(1)}, bf16[80,128]{1,0:T(8,128)(2,1)S(1)}, u32[]{:S(2)}, u32[]{:S(2)}) collective-permute-start(bf16[80,128]{1,0:T(8,128)(2,1)S(1)} %slice.14), channel_id=1, source_target_pairs={{0,9},{1,8},{8,1},{9,0},{2,11},{3,10},{10,3},{11,2},{4,13},{5,12},... | collective-permute-start | bytes 61448 | tf_op jit(solution)/shard_map/ppermute | solution.py:273
  18.2 1.2 %collective-permute-start.2 = (bf16[2,64,256]{2,1,0:T(8,128)(2,1)S(1)}, bf16[2,64,256]{2,1,0:T(8,128)(2,1)S(1)}, u32[]{:S(2)}, u32[]{:S(2)}) collective-permute-start(bf16[2,64,256]{2,1,0:T(8,128)(2,1)S(1)} %pad_maximum_fusion.2), channel_id=1, source_target_pairs={{0,129},{1,128},{64,193},{65,192},{128,1},{129,0},{192,65},{193,64... | collective-permute-start | bytes 196616 | tf_op jit(solution)/shard_map/ppermute | solution.py:273
  19.8 2.1 %collective-permute-start.7 = (bf16[224,128]{1,0:T(8,128)(2,1)S(1)}, bf16[224,128]{1,0:T(8,128)(2,1)S(1)}, u32[]{:S(2)}, u32[]{:S(2)}) collective-permute-start(bf16[224,128]{1,0:T(8,128)(2,1)S(1)} %constant_dynamic-update-slice_fusion.refs_0_), channel_id=1, source_target_pairs={{0,193},{1,192},{64,129},{65,128},{128,65},{129,64},{192,1},{193,0... | collective-permute-start | bytes 172040 | tf_op jit(solution)/shard_map/ppermute | solution.py:273
  23.7 3.3 %collective-permute-done.2 = bf16[2,64,256]{2,1,0:T(8,128)(2,1)S(1)} collective-permute-done((bf16[2,64,256]{2,1,0:T(8,128)(2,1)S(1)}, bf16[2,64,256]{2,1,0:T(8,128)(2,1)S(1)}, u32[]{:S(2)}, u32[]{:S(2)}) %collective-permute-start.2) | collective-permute-done | bytes 65568 | tf_op jit(solution)/shard_map/ppermute | solution.py:273
  27.1 1.3 %collective-permute-done.3 = bf16[4,64,256]{2,1,0:T(8,128)(2,1)S(1)} collective-permute-done((bf16[4,64,256]{2,1,0:T(8,128)(2,1)S(1)}, bf16[4,64,256]{2,1,0:T(8,128)(2,1)S(1)}, u32[]{:S(2)}, u32[]{:S(2)}) %collective-permute-start.3) | collective-permute-done | bytes 131104 | tf_op jit(solution)/shard_map/ppermute | solution.py:285
  29.3 2.8 %attend.3 = bf16[64,256]{1,0:T(8,128)(2,1)S(1)} custom-call(bf16[224,128]{1,0:T(8,128)(2,1)S(1)} %constant_dynamic-update-slice_fusion.refs_0_, bf16[224,128]{1,0:T(8,128)(2,1)S(1)} %collective-permute-done.5.refs_1_, bf16[224,128]{1,0:T(8,128)(2,1)S(1)} %collective-permute-done.6.refs_2_, bf16[224,128]{1,0:T(8,128)(2,1)S(1)} %collective-permute-done.7.refs_3_, ...), custom_call_target="tpu_custom_call" | custom-call | flops 2147483648 | bytes 1000000 | tf_op jit(solution)/shard_map/attend/pallas_call | solution.py:256
  32.1 2.9 %collective-permute-start.10 = (bf16[64,256]{1,0:T(8,128)(2,1)S(1)}, bf16[64,256]{1,0:T(8,128)(2,1)S(1)}, u32[]{:S(2)}, u32[]{:S(2)}) collective-permute-start(bf16[64,256]{1,0:T(8,128)(2,1)S(1)} %attend.3), channel_id=1, source_target_pairs={{0,7},{1,6},{2,5},{3,4},{4,3},{5,2},{6,1},{7,0},{8,15},{9,14},{10,... | collective-permute-start | bytes 98312 | tf_op jit(solution)/shard_map/ppermute | solution.py:273
  36.8 3.4 %collective-permute-done.9 = bf16[64,256]{1,0:T(8,128)(2,1)S(1)} collective-permute-done((bf16[64,256]{1,0:T(8,128)(2,1)S(1)}, bf16[64,256]{1,0:T(8,128)(2,1)S(1)}, u32[]{:S(2)}, u32[]{:S(2)}) %collective-permute-start.9) | collective-permute-done | bytes 32800 | tf_op jit(solution)/shard_map/ppermute | solution.py:273
  40.2 2.5 %collective-permute-start.13 = (bf16[64,256]{1,0:T(8,128)(2,1)S(1)}, bf16[64,256]{1,0:T(8,128)(2,1)S(1)}, u32[]{:S(2)}, u32[]{:S(2)}) collective-permute-start(bf16[64,256]{1,0:T(8,128)(2,1)S(1)} %add_convert_fusion.2), channel_id=1, source_target_pairs={{0,49},{1,48},{16,33},{17,32},{32,17},{33,16},{48,1},{49,0},{2,51}... | collective-permute-start | bytes 98312 | tf_op jit(solution)/shard_map/ppermute | solution.py:273
  44.8 3.0 %collective-permute-done.12 = bf16[64,256]{1,0:T(8,128)(2,1)S(1)} collective-permute-done((bf16[64,256]{1,0:T(8,128)(2,1)S(1)}, bf16[64,256]{1,0:T(8,128)(2,1)S(1)}, u32[]{:S(2)}, u32[]{:S(2)}) %collective-permute-start.12) | collective-permute-done | bytes 32800 | tf_op jit(solution)/shard_map/ppermute | solution.py:273
  47.8 2.5 %collective-permute-start.17 = (bf16[64,256]{1,0:T(8,128)(2,1)S(1)}, bf16[64,256]{1,0:T(8,128)(2,1)S(1)}, u32[]{:S(2)}, u32[]{:S(2)}) collective-permute-start(bf16[64,256]{1,0:T(8,128)(2,1)S(1)} %get-tuple-element.12.refs_4_.refs_5_), channel_id=1, source_target_pairs={{0,193},{1,192},{64,129},{65,128},{128,65},{129,64},{192,1},{193,0... | collective-permute-start | bytes 98312 | tf_op jit(solution)/shard_map/ppermute | solution.py:273
  50.4 1.5 %collective-permute-start.15 = (bf16[64,256]{1,0:T(8,128)(2,1)S(1)}, bf16[64,256]{1,0:T(8,128)(2,1)S(1)}, u32[]{:S(2)}, u32[]{:S(2)}) collective-permute-start(bf16[64,256]{1,0:T(8,128)(2,1)S(1)} %get-tuple-element.12.refs_4_.refs_5_), channel_id=1, source_target_pairs={{0,65},{1,64},{64,1},{65,0},{128,193},{129,192},{192,129},{193,128... | collective-permute-start | bytes 98312 | tf_op jit(solution)/shard_map/ppermute | solution.py:273
  51.9 1.4 %collective-permute-done.17.refs_8_ = bf16[64,256]{1,0:T(8,128)(2,1)S(1)} collective-permute-done((bf16[64,256]{1,0:T(8,128)(2,1)S(1)}, bf16[64,256]{1,0:T(8,128)(2,1)S(1)}, u32[]{:S(2)}, u32[]{:S(2)}) %collective-permute-start.17) | collective-permute-done | bytes 32800 | tf_op jit(solution)/shard_map/ppermute | solution.py:273
  53.3 1.3 %collective-permute-done.16.refs_7_ = bf16[64,256]{1,0:T(8,128)(2,1)S(1)} collective-permute-done((bf16[64,256]{1,0:T(8,128)(2,1)S(1)}, bf16[64,256]{1,0:T(8,128)(2,1)S(1)}, u32[]{:S(2)}, u32[]{:S(2)}) %collective-permute-start.16) | collective-permute-done | bytes 32800 | tf_op jit(solution)/shard_map/ppermute | solution.py:273
  54.9 3.7 %attend.4 = (f32[6,256,160]{2,1,0:T(8,128)S(1)}, f32[6,256,128]{2,1,0:T(8,128)S(1)}) custom-call(bf16[224,128]{1,0:T(8,128)(2,1)S(1)} %constant_dynamic-update-slice_fusion.refs_0_, bf16[224,128]{1,0:T(8,128)(2,1)S(1)} %collective-permute-done.5.refs_1_, bf16[224,128]{1,0:T(8,128)(2,1)S(1)} %collective-permute-done.6.refs_2_, ...), custom_call_target="tpu_custom_call" | custom-call | flops 3221225472 | bytes 1000000 | tf_op jit(solution)/shard_map/attend/pallas_call | solution.py:256
  58.6 5.0 %attend.5 = bf16[64,256]{1,0:T(8,128)(2,1)S(1)} custom-call(bf16[224,128]{1,0:T(8,128)(2,1)S(1)} %constant_dynamic-update-slice_fusion.refs_0_, bf16[224,128]{1,0:T(8,128)(2,1)S(1)} %collective-permute-done.5.refs_1_, bf16[224,128]{1,0:T(8,128)(2,1)S(1)} %collective-permute-done.6.refs_2_, bf16[224,128]{1,0:T(8,128)(2,1)S(1)} %collective-permute-done.7.refs_3_, ...), custom_call_target="tpu_custom_call" | custom-call | flops 3221225472 | bytes 1000000 | tf_op jit(solution)/shard_map/attend/pallas_call | solution.py:256
  63.7 1.3 %collective-permute-start.21 = (bf16[64,256]{1,0:T(8,128)(2,1)S(1)}, bf16[64,256]{1,0:T(8,128)(2,1)S(1)}, u32[]{:S(2)}, u32[]{:S(2)}) collective-permute-start(bf16[64,256]{1,0:T(8,128)(2,1)S(1)} %attend.5), channel_id=1, source_target_pairs={{0,7},{1,6},{2,5},{3,4},{4,3},{5,2},{6,1},{7,0},{8,15},{9,14},{10,... | collective-permute-start | bytes 98312 | tf_op jit(solution)/shard_map/ppermute | solution.py:273
  66.1 1.2 %collective-permute-start.19 = (bf16[64,256]{1,0:T(8,128)(2,1)S(1)}, bf16[64,256]{1,0:T(8,128)(2,1)S(1)}, u32[]{:S(2)}, u32[]{:S(2)}) collective-permute-start(bf16[64,256]{1,0:T(8,128)(2,1)S(1)} %attend.5), channel_id=1, source_target_pairs={{0,2},{1,3},{2,0},{3,1},{4,6},{5,7},{6,4},{7,5},{8,10},{9,11},{10,... | collective-permute-start | bytes 98312 | tf_op jit(solution)/shard_map/ppermute | solution.py:273
  68.3 1.5 %collective-permute-done.20 = bf16[64,256]{1,0:T(8,128)(2,1)S(1)} collective-permute-done((bf16[64,256]{1,0:T(8,128)(2,1)S(1)}, bf16[64,256]{1,0:T(8,128)(2,1)S(1)}, u32[]{:S(2)}, u32[]{:S(2)}) %collective-permute-start.20) | collective-permute-done | bytes 32800 | tf_op jit(solution)/shard_map/ppermute | solution.py:273
  69.8 1.6 %collective-permute-start.24 = (bf16[64,256]{1,0:T(8,128)(2,1)S(1)}, bf16[64,256]{1,0:T(8,128)(2,1)S(1)}, u32[]{:S(2)}, u32[]{:S(2)}) collective-permute-start(bf16[64,256]{1,0:T(8,128)(2,1)S(1)} %add_convert_fusion), channel_id=1, source_target_pairs={{0,49},{1,48},{16,33},{17,32},{32,17},{33,16},{48,1},{49,0},{2,51}... | collective-permute-start | bytes 98312 | tf_op jit(solution)/shard_map/ppermute | solution.py:273
  72.1 1.3 %collective-permute-start.22 = (bf16[64,256]{1,0:T(8,128)(2,1)S(1)}, bf16[64,256]{1,0:T(8,128)(2,1)S(1)}, u32[]{:S(2)}, u32[]{:S(2)}) collective-permute-start(bf16[64,256]{1,0:T(8,128)(2,1)S(1)} %add_convert_fusion), channel_id=1, source_target_pairs={{0,16},{1,17},{16,0},{17,1},{32,48},{33,49},{48,32},{49,33},{2,18}... | collective-permute-start | bytes 98312 | tf_op jit(solution)/shard_map/ppermute | solution.py:273
  74.8 1.5 %collective-permute-done.23 = bf16[64,256]{1,0:T(8,128)(2,1)S(1)} collective-permute-done((bf16[64,256]{1,0:T(8,128)(2,1)S(1)}, bf16[64,256]{1,0:T(8,128)(2,1)S(1)}, u32[]{:S(2)}, u32[]{:S(2)}) %collective-permute-start.23) | collective-permute-done | bytes 32800 | tf_op jit(solution)/shard_map/ppermute | solution.py:273
  (55 shorter events, 14.5 us)
Async XLA Ops:
  0.6 11.2 %collective-permute-start.1 = (bf16[64,256]{1,0:T(8,128)(2,1)}, bf16[64,256]{1,0:T(8,128)(2,1)S(1)}, u32[]{:S(2)}, u32[]{:S(2)}) collective-permute-start(bf16[64,256]{1,0:T(8,128)(2,1)} %bitcast.56), channel_id=1, source_target_pairs={{0,1},{1,0},{2,3},{3,2},{4,5},{5,4},{6,7},{7,6},{8,9},{9,8},{10,11... | collective-permute-start | bytes 98312 | tf_op jit(solution)/shard_map/ppermute | solution.py:285
  4.0 7.9 %collective-permute-start = (bf16[64,256]{1,0:T(8,128)(2,1)}, bf16[64,256]{1,0:T(8,128)(2,1)S(1)}, u32[]{:S(2)}, u32[]{:S(2)}) collective-permute-start(bf16[64,256]{1,0:T(8,128)(2,1)} %bitcast.45), channel_id=1, source_target_pairs={{0,65},{1,64},{64,1},{65,0},{128,193},{129,192},{192,129},{193,128... | collective-permute-start | bytes 98312 | tf_op jit(solution)/shard_map/ppermute | solution.py:273
  11.9 7.9 %collective-permute-start.4 = (bf16[80,128]{1,0:T(8,128)(2,1)S(1)}, bf16[80,128]{1,0:T(8,128)(2,1)S(1)}, u32[]{:S(2)}, u32[]{:S(2)}) collective-permute-start(bf16[80,128]{1,0:T(8,128)(2,1)S(1)} %slice.14), channel_id=1, source_target_pairs={{0,9},{1,8},{8,1},{9,0},{2,11},{3,10},{10,3},{11,2},{4,13},{5,12},... | collective-permute-start | bytes 61448 | tf_op jit(solution)/shard_map/ppermute | solution.py:273
  18.2 8.8 %collective-permute-start.2 = (bf16[2,64,256]{2,1,0:T(8,128)(2,1)S(1)}, bf16[2,64,256]{2,1,0:T(8,128)(2,1)S(1)}, u32[]{:S(2)}, u32[]{:S(2)}) collective-permute-start(bf16[2,64,256]{2,1,0:T(8,128)(2,1)S(1)} %pad_maximum_fusion.2), channel_id=1, source_target_pairs={{0,129},{1,128},{64,193},{65,192},{128,1},{129,0},{192,65},{193,64... | collective-permute-start | bytes 196616 | tf_op jit(solution)/shard_map/ppermute | solution.py:273
  19.8 8.7 %collective-permute-start.7 = (bf16[224,128]{1,0:T(8,128)(2,1)S(1)}, bf16[224,128]{1,0:T(8,128)(2,1)S(1)}, u32[]{:S(2)}, u32[]{:S(2)}) collective-permute-start(bf16[224,128]{1,0:T(8,128)(2,1)S(1)} %constant_dynamic-update-slice_fusion.refs_0_), channel_id=1, source_target_pairs={{0,193},{1,192},{64,129},{65,128},{128,65},{129,64},{192,1},{193,0... | collective-permute-start | bytes 172040 | tf_op jit(solution)/shard_map/ppermute | solution.py:273
  21.8 7.5 %collective-permute-start.6 = (bf16[224,128]{1,0:T(8,128)(2,1)S(1)}, bf16[224,128]{1,0:T(8,128)(2,1)S(1)}, u32[]{:S(2)}, u32[]{:S(2)}) collective-permute-start(bf16[224,128]{1,0:T(8,128)(2,1)S(1)} %constant_dynamic-update-slice_fusion.refs_0_), channel_id=1, source_target_pairs={{0,129},{1,128},{64,193},{65,192},{128,1},{129,0},{192,65},{193,64... | collective-permute-start | bytes 172040 | tf_op jit(solution)/shard_map/ppermute | solution.py:273
  22.7 6.6 %collective-permute-start.5 = (bf16[224,128]{1,0:T(8,128)(2,1)S(1)}, bf16[224,128]{1,0:T(8,128)(2,1)S(1)}, u32[]{:S(2)}, u32[]{:S(2)}) collective-permute-start(bf16[224,128]{1,0:T(8,128)(2,1)S(1)} %constant_dynamic-update-slice_fusion.refs_0_), channel_id=1, source_target_pairs={{0,65},{1,64},{64,1},{65,0},{128,193},{129,192},{192,129},{193,128... | collective-permute-start | bytes 172040 | tf_op jit(solution)/shard_map/ppermute | solution.py:273
  32.1 4.6 %collective-permute-start.10 = (bf16[64,256]{1,0:T(8,128)(2,1)S(1)}, bf16[64,256]{1,0:T(8,128)(2,1)S(1)}, u32[]{:S(2)}, u32[]{:S(2)}) collective-permute-start(bf16[64,256]{1,0:T(8,128)(2,1)S(1)} %attend.3), channel_id=1, source_target_pairs={{0,7},{1,6},{2,5},{3,4},{4,3},{5,2},{6,1},{7,0},{8,15},{9,14},{10,... | collective-permute-start | bytes 98312 | tf_op jit(solution)/shard_map/ppermute | solution.py:273
  35.0 5.1 %collective-permute-start.9 = (bf16[64,256]{1,0:T(8,128)(2,1)S(1)}, bf16[64,256]{1,0:T(8,128)(2,1)S(1)}, u32[]{:S(2)}, u32[]{:S(2)}) collective-permute-start(bf16[64,256]{1,0:T(8,128)(2,1)S(1)} %attend.3), channel_id=1, source_target_pairs={{0,5},{1,4},{2,7},{3,6},{4,1},{5,0},{6,3},{7,2},{8,13},{9,12},{10,... | collective-permute-start | bytes 98312 | tf_op jit(solution)/shard_map/ppermute | solution.py:273
  35.6 4.6 %collective-permute-start.8 = (bf16[64,256]{1,0:T(8,128)(2,1)S(1)}, bf16[64,256]{1,0:T(8,128)(2,1)S(1)}, u32[]{:S(2)}, u32[]{:S(2)}) collective-permute-start(bf16[64,256]{1,0:T(8,128)(2,1)S(1)} %attend.3), channel_id=1, source_target_pairs={{0,2},{1,3},{2,0},{3,1},{4,6},{5,7},{6,4},{7,5},{8,10},{9,11},{10,... | collective-permute-start | bytes 98312 | tf_op jit(solution)/shard_map/ppermute | solution.py:273
  40.2 4.6 %collective-permute-start.13 = (bf16[64,256]{1,0:T(8,128)(2,1)S(1)}, bf16[64,256]{1,0:T(8,128)(2,1)S(1)}, u32[]{:S(2)}, u32[]{:S(2)}) collective-permute-start(bf16[64,256]{1,0:T(8,128)(2,1)S(1)} %add_convert_fusion.2), channel_id=1, source_target_pairs={{0,49},{1,48},{16,33},{17,32},{32,17},{33,16},{48,1},{49,0},{2,51}... | collective-permute-start | bytes 98312 | tf_op jit(solution)/shard_map/ppermute | solution.py:273
  42.7 5.1 %collective-permute-start.12 = (bf16[64,256]{1,0:T(8,128)(2,1)S(1)}, bf16[64,256]{1,0:T(8,128)(2,1)S(1)}, u32[]{:S(2)}, u32[]{:S(2)}) collective-permute-start(bf16[64,256]{1,0:T(8,128)(2,1)S(1)} %add_convert_fusion.2), channel_id=1, source_target_pairs={{0,33},{1,32},{16,49},{17,48},{32,1},{33,0},{48,17},{49,16},{2,35}... | collective-permute-start | bytes 98312 | tf_op jit(solution)/shard_map/ppermute | solution.py:273
  43.5 4.2 %collective-permute-start.11 = (bf16[64,256]{1,0:T(8,128)(2,1)S(1)}, bf16[64,256]{1,0:T(8,128)(2,1)S(1)}, u32[]{:S(2)}, u32[]{:S(2)}) collective-permute-start(bf16[64,256]{1,0:T(8,128)(2,1)S(1)} %add_convert_fusion.2), channel_id=1, source_target_pairs={{0,16},{1,17},{16,0},{17,1},{32,48},{33,49},{48,32},{49,33},{2,18}... | collective-permute-start | bytes 98312 | tf_op jit(solution)/shard_map/ppermute | solution.py:273
  47.8 5.5 %collective-permute-start.17 = (bf16[64,256]{1,0:T(8,128)(2,1)S(1)}, bf16[64,256]{1,0:T(8,128)(2,1)S(1)}, u32[]{:S(2)}, u32[]{:S(2)}) collective-permute-start(bf16[64,256]{1,0:T(8,128)(2,1)S(1)} %get-tuple-element.12.refs_4_.refs_5_), channel_id=1, source_target_pairs={{0,193},{1,192},{64,129},{65,128},{128,65},{129,64},{192,1},{193,0... | collective-permute-start | bytes 98312 | tf_op jit(solution)/shard_map/ppermute | solution.py:273
  50.4 4.3 %collective-permute-start.16 = (bf16[64,256]{1,0:T(8,128)(2,1)S(1)}, bf16[64,256]{1,0:T(8,128)(2,1)S(1)}, u32[]{:S(2)}, u32[]{:S(2)}) collective-permute-start(bf16[64,256]{1,0:T(8,128)(2,1)S(1)} %get-tuple-element.12.refs_4_.refs_5_), channel_id=1, source_target_pairs={{0,129},{1,128},{64,193},{65,192},{128,1},{129,0},{192,65},{193,64... | collective-permute-start | bytes 98312 | tf_op jit(solution)/shard_map/ppermute | solution.py:273
  50.4 4.3 %collective-permute-start.15 = (bf16[64,256]{1,0:T(8,128)(2,1)S(1)}, bf16[64,256]{1,0:T(8,128)(2,1)S(1)}, u32[]{:S(2)}, u32[]{:S(2)}) collective-permute-start(bf16[64,256]{1,0:T(8,128)(2,1)S(1)} %get-tuple-element.12.refs_4_.refs_5_), channel_id=1, source_target_pairs={{0,65},{1,64},{64,1},{65,0},{128,193},{129,192},{192,129},{193,128... | collective-permute-start | bytes 98312 | tf_op jit(solution)/shard_map/ppermute | solution.py:273
  54.7 3.9 %collective-permute-start.18 = (bf16[4,64,256]{2,1,0:T(8,128)(2,1)S(1)}, bf16[4,64,256]{2,1,0:T(8,128)(2,1)S(1)}, u32[]{:S(2)}, u32[]{:S(2)}) collective-permute-start(bf16[4,64,256]{2,1,0:T(8,128)(2,1)S(1)} %pad_maximum_fusion.1), channel_id=1, source_target_pairs={{0,1},{1,0},{2,3},{3,2},{4,5},{5,4},{6,7},{7,6},{8,9},{9,8},{10,11... | collective-permute-start | bytes 393224 | tf_op jit(solution)/shard_map/ppermute | solution.py:285
  63.7 4.7 %collective-permute-start.21 = (bf16[64,256]{1,0:T(8,128)(2,1)S(1)}, bf16[64,256]{1,0:T(8,128)(2,1)S(1)}, u32[]{:S(2)}, u32[]{:S(2)}) collective-permute-start(bf16[64,256]{1,0:T(8,128)(2,1)S(1)} %attend.5), channel_id=1, source_target_pairs={{0,7},{1,6},{2,5},{3,4},{4,3},{5,2},{6,1},{7,0},{8,15},{9,14},{10,... | collective-permute-start | bytes 98312 | tf_op jit(solution)/shard_map/ppermute | solution.py:273
  64.9 4.9 %collective-permute-start.20 = (bf16[64,256]{1,0:T(8,128)(2,1)S(1)}, bf16[64,256]{1,0:T(8,128)(2,1)S(1)}, u32[]{:S(2)}, u32[]{:S(2)}) collective-permute-start(bf16[64,256]{1,0:T(8,128)(2,1)S(1)} %attend.5), channel_id=1, source_target_pairs={{0,5},{1,4},{2,7},{3,6},{4,1},{5,0},{6,3},{7,2},{8,13},{9,12},{10,... | collective-permute-start | bytes 98312 | tf_op jit(solution)/shard_map/ppermute | solution.py:273
  66.1 3.7 %collective-permute-start.19 = (bf16[64,256]{1,0:T(8,128)(2,1)S(1)}, bf16[64,256]{1,0:T(8,128)(2,1)S(1)}, u32[]{:S(2)}, u32[]{:S(2)}) collective-permute-start(bf16[64,256]{1,0:T(8,128)(2,1)S(1)} %attend.5), channel_id=1, source_target_pairs={{0,2},{1,3},{2,0},{3,1},{4,6},{5,7},{6,4},{7,5},{8,10},{9,11},{10,... | collective-permute-start | bytes 98312 | tf_op jit(solution)/shard_map/ppermute | solution.py:273
  69.8 5.0 %collective-permute-start.24 = (bf16[64,256]{1,0:T(8,128)(2,1)S(1)}, bf16[64,256]{1,0:T(8,128)(2,1)S(1)}, u32[]{:S(2)}, u32[]{:S(2)}) collective-permute-start(bf16[64,256]{1,0:T(8,128)(2,1)S(1)} %add_convert_fusion), channel_id=1, source_target_pairs={{0,49},{1,48},{16,33},{17,32},{32,17},{33,16},{48,1},{49,0},{2,51}... | collective-permute-start | bytes 98312 | tf_op jit(solution)/shard_map/ppermute | solution.py:273
  71.4 5.0 %collective-permute-start.23 = (bf16[64,256]{1,0:T(8,128)(2,1)S(1)}, bf16[64,256]{1,0:T(8,128)(2,1)S(1)}, u32[]{:S(2)}, u32[]{:S(2)}) collective-permute-start(bf16[64,256]{1,0:T(8,128)(2,1)S(1)} %add_convert_fusion), channel_id=1, source_target_pairs={{0,33},{1,32},{16,49},{17,48},{32,1},{33,0},{48,17},{49,16},{2,35}... | collective-permute-start | bytes 98312 | tf_op jit(solution)/shard_map/ppermute | solution.py:273
  72.1 4.2 %collective-permute-start.22 = (bf16[64,256]{1,0:T(8,128)(2,1)S(1)}, bf16[64,256]{1,0:T(8,128)(2,1)S(1)}, u32[]{:S(2)}, u32[]{:S(2)}) collective-permute-start(bf16[64,256]{1,0:T(8,128)(2,1)S(1)} %add_convert_fusion), channel_id=1, source_target_pairs={{0,16},{1,17},{16,0},{17,1},{32,48},{33,49},{48,32},{49,33},{2,18}... | collective-permute-start | bytes 98312 | tf_op jit(solution)/shard_map/ppermute | solution.py:273
  73.4 3.4 %collective-permute-start.14 = (bf16[64,256]{1,0:T(8,128)(2,1)S(1)}, bf16[64,256]{1,0:T(8,128)(2,1)S(1)}, u32[]{:S(2)}, u32[]{:S(2)}) collective-permute-start(bf16[64,256]{1,0:T(8,128)(2,1)S(1)} %get-tuple-element.13), channel_id=1, source_target_pairs={{0,1},{1,0},{2,3},{3,2},{4,5},{5,4},{6,7},{7,6},{8,9},{9,8},{10,11... | collective-permute-start | bytes 98312 | tf_op jit(solution)/shard_map/ppermute | solution.py:285
  (5 other events, 21.6 us)

commit v7 on v5

--- a/solution.py
+++ b/solution.py
@@ -323,8 +323,7 @@
     near = swap_all(noisy.astype(bf16), "mp", (1, 1, 1))
     far = other_core(jnp.stack(near))
     terms = ((1, 1.0), (2, -2.0), (3, 1.0))
-    state = attend(terms, packs, near[0], near, last=False)
-    grad = attend(terms, packs, near[0], list(far), state)
+    grad = attend(terms, packs, near[0], near + list(far))
     grad = add_heads(grad) * -score_sigma
     grad = jnp.where(odd, other_core(grad), grad)
     clean = clean.astype(bf16)

time: 79 us -> 78.9 us (level)
  waiting for transfers between devices: 19.7 us -> 20.9 us
  Pallas kernels: 17.3 us -> 16.3 us
    pallas_call x3 -> x2, Pallas kernels: 11.5 us -> 10.4 us  [attend(): pl.pallas_call(functools.partial(attend_kernel, terms, count, bool(state)...]
    ppermute x5, waiting for transfers between devices: 1.6 us -> 2.59 us  [other_core(): return lax.ppermute(value, 'tp', [(0, 1), (1, 0)])]
  transfers between devices with their start and end apart: 26 -> 26, of which waited for: 17 -> 19; matrix products, arithmetic and copies ran while one was open for 1% -> 1% of each run, Pallas kernels for 12% -> 7%
where the time goes in v7:
time: 78.9 us; the launch traced here: 78.7 us
  starting transfers between devices  37.3 us (47%)
  waiting for transfers between devices  20.9 us (26%)
  Pallas kernels  16.3 us (21%)
  between operations  2.11 us (3%)
  other arithmetic  1.42 us (2%)
    ppermute x21, starting transfers between devices, swap(): lax.ppermute(value, axes, [(i, i ^ flip) for i in range(lax.axis_size(axe...  32.4 us
    ppermute x21, waiting for transfers between devices, swap(): lax.ppermute(value, axes, [(i, i ^ flip) for i in range(lax.axis_size(axe...  18.3 us
    pallas_call x2, Pallas kernels, attend(): pl.pallas_call(functools.partial(attend_kernel, terms, count, bool(state)...  10.4 us
    pallas_call x1, Pallas kernels, fold_maps(): pl.pallas_call(maps_kernel, in_specs=[pl.BlockSpec(memory_space=pltpu.SME...  5.81 us
    ppermute x5, starting transfers between devices, other_core(): return lax.ppermute(value, 'tp', [(0, 1), (1, 0)])  4.92 us
    ppermute x5, waiting for transfers between devices, other_core(): return lax.ppermute(value, 'tp', [(0, 1), (1, 0)])  2.59 us
  transfers between devices with their start and end apart: 26, of which 19 were waited for; matrix products, arithmetic and copies ran while one was open for 1% of the time, Pallas kernels for 7%

profile of v7, /device:TPU:1, one launch (start us, length us, event | category | flops | bytes accessed | tf_op | source)
XLA Modules:
  0.0 78.7 jit_solution(1803327780447366812)
XLA Ops:
  0.6 3.3 %collective-permute-start.1 = (bf16[64,256]{1,0:T(8,128)(2,1)}, bf16[64,256]{1,0:T(8,128)(2,1)S(1)}, u32[]{:S(2)}, u32[]{:S(2)}) collective-permute-start(bf16[64,256]{1,0:T(8,128)(2,1)} %bitcast.56), channel_id=1, source_target_pairs={{0,1},{1,0},{2,3},{3,2},{4,5},{5,4},{6,7},{7,6},{8,9},{9,8},{10,11... | collective-permute-start | bytes 98312 | tf_op jit(solution)/shard_map/ppermute | solution.py:285
  6.0 5.8 %fold_maps.1 = bf16[144,128]{1,0:T(8,128)(2,1)S(1)} custom-call(s32[1]{0:T(128)S(6)} %copy.11.gen_ref, s32[1]{0:T(128)S(6)} %copy.12.score_ref, bf16[64,5120]{1,0:T(8,128)(2,1)} %bitcast.59, bf16[64,128]{1,0:T(8,128)(2,1)S(1)} %bitcast.55, bf16[256,10240]{1,0:T(8,128)(2,1)} %bitcast.57, bf16[384,5120]{1,0:T(8,128)(2,1)} %bitcast.58), custom_call_target="tpu_custom_call" | custom-call | flops 6000000000 | bytes 10000000 | tf_op jit(solution)/shard_map/fold_maps/pallas_call | solution.py:157
  11.9 6.3 %collective-permute-start.4 = (bf16[80,128]{1,0:T(8,128)(2,1)S(1)}, bf16[80,128]{1,0:T(8,128)(2,1)S(1)}, u32[]{:S(2)}, u32[]{:S(2)}) collective-permute-start(bf16[80,128]{1,0:T(8,128)(2,1)S(1)} %slice.14), channel_id=1, source_target_pairs={{0,9},{1,8},{8,1},{9,0},{2,11},{3,10},{10,3},{11,2},{4,13},{5,12},... | collective-permute-start | bytes 61448 | tf_op jit(solution)/shard_map/ppermute | solution.py:273
  18.2 1.2 %collective-permute-start.2 = (bf16[2,64,256]{2,1,0:T(8,128)(2,1)S(1)}, bf16[2,64,256]{2,1,0:T(8,128)(2,1)S(1)}, u32[]{:S(2)}, u32[]{:S(2)}) collective-permute-start(bf16[2,64,256]{2,1,0:T(8,128)(2,1)S(1)} %pad_maximum_fusion.2), channel_id=1, source_target_pairs={{0,129},{1,128},{64,193},{65,192},{128,1},{129,0},{192,65},{193,64... | collective-permute-start | bytes 196616 | tf_op jit(solution)/shard_map/ppermute | solution.py:273
  19.8 2.1 %collective-permute-start.7 = (bf16[224,128]{1,0:T(8,128)(2,1)S(1)}, bf16[224,128]{1,0:T(8,128)(2,1)S(1)}, u32[]{:S(2)}, u32[]{:S(2)}) collective-permute-start(bf16[224,128]{1,0:T(8,128)(2,1)S(1)} %constant_dynamic-update-slice_fusion.refs_0_), channel_id=1, source_target_pairs={{0,193},{1,192},{64,129},{65,128},{128,65},{129,64},{192,1},{193,0... | collective-permute-start | bytes 172040 | tf_op jit(solution)/shard_map/ppermute | solution.py:273
  22.7 1.0 %collective-permute-start.5 = (bf16[224,128]{1,0:T(8,128)(2,1)S(1)}, bf16[224,128]{1,0:T(8,128)(2,1)S(1)}, u32[]{:S(2)}, u32[]{:S(2)}) collective-permute-start(bf16[224,128]{1,0:T(8,128)(2,1)S(1)} %constant_dynamic-update-slice_fusion.refs_0_), channel_id=1, source_target_pairs={{0,65},{1,64},{64,1},{65,0},{128,193},{129,192},{192,129},{193,128... | collective-permute-start | bytes 172040 | tf_op jit(solution)/shard_map/ppermute | solution.py:273
  23.7 3.3 %collective-permute-done.2 = bf16[2,64,256]{2,1,0:T(8,128)(2,1)S(1)} collective-permute-done((bf16[2,64,256]{2,1,0:T(8,128)(2,1)S(1)}, bf16[2,64,256]{2,1,0:T(8,128)(2,1)S(1)}, u32[]{:S(2)}, u32[]{:S(2)}) %collective-permute-start.2) | collective-permute-done | bytes 65568 | tf_op jit(solution)/shard_map/ppermute | solution.py:273
  27.1 1.3 %collective-permute-done.3 = bf16[4,64,256]{2,1,0:T(8,128)(2,1)S(1)} collective-permute-done((bf16[4,64,256]{2,1,0:T(8,128)(2,1)S(1)}, bf16[4,64,256]{2,1,0:T(8,128)(2,1)S(1)}, u32[]{:S(2)}, u32[]{:S(2)}) %collective-permute-start.3) | collective-permute-done | bytes 131104 | tf_op jit(solution)/shard_map/ppermute | solution.py:285
  29.3 2.8 %attend.2 = bf16[64,256]{1,0:T(8,128)(2,1)S(1)} custom-call(bf16[224,128]{1,0:T(8,128)(2,1)S(1)} %constant_dynamic-update-slice_fusion.refs_0_, bf16[224,128]{1,0:T(8,128)(2,1)S(1)} %collective-permute-done.5.refs_1_, bf16[224,128]{1,0:T(8,128)(2,1)S(1)} %collective-permute-done.6.refs_2_, bf16[224,128]{1,0:T(8,128)(2,1)S(1)} %collective-permute-done.7.refs_3_, ...), custom_call_target="tpu_custom_call" | custom-call | flops 2147483648 | bytes 1000000 | tf_op jit(solution)/shard_map/attend/pallas_call | solution.py:256
  32.1 2.9 %collective-permute-start.10 = (bf16[64,256]{1,0:T(8,128)(2,1)S(1)}, bf16[64,256]{1,0:T(8,128)(2,1)S(1)}, u32[]{:S(2)}, u32[]{:S(2)}) collective-permute-start(bf16[64,256]{1,0:T(8,128)(2,1)S(1)} %attend.2), channel_id=1, source_target_pairs={{0,7},{1,6},{2,5},{3,4},{4,3},{5,2},{6,1},{7,0},{8,15},{9,14},{10,... | collective-permute-start | bytes 98312 | tf_op jit(solution)/shard_map/ppermute | solution.py:273
  36.8 2.5 %collective-permute-done.9 = bf16[64,256]{1,0:T(8,128)(2,1)S(1)} collective-permute-done((bf16[64,256]{1,0:T(8,128)(2,1)S(1)}, bf16[64,256]{1,0:T(8,128)(2,1)S(1)}, u32[]{:S(2)}, u32[]{:S(2)}) %collective-permute-start.9) | collective-permute-done | bytes 32800 | tf_op jit(solution)/shard_map/ppermute | solution.py:273
  39.3 4.1 %collective-permute-start.13 = (bf16[64,256]{1,0:T(8,128)(2,1)S(1)}, bf16[64,256]{1,0:T(8,128)(2,1)S(1)}, u32[]{:S(2)}, u32[]{:S(2)}) collective-permute-start(bf16[64,256]{1,0:T(8,128)(2,1)S(1)} %add_convert_fusion.2), channel_id=1, source_target_pairs={{0,49},{1,48},{16,33},{17,32},{32,17},{33,16},{48,1},{49,0},{2,51}... | collective-permute-start | bytes 98312 | tf_op jit(solution)/shard_map/ppermute | solution.py:273
  45.4 2.3 %collective-permute-done.12 = bf16[64,256]{1,0:T(8,128)(2,1)S(1)} collective-permute-done((bf16[64,256]{1,0:T(8,128)(2,1)S(1)}, bf16[64,256]{1,0:T(8,128)(2,1)S(1)}, u32[]{:S(2)}, u32[]{:S(2)}) %collective-permute-start.12) | collective-permute-done | bytes 32800 | tf_op jit(solution)/shard_map/ppermute | solution.py:273
  47.7 2.0 %collective-permute-start.17 = (bf16[64,256]{1,0:T(8,128)(2,1)S(1)}, bf16[64,256]{1,0:T(8,128)(2,1)S(1)}, u32[]{:S(2)}, u32[]{:S(2)}) collective-permute-start(bf16[64,256]{1,0:T(8,128)(2,1)S(1)} %get-tuple-element.8.refs_4_.refs_5_), channel_id=1, source_target_pairs={{0,193},{1,192},{64,129},{65,128},{128,65},{129,64},{192,1},{193,0... | collective-permute-start | bytes 98312 | tf_op jit(solution)/shard_map/ppermute | solution.py:273
  49.8 1.9 %collective-permute-start.15 = (bf16[64,256]{1,0:T(8,128)(2,1)S(1)}, bf16[64,256]{1,0:T(8,128)(2,1)S(1)}, u32[]{:S(2)}, u32[]{:S(2)}) collective-permute-start(bf16[64,256]{1,0:T(8,128)(2,1)S(1)} %get-tuple-element.8.refs_4_.refs_5_), channel_id=1, source_target_pairs={{0,65},{1,64},{64,1},{65,0},{128,193},{129,192},{192,129},{193,128... | collective-permute-start | bytes 98312 | tf_op jit(solution)/shard_map/ppermute | solution.py:273
  51.7 1.4 %collective-permute-done.17.refs_8_ = bf16[64,256]{1,0:T(8,128)(2,1)S(1)} collective-permute-done((bf16[64,256]{1,0:T(8,128)(2,1)S(1)}, bf16[64,256]{1,0:T(8,128)(2,1)S(1)}, u32[]{:S(2)}, u32[]{:S(2)}) %collective-permute-start.17) | collective-permute-done | bytes 32800 | tf_op jit(solution)/shard_map/ppermute | solution.py:273
  53.1 1.1 %collective-permute-done.16.refs_7_ = bf16[64,256]{1,0:T(8,128)(2,1)S(1)} collective-permute-done((bf16[64,256]{1,0:T(8,128)(2,1)S(1)}, bf16[64,256]{1,0:T(8,128)(2,1)S(1)}, u32[]{:S(2)}, u32[]{:S(2)}) %collective-permute-start.16) | collective-permute-done | bytes 32800 | tf_op jit(solution)/shard_map/ppermute | solution.py:273
  55.8 7.6 %attend.3 = bf16[64,256]{1,0:T(8,128)(2,1)S(1)} custom-call(bf16[224,128]{1,0:T(8,128)(2,1)S(1)} %constant_dynamic-update-slice_fusion.refs_0_, bf16[224,128]{1,0:T(8,128)(2,1)S(1)} %collective-permute-done.5.refs_1_, bf16[224,128]{1,0:T(8,128)(2,1)S(1)} %collective-permute-done.6.refs_2_, bf16[224,128]{1,0:T(8,128)(2,1)S(1)} %collective-permute-done.7.refs_3_, ...), custom_call_target="tpu_custom_call" | custom-call | flops 6442450944 | bytes 1000000 | tf_op jit(solution)/shard_map/attend/pallas_call | solution.py:256
  63.5 1.6 %collective-permute-start.21 = (bf16[64,256]{1,0:T(8,128)(2,1)S(1)}, bf16[64,256]{1,0:T(8,128)(2,1)S(1)}, u32[]{:S(2)}, u32[]{:S(2)}) collective-permute-start(bf16[64,256]{1,0:T(8,128)(2,1)S(1)} %attend.3), channel_id=1, source_target_pairs={{0,7},{1,6},{2,5},{3,4},{4,3},{5,2},{6,1},{7,0},{8,15},{9,14},{10,... | collective-permute-start | bytes 98312 | tf_op jit(solution)/shard_map/ppermute | solution.py:273
  65.7 1.6 %collective-permute-start.19 = (bf16[64,256]{1,0:T(8,128)(2,1)S(1)}, bf16[64,256]{1,0:T(8,128)(2,1)S(1)}, u32[]{:S(2)}, u32[]{:S(2)}) collective-permute-start(bf16[64,256]{1,0:T(8,128)(2,1)S(1)} %attend.3), channel_id=1, source_target_pairs={{0,3},{1,2},{2,1},{3,0},{4,7},{5,6},{6,5},{7,4},{8,11},{9,10},{10,... | collective-permute-start | bytes 98312 | tf_op jit(solution)/shard_map/ppermute | solution.py:273
  68.1 1.2 %collective-permute-done.20 = bf16[64,256]{1,0:T(8,128)(2,1)S(1)} collective-permute-done((bf16[64,256]{1,0:T(8,128)(2,1)S(1)}, bf16[64,256]{1,0:T(8,128)(2,1)S(1)}, u32[]{:S(2)}, u32[]{:S(2)}) %collective-permute-start.20) | collective-permute-done | bytes 32800 | tf_op jit(solution)/shard_map/ppermute | solution.py:273
  70.0 1.8 %collective-permute-start.24 = (bf16[64,256]{1,0:T(8,128)(2,1)S(1)}, bf16[64,256]{1,0:T(8,128)(2,1)S(1)}, u32[]{:S(2)}, u32[]{:S(2)}) collective-permute-start(bf16[64,256]{1,0:T(8,128)(2,1)S(1)} %add_convert_fusion), channel_id=1, source_target_pairs={{0,49},{1,48},{16,33},{17,32},{32,17},{33,16},{48,1},{49,0},{2,51}... | collective-permute-start | bytes 98312 | tf_op jit(solution)/shard_map/ppermute | solution.py:273
  72.8 1.1 %collective-permute-start.22 = (bf16[64,256]{1,0:T(8,128)(2,1)S(1)}, bf16[64,256]{1,0:T(8,128)(2,1)S(1)}, u32[]{:S(2)}, u32[]{:S(2)}) collective-permute-start(bf16[64,256]{1,0:T(8,128)(2,1)S(1)} %add_convert_fusion), channel_id=1, source_target_pairs={{0,17},{1,16},{16,1},{17,0},{32,49},{33,48},{48,33},{49,32},{2,19}... | collective-permute-start | bytes 98312 | tf_op jit(solution)/shard_map/ppermute | solution.py:273
  75.1 1.3 %collective-permute-done.23 = bf16[64,256]{1,0:T(8,128)(2,1)S(1)} collective-permute-done((bf16[64,256]{1,0:T(8,128)(2,1)S(1)}, bf16[64,256]{1,0:T(8,128)(2,1)S(1)}, u32[]{:S(2)}, u32[]{:S(2)}) %collective-permute-start.23) | collective-permute-done | bytes 32800 | tf_op jit(solution)/shard_map/ppermute | solution.py:273
  (54 shorter events, 15.0 us)
Async XLA Ops:
  0.6 11.2 %collective-permute-start.1 = (bf16[64,256]{1,0:T(8,128)(2,1)}, bf16[64,256]{1,0:T(8,128)(2,1)S(1)}, u32[]{:S(2)}, u32[]{:S(2)}) collective-permute-start(bf16[64,256]{1,0:T(8,128)(2,1)} %bitcast.56), channel_id=1, source_target_pairs={{0,1},{1,0},{2,3},{3,2},{4,5},{5,4},{6,7},{7,6},{8,9},{9,8},{10,11... | collective-permute-start | bytes 98312 | tf_op jit(solution)/shard_map/ppermute | solution.py:285
  4.0 7.9 %collective-permute-start = (bf16[64,256]{1,0:T(8,128)(2,1)}, bf16[64,256]{1,0:T(8,128)(2,1)S(1)}, u32[]{:S(2)}, u32[]{:S(2)}) collective-permute-start(bf16[64,256]{1,0:T(8,128)(2,1)} %bitcast.45), channel_id=1, source_target_pairs={{0,65},{1,64},{64,1},{65,0},{128,193},{129,192},{192,129},{193,128... | collective-permute-start | bytes 98312 | tf_op jit(solution)/shard_map/ppermute | solution.py:273
  11.9 7.9 %collective-permute-start.4 = (bf16[80,128]{1,0:T(8,128)(2,1)S(1)}, bf16[80,128]{1,0:T(8,128)(2,1)S(1)}, u32[]{:S(2)}, u32[]{:S(2)}) collective-permute-start(bf16[80,128]{1,0:T(8,128)(2,1)S(1)} %slice.14), channel_id=1, source_target_pairs={{0,9},{1,8},{8,1},{9,0},{2,11},{3,10},{10,3},{11,2},{4,13},{5,12},... | collective-permute-start | bytes 61448 | tf_op jit(solution)/shard_map/ppermute | solution.py:273
  18.2 8.8 %collective-permute-start.2 = (bf16[2,64,256]{2,1,0:T(8,128)(2,1)S(1)}, bf16[2,64,256]{2,1,0:T(8,128)(2,1)S(1)}, u32[]{:S(2)}, u32[]{:S(2)}) collective-permute-start(bf16[2,64,256]{2,1,0:T(8,128)(2,1)S(1)} %pad_maximum_fusion.2), channel_id=1, source_target_pairs={{0,129},{1,128},{64,193},{65,192},{128,1},{129,0},{192,65},{193,64... | collective-permute-start | bytes 196616 | tf_op jit(solution)/shard_map/ppermute | solution.py:273
  19.8 8.7 %collective-permute-start.7 = (bf16[224,128]{1,0:T(8,128)(2,1)S(1)}, bf16[224,128]{1,0:T(8,128)(2,1)S(1)}, u32[]{:S(2)}, u32[]{:S(2)}) collective-permute-start(bf16[224,128]{1,0:T(8,128)(2,1)S(1)} %constant_dynamic-update-slice_fusion.refs_0_), channel_id=1, source_target_pairs={{0,193},{1,192},{64,129},{65,128},{128,65},{129,64},{192,1},{193,0... | collective-permute-start | bytes 172040 | tf_op jit(solution)/shard_map/ppermute | solution.py:273
  21.8 7.5 %collective-permute-start.6 = (bf16[224,128]{1,0:T(8,128)(2,1)S(1)}, bf16[224,128]{1,0:T(8,128)(2,1)S(1)}, u32[]{:S(2)}, u32[]{:S(2)}) collective-permute-start(bf16[224,128]{1,0:T(8,128)(2,1)S(1)} %constant_dynamic-update-slice_fusion.refs_0_), channel_id=1, source_target_pairs={{0,129},{1,128},{64,193},{65,192},{128,1},{129,0},{192,65},{193,64... | collective-permute-start | bytes 172040 | tf_op jit(solution)/shard_map/ppermute | solution.py:273
  22.7 6.6 %collective-permute-start.5 = (bf16[224,128]{1,0:T(8,128)(2,1)S(1)}, bf16[224,128]{1,0:T(8,128)(2,1)S(1)}, u32[]{:S(2)}, u32[]{:S(2)}) collective-permute-start(bf16[224,128]{1,0:T(8,128)(2,1)S(1)} %constant_dynamic-update-slice_fusion.refs_0_), channel_id=1, source_target_pairs={{0,65},{1,64},{64,1},{65,0},{128,193},{129,192},{192,129},{193,128... | collective-permute-start | bytes 172040 | tf_op jit(solution)/shard_map/ppermute | solution.py:273
  32.1 4.6 %collective-permute-start.10 = (bf16[64,256]{1,0:T(8,128)(2,1)S(1)}, bf16[64,256]{1,0:T(8,128)(2,1)S(1)}, u32[]{:S(2)}, u32[]{:S(2)}) collective-permute-start(bf16[64,256]{1,0:T(8,128)(2,1)S(1)} %attend.2), channel_id=1, source_target_pairs={{0,7},{1,6},{2,5},{3,4},{4,3},{5,2},{6,1},{7,0},{8,15},{9,14},{10,... | collective-permute-start | bytes 98312 | tf_op jit(solution)/shard_map/ppermute | solution.py:273
  35.0 4.3 %collective-permute-start.9 = (bf16[64,256]{1,0:T(8,128)(2,1)S(1)}, bf16[64,256]{1,0:T(8,128)(2,1)S(1)}, u32[]{:S(2)}, u32[]{:S(2)}) collective-permute-start(bf16[64,256]{1,0:T(8,128)(2,1)S(1)} %attend.2), channel_id=1, source_target_pairs={{0,4},{1,5},{2,6},{3,7},{4,0},{5,1},{6,2},{7,3},{8,12},{9,13},{10,... | collective-permute-start | bytes 98312 | tf_op jit(solution)/shard_map/ppermute | solution.py:273
  35.4 3.9 %collective-permute-start.8 = (bf16[64,256]{1,0:T(8,128)(2,1)S(1)}, bf16[64,256]{1,0:T(8,128)(2,1)S(1)}, u32[]{:S(2)}, u32[]{:S(2)}) collective-permute-start(bf16[64,256]{1,0:T(8,128)(2,1)S(1)} %attend.2), channel_id=1, source_target_pairs={{0,3},{1,2},{2,1},{3,0},{4,7},{5,6},{6,5},{7,4},{8,11},{9,10},{10,... | collective-permute-start | bytes 98312 | tf_op jit(solution)/shard_map/ppermute | solution.py:273
  39.3 6.1 %collective-permute-start.13 = (bf16[64,256]{1,0:T(8,128)(2,1)S(1)}, bf16[64,256]{1,0:T(8,128)(2,1)S(1)}, u32[]{:S(2)}, u32[]{:S(2)}) collective-permute-start(bf16[64,256]{1,0:T(8,128)(2,1)S(1)} %add_convert_fusion.2), channel_id=1, source_target_pairs={{0,49},{1,48},{16,33},{17,32},{32,17},{33,16},{48,1},{49,0},{2,51}... | collective-permute-start | bytes 98312 | tf_op jit(solution)/shard_map/ppermute | solution.py:273
  43.4 4.3 %collective-permute-start.12 = (bf16[64,256]{1,0:T(8,128)(2,1)S(1)}, bf16[64,256]{1,0:T(8,128)(2,1)S(1)}, u32[]{:S(2)}, u32[]{:S(2)}) collective-permute-start(bf16[64,256]{1,0:T(8,128)(2,1)S(1)} %add_convert_fusion.2), channel_id=1, source_target_pairs={{0,32},{1,33},{16,48},{17,49},{32,0},{33,1},{48,16},{49,17},{2,34}... | collective-permute-start | bytes 98312 | tf_op jit(solution)/shard_map/ppermute | solution.py:273
  43.9 3.7 %collective-permute-start.11 = (bf16[64,256]{1,0:T(8,128)(2,1)S(1)}, bf16[64,256]{1,0:T(8,128)(2,1)S(1)}, u32[]{:S(2)}, u32[]{:S(2)}) collective-permute-start(bf16[64,256]{1,0:T(8,128)(2,1)S(1)} %add_convert_fusion.2), channel_id=1, source_target_pairs={{0,17},{1,16},{16,1},{17,0},{32,49},{33,48},{48,33},{49,32},{2,19}... | collective-permute-start | bytes 98312 | tf_op jit(solution)/shard_map/ppermute | solution.py:273
  47.7 5.4 %collective-permute-start.17 = (bf16[64,256]{1,0:T(8,128)(2,1)S(1)}, bf16[64,256]{1,0:T(8,128)(2,1)S(1)}, u32[]{:S(2)}, u32[]{:S(2)}) collective-permute-start(bf16[64,256]{1,0:T(8,128)(2,1)S(1)} %get-tuple-element.8.refs_4_.refs_5_), channel_id=1, source_target_pairs={{0,193},{1,192},{64,129},{65,128},{128,65},{129,64},{192,1},{193,0... | collective-permute-start | bytes 98312 | tf_op jit(solution)/shard_map/ppermute | solution.py:273
  49.8 4.5 %collective-permute-start.16 = (bf16[64,256]{1,0:T(8,128)(2,1)S(1)}, bf16[64,256]{1,0:T(8,128)(2,1)S(1)}, u32[]{:S(2)}, u32[]{:S(2)}) collective-permute-start(bf16[64,256]{1,0:T(8,128)(2,1)S(1)} %get-tuple-element.8.refs_4_.refs_5_), channel_id=1, source_target_pairs={{0,129},{1,128},{64,193},{65,192},{128,1},{129,0},{192,65},{193,64... | collective-permute-start | bytes 98312 | tf_op jit(solution)/shard_map/ppermute | solution.py:273
  49.8 4.6 %collective-permute-start.15 = (bf16[64,256]{1,0:T(8,128)(2,1)S(1)}, bf16[64,256]{1,0:T(8,128)(2,1)S(1)}, u32[]{:S(2)}, u32[]{:S(2)}) collective-permute-start(bf16[64,256]{1,0:T(8,128)(2,1)S(1)} %get-tuple-element.8.refs_4_.refs_5_), channel_id=1, source_target_pairs={{0,65},{1,64},{64,1},{65,0},{128,193},{129,192},{192,129},{193,128... | collective-permute-start | bytes 98312 | tf_op jit(solution)/shard_map/ppermute | solution.py:273
  54.4 1.4 %collective-permute-start.18 = (bf16[4,64,256]{2,1,0:T(8,128)(2,1)S(1)}, bf16[4,64,256]{2,1,0:T(8,128)(2,1)S(1)}, u32[]{:S(2)}, u32[]{:S(2)}) collective-permute-start(bf16[4,64,256]{2,1,0:T(8,128)(2,1)S(1)} %pad_maximum_fusion.1), channel_id=1, source_target_pairs={{0,1},{1,0},{2,3},{3,2},{4,5},{5,4},{6,7},{7,6},{8,9},{9,8},{10,11... | collective-permute-start | bytes 393224 | tf_op jit(solution)/shard_map/ppermute | solution.py:285
  63.5 4.7 %collective-permute-start.21 = (bf16[64,256]{1,0:T(8,128)(2,1)S(1)}, bf16[64,256]{1,0:T(8,128)(2,1)S(1)}, u32[]{:S(2)}, u32[]{:S(2)}) collective-permute-start(bf16[64,256]{1,0:T(8,128)(2,1)S(1)} %attend.3), channel_id=1, source_target_pairs={{0,7},{1,6},{2,5},{3,4},{4,3},{5,2},{6,1},{7,0},{8,15},{9,14},{10,... | collective-permute-start | bytes 98312 | tf_op jit(solution)/shard_map/ppermute | solution.py:273
  65.0 4.3 %collective-permute-start.20 = (bf16[64,256]{1,0:T(8,128)(2,1)S(1)}, bf16[64,256]{1,0:T(8,128)(2,1)S(1)}, u32[]{:S(2)}, u32[]{:S(2)}) collective-permute-start(bf16[64,256]{1,0:T(8,128)(2,1)S(1)} %attend.3), channel_id=1, source_target_pairs={{0,4},{1,5},{2,6},{3,7},{4,0},{5,1},{6,2},{7,3},{8,12},{9,13},{10,... | collective-permute-start | bytes 98312 | tf_op jit(solution)/shard_map/ppermute | solution.py:273
  65.7 4.2 %collective-permute-start.19 = (bf16[64,256]{1,0:T(8,128)(2,1)S(1)}, bf16[64,256]{1,0:T(8,128)(2,1)S(1)}, u32[]{:S(2)}, u32[]{:S(2)}) collective-permute-start(bf16[64,256]{1,0:T(8,128)(2,1)S(1)} %attend.3), channel_id=1, source_target_pairs={{0,3},{1,2},{2,1},{3,0},{4,7},{5,6},{6,5},{7,4},{8,11},{9,10},{10,... | collective-permute-start | bytes 98312 | tf_op jit(solution)/shard_map/ppermute | solution.py:273
  70.0 5.1 %collective-permute-start.24 = (bf16[64,256]{1,0:T(8,128)(2,1)S(1)}, bf16[64,256]{1,0:T(8,128)(2,1)S(1)}, u32[]{:S(2)}, u32[]{:S(2)}) collective-permute-start(bf16[64,256]{1,0:T(8,128)(2,1)S(1)} %add_convert_fusion), channel_id=1, source_target_pairs={{0,49},{1,48},{16,33},{17,32},{32,17},{33,16},{48,1},{49,0},{2,51}... | collective-permute-start | bytes 98312 | tf_op jit(solution)/shard_map/ppermute | solution.py:273
  71.8 4.6 %collective-permute-start.23 = (bf16[64,256]{1,0:T(8,128)(2,1)S(1)}, bf16[64,256]{1,0:T(8,128)(2,1)S(1)}, u32[]{:S(2)}, u32[]{:S(2)}) collective-permute-start(bf16[64,256]{1,0:T(8,128)(2,1)S(1)} %add_convert_fusion), channel_id=1, source_target_pairs={{0,32},{1,33},{16,48},{17,49},{32,0},{33,1},{48,16},{49,17},{2,34}... | collective-permute-start | bytes 98312 | tf_op jit(solution)/shard_map/ppermute | solution.py:273
  72.8 3.9 %collective-permute-start.22 = (bf16[64,256]{1,0:T(8,128)(2,1)S(1)}, bf16[64,256]{1,0:T(8,128)(2,1)S(1)}, u32[]{:S(2)}, u32[]{:S(2)}) collective-permute-start(bf16[64,256]{1,0:T(8,128)(2,1)S(1)} %add_convert_fusion), channel_id=1, source_target_pairs={{0,17},{1,16},{16,1},{17,0},{32,49},{33,48},{48,33},{49,32},{2,19}... | collective-permute-start | bytes 98312 | tf_op jit(solution)/shard_map/ppermute | solution.py:273
  73.9 3.3 %collective-permute-start.14 = (bf16[64,256]{1,0:T(8,128)(2,1)S(1)}, bf16[64,256]{1,0:T(8,128)(2,1)S(1)}, u32[]{:S(2)}, u32[]{:S(2)}) collective-permute-start(bf16[64,256]{1,0:T(8,128)(2,1)S(1)} %get-tuple-element.9), channel_id=1, source_target_pairs={{0,1},{1,0},{2,3},{3,2},{4,5},{5,4},{6,7},{7,6},{8,9},{9,8},{10,11... | collective-permute-start | bytes 98312 | tf_op jit(solution)/shard_map/ppermute | solution.py:285
  (5 other events, 21.6 us)
